TPU v7x, 256 devices: a whole 4x4x8 slice. The times are simulated.
256 devices in a mesh: cluster: 8 (over z), tm: 32 (over x, y, core).
Axes of the slice: x: 4, y: 4, z: 8, core: 2. Of those that a mesh axis runs over, the one named last changes fastest.
Arguments:
- obs: float32 [24, 2048, 128], P('cluster', 'tm'), parts along dimension 0, may hold values from -6 to 6
- present: int32 [24, 2048], P('cluster', 'tm'), parts along dimension 0, may hold values 0 or 1
- sensors: int32 [8], P('cluster'), parts along dimension 0, may hold values from 32 to 128
- log_prec: float32 [1024], P('cluster'), parts along dimension 0, may hold values from -1 to 1
- dynamics: float32 [1024, 128], P('cluster'), parts along dimension 0, may hold values from -1 to 1
- prior_var: float32 [1024], P('cluster'), parts along dimension 0, may hold values from 0 to 0.06, as said below
- obs_map: float32 [1024, 128], P('cluster'), parts along dimension 0, may hold values from -0.5 to 0.5
- init_state: float32 [24, 128], P('cluster'), parts along dimension 0, may hold values from -6 to 6
Outputs:
- smoothed: float32 [24, 2048, 128], P('cluster', 'tm'), parts along dimension 0
- new_log_prec: float32 [1024], P('cluster'), parts along dimension 0
- mean_loglik: float32 [8], P('cluster'), parts along dimension 0
There are 8 independent parts, one for each index of `cluster`. A program takes and returns all parts, laid end to end along the dimension named above; each array names one. Nothing has to cross between parts.
Inputs may be any that keep to these rules, and one draw needn't show every extreme that they name: `prior_var`: positive variances.
All inputs are finite; a program needn't handle non-finite values. No bound on the sum of `present` on one device may be relied on, other than what follows from the above.
Results may differ from a plain program's by a relative error of at most 0.0003.
Values sent between devices are 32-bit elements; how exact they have to be, the bound alone decides.
No kernel may reach another device: no remote copies, remote signals or barrier semaphores. Data moves between devices by JAX's collectives and lax.ppermute only.
A program may use at most 128 MiB of HBM per device.

v0:
```python
import jax
import jax.numpy as jnp
from jax import lax
from jax.experimental import pallas as pl
from jax.experimental.pallas import tpu as pltpu
from jax.sharding import Mesh
from jax.sharding import PartitionSpec as P

F32, BF16 = jnp.float32, jnp.bfloat16
TM = ("tm_0", "tm_1", "tm_2")
N = 128
SEQ, STEPS, SUB = 3, 64, 4
LEAVES = STEPS // SUB
ROWS = SEQ * LEAVES
AUG = N + 8
BLOCKS = 32
VMEM_LIMIT = 40 * 1024 * 1024


def dot(a, b):
    return lax.dot(a, b, preferred_element_type=F32)


def lanes(*parts):
    return jnp.concatenate(parts, axis=1)


def stacked(*parts):
    return jnp.concatenate(parts, axis=0)


def split2(a):
    hi = a.astype(BF16)
    return hi, (a - hi.astype(F32)).astype(BF16)


def split3(a):
    hi = a.astype(BF16)
    rest = a - hi.astype(F32)
    mid = rest.astype(BF16)
    return hi, mid, (rest - mid.astype(F32)).astype(BF16)


def pair(a):
    return lanes(*split2(a))


def whole(x):
    n = x.shape[1] // 2
    return x[:, :n].astype(F32) + x[:, n:].astype(F32)


def mul_pair(x, y):
    d = dot(x, stacked(y, y))
    n = y.shape[1] // 2
    return d[:, :n] + d[:, n:]


def mul_exact(a, b):
    a0, a1, a2 = split3(a)
    b0, b1, b2 = split3(b)
    n = b.shape[1]
    y = lanes(b0, b1)
    d = dot(lanes(a0, a1), stacked(y, y))
    return d[:, :n] + (d[:, n:] + dot(lanes(a0, a2), stacked(b2, b0)))


def apply_row(row, matrix):
    column = jnp.transpose(jnp.broadcast_to(row, (N, N)))
    return jnp.sum(column * matrix, axis=0, keepdims=True)


def step_major(ref, i):
    return stacked(*(ref[b, pl.ds(i, LEAVES, stride=SUB), :] for b in range(SEQ)))


def model(sensors_ref, lp_ref, dyn_ref, pv_ref, map_ref):
    on = (lax.broadcasted_iota(jnp.int32, (1, N), 1) < sensors_ref[0]).astype(F32)
    weight = jnp.exp(lp_ref[...]) * on
    dyn_t = jnp.transpose(dyn_ref[...])
    out_t = mul_exact(dyn_t, jnp.transpose(map_ref[...]))
    filt_t = dyn_t - mul_exact(out_t * weight, map_ref[...]) * pv_ref[...]
    return on, weight, dyn_t, out_t, filt_t


def drives(obs_ref, pres_ref, weight, pv, obs_map, mask_scr, u_scr):
    flags = pres_ref[...].astype(F32)
    flags = jnp.transpose(stacked(flags, jnp.zeros((8 - SEQ, STEPS), F32)))
    y = pair(obs_map)
    for b in range(SEQ):
        mask = jnp.broadcast_to(flags[:, b : b + 1], (STEPS, N))
        mask_scr[b] = mask
        u_scr[b] = mul_pair(pair(obs_ref[b] * weight), y) * pv * mask


def tree(pres_smem, dyn_t, filt_t, mask_scr, u_scr, table, nodes1, nodes2, nodes3, offs):
    two = mul_exact(stacked(dyn_t, filt_t), lanes(dyn_t, filt_t))
    twos = [two[i * N : (i + 1) * N, j * N : (j + 1) * N] for i in (0, 1) for j in (0, 1)]
    wide = lanes(*twos)
    for i in range(4):
        four = mul_exact(twos[i], wide)
        for j in range(4):
            table[4 * i + j] = pair(four[:, j * N : (j + 1) * N])
    y = pair(lanes(dyn_t, filt_t))
    z = step_major(u_scr, 0)
    for i in range(1, SUB):
        d = mul_pair(pair(z), y)
        z = jnp.where(step_major(mask_scr, i) > 0.5, d[:, N:], d[:, :N]) + step_major(u_scr, i)
    offs[0:ROWS, :] = z

    def leaf(k):
        b, j = k // LEAVES, k % LEAVES
        at = 0
        for i in range(SUB):
            at = at * 2 + pres_smem[b, SUB * j + i]
        return table[at]

    def join(left, left_off, right, right_off):
        off = pair(jnp.broadcast_to(left_off, (16, N)))
        got = mul_pair(stacked(left, off), right)
        return got[:N], got[N : N + 1] + right_off

    base, count = 0, ROWS
    roots = []
    get = leaf
    for store in (nodes1, nodes2, nodes3, None):
        for k in range(count // 2):
            matrix, off = join(
                get(2 * k),
                offs[base + 2 * k : base + 2 * k + 1, :],
                get(2 * k + 1),
                offs[base + 2 * k + 1 : base + 2 * k + 2, :],
            )
            if store is None:
                roots.append((matrix, off))
            else:
                store[k] = pair(matrix)
                offs[base + count + k : base + count + k + 1, :] = off
        base, count = base + count, count // 2
        if store is not None:
            get = lambda k, store=store: store[k]
    return roots, leaf


TREE_SCRATCH = [
    pltpu.VMEM((SEQ, STEPS, N), F32),
    pltpu.VMEM((SEQ, STEPS, N), F32),
    pltpu.VMEM((16, N, 2 * N), BF16),
    pltpu.VMEM((24, N, 2 * N), BF16),
    pltpu.VMEM((12, N, 2 * N), BF16),
    pltpu.VMEM((6, N, 2 * N), BF16),
    pltpu.VMEM((96, N), F32),
]


def k_block(
    pres_smem, sensors_ref, obs_ref, pres_ref, lp_ref, dyn_ref, pv_ref, map_ref, msg_ref,
    mask_scr, u_scr, table, nodes1, nodes2, nodes3, offs,
):
    on, weight, dyn_t, out_t, filt_t = model(sensors_ref, lp_ref, dyn_ref, pv_ref, map_ref)
    drives(obs_ref, pres_ref, weight, pv_ref[...], map_ref[...], mask_scr, u_scr)
    roots, leaf = tree(
        pres_smem, dyn_t, filt_t, mask_scr, u_scr, table, nodes1, nodes2, nodes3, offs
    )
    for b in range(SEQ):
        msg_ref[b, 0:N, :] = roots[b][0]
        msg_ref[b, N:AUG, :] = jnp.broadcast_to(roots[b][1], (8, N))


def k_tables(
    pres_smem, sensors_ref, obs_ref, pres_ref, lp_ref, dyn_ref, pv_ref, map_ref,
    pre_ref, preoff_ref, step_ref, u_ref, mask_ref, far_ref, near_ref, cross_ref, resid_ref,
    mask_scr, u_scr, table, nodes1, nodes2, nodes3, offs,
):
    on, weight, dyn_t, out_t, filt_t = model(sensors_ref, lp_ref, dyn_ref, pv_ref, map_ref)
    drives(obs_ref, pres_ref, weight, pv_ref[...], map_ref[...], mask_scr, u_scr)
    roots, leaf = tree(
        pres_smem, dyn_t, filt_t, mask_scr, u_scr, table, nodes1, nodes2, nodes3, offs
    )
    for i in range(SUB):
        u_ref[i] = step_major(u_scr, i)
        mask_ref[i] = step_major(mask_scr, i)
    step_ref[...] = pair(lanes(dyn_t, filt_t, out_t))
    starts = {1: ROWS + 24 + 12, 2: ROWS + 24, 4: ROWS, 8: 0}
    stores = {1: nodes3, 2: nodes2, 4: nodes1}
    preoff_ref[...] = jnp.zeros_like(preoff_ref)
    for b in range(SEQ):
        pre_ref[b * LEAVES] = jnp.zeros((N, N), F32)
        for parents in (1, 2, 4, 8):
            span = LEAVES // parents
            for k in range(parents):
                at = b * LEAVES + k * span
                left = b * 2 * parents + 2 * k
                off = offs[starts[parents] + left : starts[parents] + left + 1, :]
                got = leaf(left) if parents == 8 else stores[parents][left]
                if k == 0:
                    matrix = whole(got)
                else:
                    before = stacked(
                        pair(pre_ref[at]),
                        pair(jnp.broadcast_to(preoff_ref[at : at + 1, :], (16, N))),
                    )
                    both = mul_pair(before, got)
                    matrix, off = both[:N], both[N : N + 1] + off
                to = at + span // 2
                pre_ref[to] = matrix
                preoff_ref[to : to + 1, :] = off
    dyn = dyn_ref[...]
    eye = (
        lax.broadcasted_iota(jnp.int32, (N, N), 0) == lax.broadcasted_iota(jnp.int32, (N, N), 1)
    ).astype(F32)
    resid_ref[...] = pair(eye - mul_exact(dyn_t, dyn))
    d2 = mul_exact(dyn, dyn)
    d34 = mul_exact(d2, lanes(dyn, d2))
    d4 = d34[:, N:]
    for i, a in enumerate((dyn, d2, d34[:, :N], d4)):
        near_ref[i] = pair(a)
    far_ref[0] = eye
    far_ref[1] = d4
    for have in (1, 2, 4, 8):
        last = far_ref[have]
        for k in range(1, have + 1):
            got = mul_exact(last, far_ref[k])
            if have + k < LEAVES:
                far_ref[have + k] = got
    for i, k in enumerate((2, 4, 8)):
        near_ref[4 + i] = pair(far_ref[k])
    block = got
    cross_ref[0] = pair(eye)
    powers = [None, block]
    for k in range(2, 9):
        powers.append(mul_exact(powers[k // 2], powers[k - k // 2]))
    for k in range(1, 8):
        cross_ref[k] = pair(powers[k])
    w16 = mul_exact(powers[8], powers[8])
    cross_ref[8] = pair(powers[8])
    cross_ref[9] = pair(w16)
    cross_ref[10] = pair(mul_exact(w16, powers[8]))


def aug_pair(a):
    return pair(stacked(a, a[N:AUG]))


def compose(a, b):
    got = mul_pair(aug_pair(a), pair(b[:N]))
    return stacked(got[:N], got[N:AUG] + b[N:AUG])


def pick(flag, a, b):
    return jnp.where(flag, a, b)


def k_core(own_ref, other_ref, out_ref):
    first = lax.axis_index("tm_2") == 0
    for b in range(SEQ):
        own, other = own_ref[b], other_ref[b]
        out_ref[b] = compose(pick(first, own, other), pick(first, other, own))


def ordered(axis, refs, scr):
    me = lax.axis_index(axis)
    for d, ref in enumerate(refs):
        scr[lax.rem(me + 4 - d, 4)] = ref[...]


def k_total(own_ref, r1_ref, r2_ref, r3_ref, out_ref, scr):
    ordered("tm_1", (own_ref, r1_ref, r2_ref, r3_ref), scr)
    for b in range(SEQ):
        out_ref[b] = compose(compose(scr[0, b], scr[1, b]), compose(scr[2, b], scr[3, b]))


def k_entry(own_ref, r1_ref, r2_ref, r3_ref, mate_ref, out_ref, scr):
    ordered("tm_1", (own_ref, r1_ref, r2_ref, r3_ref), scr)
    me, second = lax.axis_index("tm_1"), lax.axis_index("tm_2") == 1
    eye = (
        lax.broadcasted_iota(jnp.int32, (AUG, N), 0) == lax.broadcasted_iota(jnp.int32, (AUG, N), 1)
    ).astype(F32)
    for b in range(SEQ):
        so_far = eye
        for k in range(3):
            so_far = pick(k < me, compose(so_far, scr[k, b]), so_far)
        out_ref[b] = pick(second, compose(so_far, mate_ref[b]), so_far)


def k_filter(
    sensors_ref, own_ref, r1_ref, r2_ref, r3_ref, entry_ref, init_ref, obs_ref, lp_ref,
    dyn_ref, pre_ref, preoff_ref, step_ref, u_ref, mask_ref, far_ref, near_ref, resid_ref,
    send_ref, local_ref, suffix_ref, final_ref, scr,
):
    ordered("tm_0", (own_ref, r1_ref, r2_ref, r3_ref), scr)
    group = lax.axis_index("tm_0")
    last = (group == 3) & (lax.axis_index("tm_1") == 3) & (lax.axis_index("tm_2") == 1)
    starts = []
    for b in range(SEQ):
        row = init_ref[b : b + 1, :]
        for k in range(3):
            row = pick(k < group, apply_row(row, scr[k, b, 0:N, :]) + scr[k, b, N : N + 1, :], row)
        row = apply_row(row, entry_ref[b, 0:N, :]) + entry_ref[b, N : N + 1, :]
        starts.append(row)
    rows = []
    for b in range(SEQ):
        column = jnp.transpose(jnp.broadcast_to(starts[b], (N, N)))
        rows.append(starts[b])
        for j in range(1, LEAVES):
            k = b * LEAVES + j
            rows.append(
                jnp.sum(column * pre_ref[k], axis=0, keepdims=True) + preoff_ref[k : k + 1, :]
            )
    state = stacked(*rows)
    on = (lax.broadcasted_iota(jnp.int32, (1, N), 1) < sensors_ref[0]).astype(F32)
    weight = jnp.exp(lp_ref[...]) * on
    step = step_ref[...]
    resid = resid_ref[...]
    square = jnp.zeros((ROWS, N), F32)
    seen = jnp.zeros((ROWS, N), F32)
    residuals = []
    for i in range(SUB):
        d = mul_pair(pair(state), step)
        mask = mask_ref[i]
        error = step_major(obs_ref, i) - d[:, 2 * N :]
        square = square + mask * (error * error)
        seen = seen + mask
        state = pick(mask > 0.5, d[:, N : 2 * N], d[:, :N]) + u_ref[i]
        residuals.append(mul_pair(pair(state), resid))
    square = jnp.sum(square, axis=0, keepdims=True) * weight
    seen = jnp.sum(seen, axis=0, keepdims=True)
    ends = stacked(*(state[(b + 1) * LEAVES - 1 : (b + 1) * LEAVES, :] for b in range(SEQ)))
    ends = stacked(ends, jnp.zeros((8 - SEQ, N), F32))
    final = mul_pair(pair(ends), pair(jnp.transpose(dyn_ref[...])))
    final_ref[...] = final
    y = near_ref[0]
    run = residuals[SUB - 1]
    local_ref[SUB - 1] = run
    for i in reversed(range(SUB - 1)):
        run = mul_pair(pair(run), y) + residuals[i]
        local_ref[i] = run
    place = lax.broadcasted_iota(jnp.int32, (ROWS, N), 0) % LEAVES
    for k, reach in zip((3, 4, 5, 6), (1, 2, 4, 8)):
        moved = mul_pair(pair(run), near_ref[k])
        moved = pltpu.roll(moved, ROWS - reach, 0)
        run = run + pick(place < LEAVES - reach, moved, 0.0)
    suffix_ref[...] = run
    offsets = stacked(*(run[b * LEAVES : b * LEAVES + 1, :] for b in range(SEQ)))
    offsets = stacked(offsets, jnp.zeros((8 - SEQ, N), F32))
    half = mul_pair(pair(final), near_ref[6])
    through = mul_pair(pair(half), near_ref[6])
    offsets = offsets + pick(last, through, 0.0)
    packed = stacked(offsets[:SEQ], square, seen, jnp.zeros((8 - SEQ - 2, N), F32))
    send_ref[...] = jnp.broadcast_to(packed[None], (BLOCKS, 8, N))


def k_smooth(
    sensors_ref, got_ref, local_ref, suffix_ref, final_ref, lp_ref, far_ref, near_ref, cross_ref,
    out_ref, prec_ref, lik_ref,
):
    me = (lax.axis_index("tm_0") * 4 + lax.axis_index("tm_1")) * 2 + lax.axis_index("tm_2")
    on = (lax.broadcasted_iota(jnp.int32, (1, N), 1) < sensors_ref[0]).astype(F32)
    acc = jnp.zeros((4 * 8, N), F32)
    for h in range(8):
        parts = []
        for g in range(4):
            at = me + 1 + 8 * g + h
            parts.append(pick(at < BLOCKS, got_ref[jnp.minimum(at, BLOCKS - 1)], 0.0))
        acc = acc + mul_pair(pair(stacked(*parts)), cross_ref[h])
    leaving = acc[0:8]
    for g in range(1, 4):
        leaving = leaving + mul_pair(pair(acc[8 * g : 8 * g + 8]), cross_ref[7 + g])
    leaving = pick(me == BLOCKS - 1, final_ref[...], leaving)
    rows = []
    for b in range(SEQ):
        column = jnp.transpose(jnp.broadcast_to(leaving[b : b + 1, :], (N, N)))
        for j in range(LEAVES - 1):
            k = b * LEAVES + j
            rows.append(
                jnp.sum(column * far_ref[LEAVES - 1 - j], axis=0, keepdims=True)
                + suffix_ref[k + 1 : k + 2, :]
            )
        rows.append(leaving[b : b + 1, :])
    x = pair(stacked(*rows))
    for i in range(SUB):
        got = mul_pair(x, near_ref[SUB - 1 - i]) + local_ref[i]
        for b in range(SEQ):
            out_ref[b, pl.ds(i, LEAVES, stride=SUB), :] = got[b * LEAVES : (b + 1) * LEAVES]
    sums = jnp.sum(got_ref[...], axis=0)
    square, seen = sums[SEQ : SEQ + 1], sums[SEQ + 1 : SEQ + 2]
    total = float(SEQ * STEPS * BLOCKS)
    lp = lp_ref[...]
    prec_ref[...] = lp + (0.5 / total) * on * (seen - square)
    lik = jnp.sum(on * (seen * lp - square), axis=1, keepdims=True) * (0.5 / (total * N))
    lik_ref[...] = jnp.broadcast_to(lik, (1, N))


VM = pl.BlockSpec(memory_space=pltpu.VMEM)
SM = pl.BlockSpec(memory_space=pltpu.SMEM)


def call(kernel, name, specs, shapes, scratch=(), flops=0, moved=0):
    return pl.pallas_call(
        kernel,
        out_shape=shapes,
        in_specs=specs,
        out_specs=jax.tree.map(lambda _: VM, shapes),
        scratch_shapes=list(scratch),
        compiler_params=pltpu.CompilerParams(vmem_limit_bytes=VMEM_LIMIT),
        cost_estimate=pl.CostEstimate(flops=flops, bytes_accessed=moved, transcendentals=0),
        name=name,
    )


def out(shape, dtype=F32):
    return jax.ShapeDtypeStruct(shape, dtype)


def shifted(a, axis, by):
    count = lax.axis_size(axis)
    return lax.ppermute(a, axis, [(i, (i + by) % count) for i in range(count)])


def local(obs, present, sensors, log_prec, dynamics, prior_var, obs_map, init_state):
    lp, pv = log_prec.reshape(1, N), prior_var.reshape(1, N)
    msg = out((SEQ, AUG, N))
    args = (present, sensors, obs, present, lp, dynamics, pv, obs_map)
    specs = [SM, SM] + [VM] * 6
    four = pltpu.VMEM((4, SEQ, AUG, N), F32)
    block = call(k_block, "k_block", specs, msg, TREE_SCRATCH, 10**9, 10**6)(*args)
    mate = shifted(block, "tm_2", 1)
    pre, preoff, step, u, mask, far, near, cross, resid = call(
        k_tables,
        "k_tables",
        specs,
        (
            out((ROWS, N, N)),
            out((ROWS, N)),
            out((N, 6 * N), BF16),
            out((SUB, ROWS, N)),
            out((SUB, ROWS, N)),
            out((LEAVES, N, N)),
            out((7, N, 2 * N), BF16),
            out((11, N, 2 * N), BF16),
            out((N, 2 * N), BF16),
        ),
        TREE_SCRATCH,
        6 * 10**9,
        10**7,
    )(*args)
    chip = call(k_core, "k_core", [VM] * 2, msg, (), 10**7, 10**6)(block, mate)
    ys = [shifted(chip, "tm_1", d) for d in (1, 2, 3)]
    column = call(k_total, "k_total", [VM] * 4, msg, [four], 10**7, 10**6)(chip, *ys)
    xs = [shifted(column, "tm_0", d) for d in (1, 2, 3)]
    entry = call(k_entry, "k_entry", [VM] * 5, msg, [four], 10**8, 10**6)(chip, *ys, mate)
    send, near_sums, suffix, final = call(
        k_filter,
        "k_filter",
        [SM] + [VM] * 17,
        (out((BLOCKS, 8, N)), out((SUB, ROWS, N)), out((ROWS, N)), out((8, N))),
        [four],
        10**7,
        10**6,
    )(
        sensors, column, *xs, entry, init_state, obs, lp, dynamics, pre, preoff, step, u, mask,
        far, near, resid,
    )
    got = lax.all_to_all(send, TM, 0, 0, tiled=True)
    smoothed, prec, lik = call(
        k_smooth,
        "k_smooth",
        [SM] + [VM] * 8,
        (out((SEQ, STEPS, N)), out((1, N)), out((1, N))),
        (),
        10**7,
        10**6,
    )(sensors, got, near_sums, suffix, final, lp, far, near, cross)
    return smoothed, prec.reshape(N), lik[0, :1]


def solution(mesh):
    split = Mesh(
        mesh.devices.reshape(mesh.shape["cluster"], 4, 4, 2), ("cluster", "tm_0", "tm_1", "tm_2")
    )
    return jax.shard_map(
        local,
        mesh=split,
        in_specs=(
            P("cluster", TM, None),
            P("cluster", TM),
            P("cluster"),
            P("cluster"),
            P("cluster", None),
            P("cluster"),
            P("cluster", None),
            P("cluster", None),
        ),
        out_specs=(P("cluster", TM, None), P("cluster"), P("cluster")),
        check_vma=False,
    )
```

profile of v0, /device:TPU:1, one launch (start us, length us, event | category | flops | bytes accessed | tf_op | source)
XLA Modules:
  0.0 59.5 jit_solution(3638226948635120507)
XLA Ops:
  1.3 0.0 copy-start
  1.3 0.9 %copy-done = f32[3,64,128]{2,1,0:T(8,128)S(1)} copy-done((f32[3,64,128]{2,1,0:T(8,128)S(1)}, f32[3,64,128]{2,1,0:T(8,128)}, u32[]{:S(2)}) %copy-start) | copy-done | bytes 98328
  2.2 0.8 %copy-done.2 = f32[128,128]{1,0:T(8,128)S(1)} copy-done((f32[128,128]{1,0:T(8,128)S(1)}, f32[128,128]{1,0:T(8,128)}, u32[]{:S(2)}) %copy-start.2) | copy-done | bytes 65560
  3.0 0.7 %copy-done.4 = f32[128]{0:T(128)S(1)} copy-done((f32[128]{0:T(128)S(1)}, f32[128]{0:T(128)}, u32[]{:S(2)}) %copy-start.4) | copy-done | bytes 536
  3.7 0.8 %copy-done.6 = f32[128,128]{1,0:T(8,128)S(1)} copy-done((f32[128,128]{1,0:T(8,128)S(1)}, f32[128,128]{1,0:T(8,128)}, u32[]{:S(2)}) %copy-start.6) | copy-done | bytes 65560
  4.5 0.7 %copy-done.7 = s32[3,64]{1,0:T(4,128)S(1)} copy-done((s32[3,64]{1,0:T(4,128)S(1)}, s32[3,64]{1,0:T(4,128)}, u32[]{:S(2)}) %copy-start.7) | copy-done | bytes 792
  5.2 0.7 %copy-done.8 = f32[128]{0:T(128)S(1)} copy-done((f32[128]{0:T(128)S(1)}, f32[128]{0:T(128)}, u32[]{:S(2)}) %copy-start.8) | copy-done | bytes 536
  5.8 3.4 %k_block.1.own_ref = f32[3,136,128]{2,1,0:T(8,128)S(1)} custom-call(s32[3,64]{1,0:T(4,128)S(1)} %copy-done.7, s32[1]{0:T(128)S(6)} %copy.11.sensors_ref, f32[3,64,128]{2,1,0:T(8,128)S(1)} %copy-done, s32[3,64]{1,0:T(4,128)S(1)} %copy-done.7, f32[1,128]{1,0:T(1,128)S(1)} %bitcast.5, f32[128,128]{1,0:T(8,128)S(1)} %copy-done.2, f32[1,128]{1,0:T(1,128)S(1)} %bitcast.9, ...), custom_call_target="tpu_custom_call" | custom-call | flops 1000000000 | bytes 1000000 | tf_op jit(solution)/shard_map/k_block/pallas_call | solution.py:426
  9.2 3.3 %collective-permute-start = (f32[3,136,128]{2,1,0:T(8,128)S(1)}, f32[3,136,128]{2,1,0:T(8,128)S(1)}, u32[]{:S(2)}, u32[]{:S(2)}) collective-permute-start(f32[3,136,128]{2,1,0:T(8,128)S(1)} %k_block.1.own_ref), channel_id=1, source_target_pairs={{0,1},{1,0},{2,3},{3,2},{4,5},{5,4},{6,7},{7,6},{8,9},{9,8},{10,11... | collective-permute-start | bytes 626696 | tf_op jit(solution)/shard_map/ppermute | solution.py:417
  12.6 1.1 %collective-permute-done.other_ref.mate_ref = f32[3,136,128]{2,1,0:T(8,128)S(1)} collective-permute-done((f32[3,136,128]{2,1,0:T(8,128)S(1)}, f32[3,136,128]{2,1,0:T(8,128)S(1)}, u32[]{:S(2)}, u32[]{:S(2)}) %collective-permute-start) | collective-permute-done | bytes 208928 | tf_op jit(solution)/shard_map/ppermute | solution.py:417
  13.6 0.2 k_core.1.own_ref
  13.9 1.1 %collective-permute-start.3 = (f32[3,136,128]{2,1,0:T(8,128)S(1)}, f32[3,136,128]{2,1,0:T(8,128)S(1)}, u32[]{:S(2)}, u32[]{:S(2)}) collective-permute-start(f32[3,136,128]{2,1,0:T(8,128)S(1)} %k_core.1.own_ref), channel_id=1, source_target_pairs={{0,6},{2,0},{4,2},{6,4},{1,7},{3,1},{5,3},{7,5},{8,14},{10,8},{12,... | collective-permute-start | bytes 626696 | tf_op jit(solution)/shard_map/ppermute | solution.py:417
  15.0 0.3 collective-permute-start.2
  15.3 0.7 %collective-permute-start.1 = (f32[3,136,128]{2,1,0:T(8,128)S(1)}, f32[3,136,128]{2,1,0:T(8,128)S(1)}, u32[]{:S(2)}, u32[]{:S(2)}) collective-permute-start(f32[3,136,128]{2,1,0:T(8,128)S(1)} %k_core.1.own_ref), channel_id=1, source_target_pairs={{0,2},{2,4},{4,6},{6,0},{1,3},{3,5},{5,7},{7,1},{8,10},{10,12},{12... | collective-permute-start | bytes 626696 | tf_op jit(solution)/shard_map/ppermute | solution.py:417
  16.0 4.3 %collective-permute-done.3.r3_ref = f32[3,136,128]{2,1,0:T(8,128)S(1)} collective-permute-done((f32[3,136,128]{2,1,0:T(8,128)S(1)}, f32[3,136,128]{2,1,0:T(8,128)S(1)}, u32[]{:S(2)}, u32[]{:S(2)}) %collective-permute-start.3) | collective-permute-done | bytes 208928 | tf_op jit(solution)/shard_map/ppermute | solution.py:417
  20.3 2.2 %collective-permute-done.2.r2_ref = f32[3,136,128]{2,1,0:T(8,128)S(1)} collective-permute-done((f32[3,136,128]{2,1,0:T(8,128)S(1)}, f32[3,136,128]{2,1,0:T(8,128)S(1)}, u32[]{:S(2)}, u32[]{:S(2)}) %collective-permute-start.2) | collective-permute-done | bytes 208928 | tf_op jit(solution)/shard_map/ppermute | solution.py:417
  22.6 5.5 %collective-permute-done.1.r1_ref = f32[3,136,128]{2,1,0:T(8,128)S(1)} collective-permute-done((f32[3,136,128]{2,1,0:T(8,128)S(1)}, f32[3,136,128]{2,1,0:T(8,128)S(1)}, u32[]{:S(2)}, u32[]{:S(2)}) %collective-permute-start.1) | collective-permute-done | bytes 208928 | tf_op jit(solution)/shard_map/ppermute | solution.py:417
  28.0 0.8 %k_total.1.own_ref = f32[3,136,128]{2,1,0:T(8,128)S(1)} custom-call(f32[3,136,128]{2,1,0:T(8,128)S(1)} %k_core.1.own_ref, f32[3,136,128]{2,1,0:T(8,128)S(1)} %collective-permute-done.1.r1_ref, f32[3,136,128]{2,1,0:T(8,128)S(1)} %collective-permute-done.2.r2_ref, f32[3,136,128]{2,1,0:T(8,128)S(1)} %collective-permute-done.3.r3_ref), custom_call_target="tpu_custom_call" | custom-call | flops 10000000 | bytes 1000000 | tf_op jit(solution)/shard_map/k_total/pallas_call | solution.py:449
  28.9 0.0 copy-start.1
  28.9 0.0 copy-start.3
  28.9 0.0 copy-start.5
  28.9 2.6 %collective-permute-start.6 = (f32[3,136,128]{2,1,0:T(8,128)S(1)}, f32[3,136,128]{2,1,0:T(8,128)S(1)}, u32[]{:S(2)}, u32[]{:S(2)}) collective-permute-start(f32[3,136,128]{2,1,0:T(8,128)S(1)} %k_total.1.own_ref), channel_id=1, source_target_pairs={{0,24},{8,0},{16,8},{24,16},{1,25},{9,1},{17,9},{25,17},{2,26},{10... | collective-permute-start | bytes 626696 | tf_op jit(solution)/shard_map/ppermute | solution.py:417
  31.5 0.5 collective-permute-start.5
  32.0 0.6 %collective-permute-start.4 = (f32[3,136,128]{2,1,0:T(8,128)S(1)}, f32[3,136,128]{2,1,0:T(8,128)S(1)}, u32[]{:S(2)}, u32[]{:S(2)}) collective-permute-start(f32[3,136,128]{2,1,0:T(8,128)S(1)} %k_total.1.own_ref), channel_id=1, source_target_pairs={{0,8},{8,16},{16,24},{24,0},{1,9},{9,17},{17,25},{25,1},{2,10},{10... | collective-permute-start | bytes 626696 | tf_op jit(solution)/shard_map/ppermute | solution.py:417
  32.6 6.4 %k_tables.1 = (f32[48,128,128]{2,1,0:T(8,128)S(1)}, f32[48,128]{1,0:T(8,128)S(1)}, bf16[128,768]{1,0:T(8,128)(2,1)S(1)}, f32[4,48,128]{2,1,0:T(8,128)S(1)}, f32[...) custom-call(s32[3,64]{1,0:T(4,128)S(1)} %copy-done.7, ...), custom_call_target="tpu_custom_call" | custom-call | flops 6000000000 | bytes 10000000 | tf_op jit(solution)/shard_map/k_tables/pallas_call | solution.py:428
  39.0 1.2 %k_entry.1.entry_ref = f32[3,136,128]{2,1,0:T(8,128)S(1)} custom-call(f32[3,136,128]{2,1,0:T(8,128)S(1)} %k_core.1.own_ref, f32[3,136,128]{2,1,0:T(8,128)S(1)} %collective-permute-done.1.r1_ref, f32[3,136,128]{2,1,0:T(8,128)S(1)} %collective-permute-done.2.r2_ref, f32[3,136,128]{2,1,0:T(8,128)S(1)} %collective-permute-done.3.r3_ref, ...), custom_call_target="tpu_custom_call" | custom-call | flops 100000000 | bytes 1000000 | tf_op jit(solution)/shard_map/k_entry/pallas_call | solution.py:451
  40.2 0.0 collective-permute-done.6.r3_ref
  40.2 0.0 collective-permute-done.5.r2_ref
  40.2 4.3 %collective-permute-done.4.r1_ref = f32[3,136,128]{2,1,0:T(8,128)S(1)} collective-permute-done((f32[3,136,128]{2,1,0:T(8,128)S(1)}, f32[3,136,128]{2,1,0:T(8,128)S(1)}, u32[]{:S(2)}, u32[]{:S(2)}) %collective-permute-start.4) | collective-permute-done | bytes 208928 | tf_op jit(solution)/shard_map/ppermute | solution.py:417
  44.5 2.5 %k_filter.1 = (f32[32,8,128]{2,1,0:T(8,128)S(1)}, f32[4,48,128]{2,1,0:T(8,128)S(1)}, f32[48,128]{1,0:T(8,128)S(1)}, f32[8,128]{1,0:T(8,128)S(1)}) custom-call(s32[1]{0:T(128)S(6)} %copy.11.sensors_ref, f32[3,136,128]{2,1,0:T(8,128)S(1)} %k_total.1.own_ref, f32[3,136,128]{2,1,0:T(8,128)S(1)} %collective-permute-done.4.r1_ref, ...), custom_call_target="tpu_custom_call" | custom-call | flops 10000000 | bytes 1000000 | tf_op jit(solution)/shard_map/k_filter/pallas_call | solution.py:452
  47.0 10.9 %all_to_all.5.got_ref = f32[32,8,128]{2,1,0:T(8,128)S(1)} all-to-all(f32[32,8,128]{2,1,0:T(8,128)S(1)} %get-tuple-element.27), channel_id=1, replica_groups=mesh['cluster'=8,'tm_0'=4,'tm_1'=4,'tm_2'=2] {'tm_0','tm_1','tm_2'}, dimensions={0} | all-to-all | bytes 262144 | tf_op jit(solution)/shard_map/all_to_all | solution.py:464
  57.9 1.6 %k_smooth.1 = (f32[3,64,128]{2,1,0:T(8,128)}, f32[1,128]{1,0:T(1,128)}, f32[1,128]{1,0:T(1,128)}) custom-call(s32[1]{0:T(128)S(6)} %copy.11.sensors_ref, f32[32,8,128]{2,1,0:T(8,128)S(1)} %all_to_all.5.got_ref, f32[4,48,128]{2,1,0:T(8,128)S(1)} %get-tuple-element.28.local_ref, f32[48,128]{1,0:T(8,128)S(1)} %get-tuple-element.29.suffix_ref, ...), custom_call_target="tpu_custom_call" | custom-call | flops 10000000 | bytes 1000000 | tf_op jit(solution)/shard_map/k_smooth/pallas_call | solution.py:465
  (8 shorter events, 0.0 us)
Async XLA Ops:
  1.3 0.9 %copy-start = (f32[3,64,128]{2,1,0:T(8,128)S(1)}, f32[3,64,128]{2,1,0:T(8,128)}, u32[]{:S(2)}) copy-start(f32[3,64,128]{2,1,0:T(8,128)} %obs_ref.5) | copy-start | bytes 294916
  2.2 0.8 %copy-start.2 = (f32[128,128]{1,0:T(8,128)S(1)}, f32[128,128]{1,0:T(8,128)}, u32[]{:S(2)}) copy-start(f32[128,128]{1,0:T(8,128)} %dyn_ref.5) | copy-start | bytes 196612
  3.0 0.7 %copy-start.4 = (f32[128]{0:T(128)S(1)}, f32[128]{0:T(128)}, u32[]{:S(2)}) copy-start(f32[128]{0:T(128)} %param.11) | copy-start | bytes 1540
  3.7 0.8 %copy-start.6 = (f32[128,128]{1,0:T(8,128)S(1)}, f32[128,128]{1,0:T(8,128)}, u32[]{:S(2)}) copy-start(f32[128,128]{1,0:T(8,128)} %map_ref.3) | copy-start | bytes 196612
  4.5 0.7 %copy-start.7 = (s32[3,64]{1,0:T(4,128)S(1)}, s32[3,64]{1,0:T(4,128)}, u32[]{:S(2)}) copy-start(s32[3,64]{1,0:T(4,128)} %pres_ref.3) | copy-start | bytes 2308
  5.2 0.7 %copy-start.8 = (f32[128]{0:T(128)S(1)}, f32[128]{0:T(128)}, u32[]{:S(2)}) copy-start(f32[128]{0:T(128)} %param.13) | copy-start | bytes 1540
  9.2 4.4 %collective-permute-start = (f32[3,136,128]{2,1,0:T(8,128)S(1)}, f32[3,136,128]{2,1,0:T(8,128)S(1)}, u32[]{:S(2)}, u32[]{:S(2)}) collective-permute-start(f32[3,136,128]{2,1,0:T(8,128)S(1)} %k_block.1.own_ref), channel_id=1, source_target_pairs={{0,1},{1,0},{2,3},{3,2},{4,5},{5,4},{6,7},{7,6},{8,9},{9,8},{10,11... | collective-permute-start | bytes 626696 | tf_op jit(solution)/shard_map/ppermute | solution.py:417
  13.9 6.5 %collective-permute-start.3 = (f32[3,136,128]{2,1,0:T(8,128)S(1)}, f32[3,136,128]{2,1,0:T(8,128)S(1)}, u32[]{:S(2)}, u32[]{:S(2)}) collective-permute-start(f32[3,136,128]{2,1,0:T(8,128)S(1)} %k_core.1.own_ref), channel_id=1, source_target_pairs={{0,6},{2,0},{4,2},{6,4},{1,7},{3,1},{5,3},{7,5},{8,14},{10,8},{12,... | collective-permute-start | bytes 626696 | tf_op jit(solution)/shard_map/ppermute | solution.py:417
  15.0 7.6 %collective-permute-start.2 = (f32[3,136,128]{2,1,0:T(8,128)S(1)}, f32[3,136,128]{2,1,0:T(8,128)S(1)}, u32[]{:S(2)}, u32[]{:S(2)}) collective-permute-start(f32[3,136,128]{2,1,0:T(8,128)S(1)} %k_core.1.own_ref), channel_id=1, source_target_pairs={{0,4},{2,6},{4,0},{6,2},{1,5},{3,7},{5,1},{7,3},{8,12},{10,14},{12... | collective-permute-start | bytes 626696 | tf_op jit(solution)/shard_map/ppermute | solution.py:417
  15.3 12.7 %collective-permute-start.1 = (f32[3,136,128]{2,1,0:T(8,128)S(1)}, f32[3,136,128]{2,1,0:T(8,128)S(1)}, u32[]{:S(2)}, u32[]{:S(2)}) collective-permute-start(f32[3,136,128]{2,1,0:T(8,128)S(1)} %k_core.1.own_ref), channel_id=1, source_target_pairs={{0,2},{2,4},{4,6},{6,0},{1,3},{3,5},{5,7},{7,1},{8,10},{10,12},{12... | collective-permute-start | bytes 626696 | tf_op jit(solution)/shard_map/ppermute | solution.py:417
  28.9 15.7 %copy-start.1 = (f32[3,64,128]{2,1,0:T(8,128)S(1)}, f32[3,64,128]{2,1,0:T(8,128)}, u32[]{:S(2)}) copy-start(f32[3,64,128]{2,1,0:T(8,128)} %obs_ref.5) | copy-start | bytes 294916
  28.9 15.6 %copy-start.3 = (f32[3,128]{1,0:T(4,128)S(1)}, f32[3,128]{1,0:T(4,128)}, u32[]{:S(2)}) copy-start(f32[3,128]{1,0:T(4,128)} %init_ref.1) | copy-start | bytes 4612
  28.9 15.6 %copy-start.5 = (f32[128]{0:T(128)S(1)}, f32[128]{0:T(128)}, u32[]{:S(2)}) copy-start(f32[128]{0:T(128)} %param.11) | copy-start | bytes 1540
  28.9 11.3 %collective-permute-start.6 = (f32[3,136,128]{2,1,0:T(8,128)S(1)}, f32[3,136,128]{2,1,0:T(8,128)S(1)}, u32[]{:S(2)}, u32[]{:S(2)}) collective-permute-start(f32[3,136,128]{2,1,0:T(8,128)S(1)} %k_total.1.own_ref), channel_id=1, source_target_pairs={{0,24},{8,0},{16,8},{24,16},{1,25},{9,1},{17,9},{25,17},{2,26},{10... | collective-permute-start | bytes 626696 | tf_op jit(solution)/shard_map/ppermute | solution.py:417
  31.5 8.7 %collective-permute-start.5 = (f32[3,136,128]{2,1,0:T(8,128)S(1)}, f32[3,136,128]{2,1,0:T(8,128)S(1)}, u32[]{:S(2)}, u32[]{:S(2)}) collective-permute-start(f32[3,136,128]{2,1,0:T(8,128)S(1)} %k_total.1.own_ref), channel_id=1, source_target_pairs={{0,16},{8,24},{16,0},{24,8},{1,17},{9,25},{17,1},{25,9},{2,18},{10... | collective-permute-start | bytes 626696 | tf_op jit(solution)/shard_map/ppermute | solution.py:417
  32.0 12.5 %collective-permute-start.4 = (f32[3,136,128]{2,1,0:T(8,128)S(1)}, f32[3,136,128]{2,1,0:T(8,128)S(1)}, u32[]{:S(2)}, u32[]{:S(2)}) collective-permute-start(f32[3,136,128]{2,1,0:T(8,128)S(1)} %k_total.1.own_ref), channel_id=1, source_target_pairs={{0,8},{8,16},{16,24},{24,0},{1,9},{9,17},{17,25},{25,1},{2,10},{10... | collective-permute-start | bytes 626696 | tf_op jit(solution)/shard_map/ppermute | solution.py:417
where the time goes:
time: 59.8 us; the launch traced here: 59.5 us
  waiting for transfers between devices  17.5 us (29%)
  Pallas kernels  16.1 us (27%)
  blocking collectives  10.9 us (18%)
  starting transfers between devices  9.13 us (15%)
  local copies, waits for them, and re-layouts  4.58 us (8%)
  between operations  1.38 us (2%)
    ppermute x7, waiting for transfers between devices, shifted(): return lax.ppermute(a, axis, [(i, (i + by) % count) for i in range(count)])  17.5 us
    all_to_all x1, blocking collectives, local(): got = lax.all_to_all(send, TM, 0, 0, tiled=True)  10.9 us
    ppermute x7, starting transfers between devices, shifted(): return lax.ppermute(a, axis, [(i, (i + by) % count) for i in range(count)])  9.13 us
    pallas_call x1, Pallas kernels, local(): call(k_tables, 'k_tables', specs, (out((ROWS, N, N)), out((ROWS, N)), out...  6.4 us
    unnamed x18, local copies, waits for them, and re-layouts  4.58 us
    pallas_call x1, Pallas kernels, local(): call(k_block, 'k_block', specs, msg, TREE_SCRATCH, 10 ** 9, 10 ** 6)(*args)  3.37 us
    pallas_call x1, Pallas kernels, local(): call(k_filter, 'k_filter', [SM] + [VM] * 17, (out((BLOCKS, 8, N)), out((S...  2.46 us
    pallas_call x1, Pallas kernels, local(): call(k_smooth, 'k_smooth', [SM] + [VM] * 8, (out((SEQ, STEPS, N)), out((1...  1.61 us
  transfers between devices with their start and end apart: 7, of which 5 were waited for; matrix products, arithmetic and copies ran while one was open for 0% of the time, Pallas kernels for 13%

commit v1 on v0

v1 whole, which is shorter than its diff:
```python
import jax
import jax.numpy as jnp
from jax import lax
from jax.experimental import pallas as pl
from jax.experimental.pallas import tpu as pltpu
from jax.sharding import Mesh
from jax.sharding import PartitionSpec as P

F32, BF16 = jnp.float32, jnp.bfloat16
TM = ("tm_0", "tm_1", "tm_2")
N = 128
SEQ, STEPS, SUB = 3, 64, 4
LEAVES = STEPS // SUB
ROWS = SEQ * LEAVES
HALF = N // 2
BLOCKS = 32
VMEM_LIMIT = 40 * 1024 * 1024


def dot(a, b):
    return lax.dot(a, b, preferred_element_type=F32)


def lanes(*parts):
    return jnp.concatenate(parts, axis=1)


def stacked(*parts):
    return jnp.concatenate(parts, axis=0)


def split2(a):
    hi = a.astype(BF16)
    return hi, (a - hi.astype(F32)).astype(BF16)


def split3(a):
    hi = a.astype(BF16)
    rest = a - hi.astype(F32)
    mid = rest.astype(BF16)
    return hi, mid, (rest - mid.astype(F32)).astype(BF16)


def pair(a):
    return lanes(*split2(a))


def whole(x):
    n = x.shape[1] // 2
    return x[:, :n].astype(F32) + x[:, n:].astype(F32)


def mul_pair(x, y):
    d = dot(x, stacked(y, y))
    n = y.shape[1] // 2
    return d[:, :n] + d[:, n:]


def mul_exact(a, b):
    a0, a1, a2 = split3(a)
    b0, b1, b2 = split3(b)
    n = b.shape[1]
    y = lanes(b0, b1)
    d = dot(lanes(a0, a1), stacked(y, y))
    return d[:, :n] + (d[:, n:] + dot(lanes(a0, a2), stacked(b2, b0)))


def apply_row(row, matrix):
    column = jnp.transpose(jnp.broadcast_to(row, (N, N)))
    return jnp.sum(column * matrix, axis=0, keepdims=True)


def step_major(ref, i):
    return stacked(*(ref[b, pl.ds(i, LEAVES, stride=SUB), :] for b in range(SEQ)))


def pick(flag, a, b):
    return jnp.where(flag, a, b)


def on_row(sensors_ref):
    return (lax.broadcasted_iota(jnp.int32, (1, N), 1) < sensors_ref[0]).astype(F32)


def identity(rows=N):
    shape = (rows, N)
    return (
        lax.broadcasted_iota(jnp.int32, shape, 0) == lax.broadcasted_iota(jnp.int32, shape, 1)
    ).astype(F32)


def leaf_number(flags, b, j):
    at = 0
    for i in range(SUB):
        at = at * 2 + flags[b, SUB * j + i]
    return at


def joined(left, left_off, right, right_off):
    off = pair(jnp.broadcast_to(left_off, (16, N)))
    got = mul_pair(stacked(left, off), right)
    return got[:N], got[N : N + 1] + right_off


LEVELS = ((0, 24), (24, 12), (36, 6))
OFFS = (0, 48, 72, 84)
PART = HALF + 8


def k_first(dyn_ref, dynt_ref, near_ref, d4_ref, resid_ref):
    dyn = dyn_ref[...]
    dyn_t = jnp.transpose(dyn)
    dynt_ref[...] = dyn_t
    resid_ref[...] = pair(identity() - mul_exact(dyn_t, dyn))
    d2 = mul_exact(dyn, dyn)
    d34 = mul_exact(d2, lanes(dyn, d2))
    d4_ref[...] = d34[:, N:]
    for i, a in enumerate((dyn, d2, d34[:, :N], d34[:, N:])):
        near_ref[i] = pair(a)


def k_block(
    flags, sensors_ref, obs_raw, pres_ref, lp_ref, dynt_ref, pv_ref, map_ref,
    root_ref, table, nodes, offs, step_ref, u_ref, mask_ref, obs_ref, rows_ref, mask_scr, u_scr,
):
    on = on_row(sensors_ref)
    weight = jnp.exp(lp_ref[...]) * on
    pv, obs_map = pv_ref[...], map_ref[...]
    dyn_t = dynt_ref[...]
    out_t = mul_exact(dyn_t, jnp.transpose(obs_map))
    filt_t = dyn_t - mul_exact(out_t * weight, obs_map) * pv
    rows_ref[...] = stacked(on, weight, lp_ref[...], jnp.zeros((5, N), F32))
    step_ref[...] = pair(lanes(dyn_t, filt_t, out_t))
    seen = pres_ref[...].astype(F32)
    seen = jnp.transpose(stacked(seen, jnp.zeros((8 - SEQ, STEPS), F32)))
    y = pair(obs_map)
    for b in range(SEQ):
        mask = jnp.broadcast_to(seen[:, b : b + 1], (STEPS, N))
        mask_scr[b] = mask
        u_scr[b] = mul_pair(pair(obs_raw[b] * weight), y) * pv * mask
    for i in range(SUB):
        u_ref[i] = step_major(u_scr, i)
        mask_ref[i] = step_major(mask_scr, i)
        obs_ref[i] = step_major(obs_raw, i)
    two = mul_exact(stacked(dyn_t, filt_t), lanes(dyn_t, filt_t))
    twos = [two[i * N : (i + 1) * N, j * N : (j + 1) * N] for i in (0, 1) for j in (0, 1)]
    wide = lanes(*twos)
    for i in range(4):
        four = mul_exact(twos[i], wide)
        for j in range(4):
            table[4 * i + j] = pair(four[:, j * N : (j + 1) * N])
    y = pair(lanes(dyn_t, filt_t))
    z = u_ref[0]
    for i in range(1, SUB):
        d = mul_pair(pair(z), y)
        z = pick(mask_ref[i] > 0.5, d[:, N:], d[:, :N]) + u_ref[i]
    offs[0:ROWS, :] = z

    def leaf(k):
        return table[leaf_number(flags, k // LEAVES, k % LEAVES)]

    get = leaf
    for level in range(4):
        count = ROWS >> (level + 1)
        for k in range(count):
            at = OFFS[level] + 2 * k
            matrix, off = joined(
                get(2 * k), offs[at : at + 1, :], get(2 * k + 1), offs[at + 1 : at + 2, :]
            )
            if level == 3:
                root_ref[k, 0:N, :] = matrix
                root_ref[k, N : N + 8, :] = jnp.broadcast_to(off, (8, N))
            else:
                nodes[LEVELS[level][0] + k] = pair(matrix)
                to = OFFS[level + 1] + k
                offs[to : to + 1, :] = off
        if level < 3:
            get = lambda k, level=level: nodes[LEVELS[level][0] + k]


def put_halves(refs, b, matrix, off):
    off = jnp.broadcast_to(off, (8, N))
    for c, ref in enumerate(refs):
        ref[b, 0:HALF, :] = matrix[c * HALF : (c + 1) * HALF]
        ref[b, HALF:PART, :] = off


def from_halves(low_ref, high_ref, b):
    return stacked(low_ref[b, 0:HALF, :], high_ref[b, 0:HALF, :]), low_ref[b, HALF : HALF + 1, :]


def in_order(mine_ref, mate_ref, b):
    first = lax.axis_index("tm_2") == 0
    mine, mate = mine_ref[b, 0:HALF, :], mate_ref[b, 0:HALF, :]
    matrix = stacked(pick(first, mine, mate), pick(first, mate, mine))
    return matrix, mine_ref[b, HALF : HALF + 1, :]


def then(p, q):
    return joined(pair(p[0]), p[1], pair(q[0]), q[1])


def then_half(p, q, ref, b):
    left = pick(lax.axis_index("tm_2") == 0, p[0][:HALF], p[0][HALF:])
    got = mul_pair(
        stacked(pair(left), pair(jnp.broadcast_to(p[1], (16, N)))), pair(q[0])
    )
    ref[b, 0:HALF, :] = got[:HALF]
    ref[b, HALF:PART, :] = got[HALF:PART] + q[1]


def k_core(own_ref, mate_ref, mine_ref, low_ref, high_ref):
    first = lax.axis_index("tm_2") == 0
    for b in range(SEQ):
        own, mate = own_ref[b], mate_ref[b]
        p, q = pick(first, own, mate), pick(first, mate, own)
        matrix, off = then((p[:N], p[N : N + 1]), (q[:N], q[N : N + 1]))
        put_halves((low_ref, high_ref), b, matrix, off)
        mine_ref[b, 0:HALF, :] = pick(first, matrix[:HALF], matrix[HALF:])
        mine_ref[b, HALF:PART, :] = jnp.broadcast_to(off, (8, N))


def k_total(low_ref, high_ref, r1, r2, r3, m1, m2, m3, out_ref, full_ref, maps, offs):
    me = lax.axis_index("tm_1")
    for b in range(SEQ):
        for d, (r, m) in enumerate(((r1, m1), (r2, m2), (r3, m3))):
            matrix, off = in_order(r, m, b)
            slot = lax.rem(me + 3 - d, 4)
            maps[slot, b] = matrix
            offs[slot, b] = jnp.broadcast_to(off, (8, N))
            full_ref[d, b, 0:N, :] = matrix
            full_ref[d, b, N : N + 8, :] = jnp.broadcast_to(off, (8, N))
        matrix, off = from_halves(low_ref, high_ref, b)
        maps[me, b] = matrix
        offs[me, b] = jnp.broadcast_to(off, (8, N))
    for b in range(SEQ):
        p = [(maps[k, b], offs[k, b, 0:1, :]) for k in range(4)]
        then_half(then(p[0], p[1]), then(p[2], p[3]), out_ref, b)


def k_prefix(chip_ref, flags, table, nodes, offs, pre_ref, preoff_ref):
    preoff_ref[...] = jnp.zeros_like(preoff_ref)
    for b in range(SEQ):
        pre_ref[b * LEAVES] = jnp.zeros((N, N), F32)
        for level in (3, 2, 1, 0):
            parents = 8 >> level
            span = LEAVES // parents
            for k in range(parents):
                at = b * LEAVES + k * span
                left = b * 2 * parents + 2 * k
                off = offs[OFFS[level] + left : OFFS[level] + left + 1, :]
                if level == 0:
                    got = table[leaf_number(flags, left // LEAVES, left % LEAVES)]
                else:
                    got = nodes[LEVELS[level - 1][0] + left]
                if k == 0:
                    matrix = whole(got)
                else:
                    matrix, off = joined(
                        pair(pre_ref[at]), preoff_ref[at : at + 1, :], got, off
                    )
                to = at + span // 2
                pre_ref[to] = matrix
                preoff_ref[to : to + 1, :] = off


def k_powers(after_ref, d4_ref, far_ref, reach_ref, cross_ref):
    eye = identity()
    far_ref[0] = eye
    far_ref[1] = d4_ref[...]
    for have in (1, 2, 4, 8):
        last = far_ref[have]
        for k in range(1, have + 1):
            got = mul_exact(last, far_ref[k])
            if have + k < LEAVES:
                far_ref[have + k] = got
    for i, k in enumerate((1, 2, 4, 8)):
        reach_ref[i] = pair(far_ref[k])
    cross_ref[0] = pair(eye)
    powers = [None, got]
    for k in range(2, 9):
        powers.append(mul_exact(powers[k // 2], powers[k - k // 2]))
    for k in range(1, 8):
        cross_ref[k] = pair(powers[k])
    w16 = mul_exact(powers[8], powers[8])
    cross_ref[8] = pair(powers[8])
    cross_ref[9] = pair(w16)
    cross_ref[10] = pair(mul_exact(w16, powers[8]))


def k_entry(after_ref, full_ref, mate_ref, entry_ref, entryoff_ref):
    me, second = lax.axis_index("tm_1"), lax.axis_index("tm_2") == 1
    entryoff_ref[...] = jnp.zeros_like(entryoff_ref)
    for b in range(SEQ):
        so_far = (identity(), jnp.zeros((1, N), F32))
        for source, flag in (
            (full_ref.at[2], me >= 3), (full_ref.at[1], me >= 2), (full_ref.at[0], me >= 1),
            (mate_ref, second),
        ):
            got = then(so_far, (source[b, 0:N, :], source[b, N : N + 1, :]))
            so_far = (pick(flag, got[0], so_far[0]), pick(flag, got[1], so_far[1]))
        entry_ref[b] = so_far[0]
        entryoff_ref[b : b + 1, :] = so_far[1]


def k_filter(
    r1, r2, r3, m1, m2, m3, entry_ref, entryoff_ref, init_ref, obs_ref,
    rows_ref, dynt_ref, pre_ref, preoff_ref, step_ref, u_ref, mask_ref, near_ref, reach_ref,
    resid_ref, send_ref, local_ref, suffix_ref, final_ref,
):
    group = lax.axis_index("tm_0")
    last = (group == 3) & (lax.axis_index("tm_1") == 3) & (lax.axis_index("tm_2") == 1)
    starts = []
    for b in range(SEQ):
        row = init_ref[b : b + 1, :]
        for d, r, m in ((3, r3, m3), (2, r2, m2), (1, r1, m1)):
            matrix, off = in_order(r, m, b)
            row = pick(group >= d, apply_row(row, matrix) + off, row)
        starts.append(apply_row(row, entry_ref[b]) + entryoff_ref[b : b + 1, :])
    rows = []
    for b in range(SEQ):
        column = jnp.transpose(jnp.broadcast_to(starts[b], (N, N)))
        rows.append(starts[b])
        for j in range(1, LEAVES):
            k = b * LEAVES + j
            rows.append(
                jnp.sum(column * pre_ref[k], axis=0, keepdims=True) + preoff_ref[k : k + 1, :]
            )
    state = stacked(*rows)
    weight = rows_ref[1:2, :]
    step = step_ref[...]
    resid = resid_ref[...]
    square = jnp.zeros((ROWS, N), F32)
    seen = jnp.zeros((ROWS, N), F32)
    residuals = []
    for i in range(SUB):
        d = mul_pair(pair(state), step)
        mask = mask_ref[i]
        error = obs_ref[i] - d[:, 2 * N :]
        square = square + mask * (error * error)
        seen = seen + mask
        state = pick(mask > 0.5, d[:, N : 2 * N], d[:, :N]) + u_ref[i]
        residuals.append(mul_pair(pair(state), resid))
    square = jnp.sum(square, axis=0, keepdims=True) * weight
    seen = jnp.sum(seen, axis=0, keepdims=True)
    ends = stacked(*(state[(b + 1) * LEAVES - 1 : (b + 1) * LEAVES, :] for b in range(SEQ)))
    ends = stacked(ends, jnp.zeros((8 - SEQ, N), F32))
    final = mul_pair(pair(ends), pair(dynt_ref[...]))
    final_ref[...] = final
    y = near_ref[0]
    run = residuals[SUB - 1]
    local_ref[SUB - 1] = run
    for i in reversed(range(SUB - 1)):
        run = mul_pair(pair(run), y) + residuals[i]
        local_ref[i] = run
    place = lax.broadcasted_iota(jnp.int32, (ROWS, N), 0) % LEAVES
    for k, reach in enumerate((1, 2, 4, 8)):
        moved = mul_pair(pair(run), reach_ref[k])
        moved = pltpu.roll(moved, ROWS - reach, 0)
        run = run + pick(place < LEAVES - reach, moved, 0.0)
    suffix_ref[...] = run
    offsets = stacked(*(run[b * LEAVES : b * LEAVES + 1, :] for b in range(SEQ)))
    offsets = stacked(offsets, jnp.zeros((8 - SEQ, N), F32))
    half = mul_pair(pair(final), reach_ref[3])
    through = mul_pair(pair(half), reach_ref[3])
    offsets = offsets + pick(last, through, 0.0)
    packed = stacked(offsets[:SEQ], square, seen, jnp.zeros((8 - SEQ - 2, N), F32))
    send_ref[...] = jnp.broadcast_to(packed[None], (BLOCKS, 8, N))


def k_smooth(
    got_ref, local_ref, suffix_ref, final_ref, rows_ref, far_ref, near_ref, cross_ref,
    out_ref, prec_ref, lik_ref,
):
    me = (lax.axis_index("tm_0") * 4 + lax.axis_index("tm_1")) * 2 + lax.axis_index("tm_2")
    on, lp = rows_ref[0:1, :], rows_ref[2:3, :]
    acc = jnp.zeros((4 * 8, N), F32)
    for h in range(8):
        parts = []
        for g in range(4):
            at = me + 1 + 8 * g + h
            parts.append(pick(at < BLOCKS, got_ref[jnp.minimum(at, BLOCKS - 1)], 0.0))
        acc = acc + mul_pair(pair(stacked(*parts)), cross_ref[h])
    leaving = acc[0:8]
    for g in range(1, 4):
        leaving = leaving + mul_pair(pair(acc[8 * g : 8 * g + 8]), cross_ref[7 + g])
    leaving = pick(me == BLOCKS - 1, final_ref[...], leaving)
    rows = []
    for b in range(SEQ):
        column = jnp.transpose(jnp.broadcast_to(leaving[b : b + 1, :], (N, N)))
        for j in range(LEAVES - 1):
            k = b * LEAVES + j
            rows.append(
                jnp.sum(column * far_ref[LEAVES - 1 - j], axis=0, keepdims=True)
                + suffix_ref[k + 1 : k + 2, :]
            )
        rows.append(leaving[b : b + 1, :])
    x = pair(stacked(*rows))
    for i in range(SUB):
        got = mul_pair(x, near_ref[SUB - 1 - i]) + local_ref[i]
        for b in range(SEQ):
            out_ref[b, pl.ds(i, LEAVES, stride=SUB), :] = got[b * LEAVES : (b + 1) * LEAVES]
    sums = jnp.sum(got_ref[...], axis=0)
    square, seen = sums[SEQ : SEQ + 1], sums[SEQ + 1 : SEQ + 2]
    total = float(SEQ * STEPS * BLOCKS)
    prec_ref[...] = lp + (0.5 / total) * on * (seen - square)
    lik = jnp.sum(on * (seen * lp - square), axis=1, keepdims=True) * (0.5 / (total * N))
    lik_ref[...] = jnp.broadcast_to(lik, (1, N))


VM = pl.BlockSpec(memory_space=pltpu.VMEM)
SM = pl.BlockSpec(memory_space=pltpu.SMEM)


def call(kernel, name, specs, shapes, scratch=(), flops=0, moved=0):
    return pl.pallas_call(
        kernel,
        out_shape=shapes,
        in_specs=specs,
        out_specs=jax.tree.map(lambda _: VM, shapes),
        scratch_shapes=list(scratch),
        compiler_params=pltpu.CompilerParams(vmem_limit_bytes=VMEM_LIMIT),
        cost_estimate=pl.CostEstimate(flops=flops, bytes_accessed=moved, transcendentals=0),
        name=name,
    )


def out(shape, dtype=F32):
    return jax.ShapeDtypeStruct(shape, dtype)


def shifted(a, axis, by):
    count = lax.axis_size(axis)
    return lax.ppermute(a, axis, [(i, (i + by) % count) for i in range(count)])


def exchanged(mine, axis, work):
    got = [shifted(mine, axis, d) for d in (1, 2, 3)]
    done = work(mine)
    tied, done = lax.optimization_barrier((got, done))
    return got, [shifted(a, "tm_2", 1) for a in tied], done


def local(obs, present, sensors, log_prec, dynamics, prior_var, obs_map, init_state):
    lp, pv = log_prec.reshape(1, N), prior_var.reshape(1, N)
    part = out((SEQ, PART, N))
    square = out((N, N))
    dyn_t, near, d4, resid = call(
        k_first,
        "k_first",
        [VM],
        (square, out((4, N, 2 * N), BF16), square, out((N, 2 * N), BF16)),
        (),
        4 * 10**9,
        10**7,
    )(dynamics)
    root, table, nodes, offs, step, u, mask, obs_s, rows = call(
        k_block,
        "k_block",
        [SM] * 2 + [VM] * 6,
        (
            out((SEQ, N + 8, N)),
            out((16, N, 2 * N), BF16),
            out((42, N, 2 * N), BF16),
            out((96, N)),
            out((N, 6 * N), BF16),
            out((SUB, ROWS, N)),
            out((SUB, ROWS, N)),
            out((SUB, ROWS, N)),
            out((8, N)),
        ),
        [pltpu.VMEM((SEQ, STEPS, N), F32), pltpu.VMEM((SEQ, STEPS, N), F32)],
        10**9,
        10**6,
    )(present, sensors, obs, present, lp, dyn_t, pv, obs_map)
    mate = shifted(root, "tm_2", 1)
    chip, low, high = call(k_core, "k_core", [VM] * 2, (part, part, part), (), 10**7, 10**6)(
        root, mate
    )
    prefix = call(
        k_prefix,
        "k_prefix",
        [VM, SM] + [VM] * 3,
        (out((ROWS, N, N)), out((ROWS, N))),
        (),
        3 * 10**9,
        10**7,
    )
    got, mates, (pre, preoff) = exchanged(
        chip, "tm_1", lambda a: prefix(a, present, table, nodes, offs)
    )
    group, full = call(
        k_total,
        "k_total",
        [VM] * 8,
        (part, out((3, SEQ, N + 8, N))),
        [pltpu.VMEM((4, SEQ, N, N), F32), pltpu.VMEM((4, SEQ, 8, N), F32)],
        10**8,
        10**6,
    )(low, high, *got, *mates)
    powers = call(
        k_powers,
        "k_powers",
        [VM] * 2,
        (out((LEAVES, N, N)), out((4, N, 2 * N), BF16), out((11, N, 2 * N), BF16)),
        (),
        3 * 10**9,
        10**7,
    )
    entries = call(
        k_entry, "k_entry", [VM] * 3, (out((SEQ, N, N)), out((8, N))), (), 10**9, 10**7
    )
    got, mates, ((far, reach, cross), (entry, entryoff)) = exchanged(
        group, "tm_0", lambda a: (powers(a, d4), entries(a, full, mate))
    )
    send, near_sums, suffix, final = call(
        k_filter,
        "k_filter",
        [VM] * 20,
        (out((BLOCKS, 8, N)), out((SUB, ROWS, N)), out((ROWS, N)), out((8, N))),
        (),
        10**7,
        10**6,
    )(
        *got, *mates, entry, entryoff, init_state, obs_s, rows, dyn_t, pre, preoff, step, u,
        mask, near, reach, resid,
    )
    got = lax.all_to_all(send, TM, 0, 0, tiled=True)
    smoothed, prec, lik = call(
        k_smooth,
        "k_smooth",
        [VM] * 8,
        (out((SEQ, STEPS, N)), out((1, N)), out((1, N))),
        (),
        10**7,
        10**6,
    )(got, near_sums, suffix, final, rows, far, near, cross)
    return smoothed, prec.reshape(N), lik[0, :1]


def solution(mesh):
    split = Mesh(
        mesh.devices.reshape(mesh.shape["cluster"], 4, 4, 2), ("cluster", "tm_0", "tm_1", "tm_2")
    )
    return jax.shard_map(
        local,
        mesh=split,
        in_specs=(
            P("cluster", TM, None),
            P("cluster", TM),
            P("cluster"),
            P("cluster"),
            P("cluster", None),
            P("cluster"),
            P("cluster", None),
            P("cluster", None),
        ),
        out_specs=(P("cluster", TM, None), P("cluster"), P("cluster")),
        check_vma=False,
    )
```

time: 59.8 us -> 52.2 us (0.87)
  waiting for transfers between devices: 17.5 us -> 13.7 us
  local copies, waits for them, and re-layouts: 4.58 us -> 1.17 us
  Pallas kernels: 16.1 us -> 13.8 us
  starting transfers between devices: 9.13 us -> 11.2 us
    ppermute x7 -> x13, waiting for transfers between devices: 17.5 us -> 13.7 us  [shifted(): return lax.ppermute(a, axis, [(i, (i + by) % count) for i in range(count)])]
    unnamed x18 -> x14, local copies, waits for them, and re-layouts: 4.58 us -> 1.17 us
    pallas_call x7 -> x9, Pallas kernels: 16.1 us -> 13.8 us  [the longest x1 3.39 us: local(): call(k_block, 'k_block', [SM] * 2 + [VM] * 6, (out((SEQ, N + 8, N)), out(...]
    ppermute x7 -> x13, starting transfers between devices: 9.13 us -> 11.2 us  [shifted(): return lax.ppermute(a, axis, [(i, (i + by) % count) for i in range(count)])]
  transfers between devices with their start and end apart: 7 -> 13, of which waited for: 5 -> 13; matrix products, arithmetic and copies ran while one was open for 0% -> 0% of each run, Pallas kernels for 13% -> 9%
where the time goes in v1:
time: 52.2 us; the launch traced here: 52 us
  Pallas kernels  13.8 us (26%)
  waiting for transfers between devices  13.7 us (26%)
  starting transfers between devices  11.2 us (21%)
  blocking collectives  10.8 us (21%)
  between operations  1.39 us (3%)
  local copies, waits for them, and re-layouts  1.17 us (2%)
    ppermute x13, waiting for transfers between devices, shifted(): return lax.ppermute(a, axis, [(i, (i + by) % count) for i in range(count)])  13.7 us
    ppermute x13, starting transfers between devices, shifted(): return lax.ppermute(a, axis, [(i, (i + by) % count) for i in range(count)])  11.2 us
    all_to_all x1, blocking collectives, local(): got = lax.all_to_all(send, TM, 0, 0, tiled=True)  10.8 us
    pallas_call x1, Pallas kernels, local(): call(k_block, 'k_block', [SM] * 2 + [VM] * 6, (out((SEQ, N + 8, N)), out(...  3.39 us
    pallas_call x1, Pallas kernels, local(): call(k_filter, 'k_filter', [VM] * 20, (out((BLOCKS, 8, N)), out((SUB, ROW...  2.42 us
    pallas_call x1, Pallas kernels, local(): powers(a, d4)  1.99 us
    pallas_call x1, Pallas kernels, local(): prefix(a, present, table, nodes, offs)  1.64 us
    pallas_call x1, Pallas kernels, local(): call(k_smooth, 'k_smooth', [VM] * 8, (out((SEQ, STEPS, N)), out((1, N)),...  1.6 us
  transfers between devices with their start and end apart: 13, of which 13 were waited for; matrix products, arithmetic and copies ran while one was open for 0% of the time, Pallas kernels for 9%

profile of v1, /device:TPU:1, one launch (start us, length us, event | category | flops | bytes accessed | tf_op | source)
XLA Modules:
  0.0 52.0 jit_solution(1472586106071742443)
XLA Ops:
  1.3 0.8 %copy-done.2 = f32[128,128]{1,0:T(8,128)S(1)} copy-done((f32[128,128]{1,0:T(8,128)S(1)}, f32[128,128]{1,0:T(8,128)}, u32[]{:S(2)}) %copy-start.2) | copy-done | bytes 65560
  2.1 0.5 %k_first.1 = (f32[128,128]{1,0:T(8,128)S(1)}, bf16[4,128,256]{2,1,0:T(8,128)(2,1)S(1)}, f32[128,128]{1,0:T(8,128)S(1)}, bf16[128,256]{1,0:T(8,128)(2,1)S(1)}) custom-call(f32[128,128]{1,0:T(8,128)S(1)} %copy-done.2), custom_call_target="tpu_custom_call" | custom-call | flops 4000000000 | bytes 10000000 | tf_op jit(solution)/shard_map/k_first/pallas_call | solution.py:448
  2.7 0.3 copy-done.1
  3.0 3.4 %k_block.1 = (f32[3,136,128]{2,1,0:T(8,128)S(1)}, bf16[16,128,256]{2,1,0:T(8,128)(2,1)S(1)}, bf16[42,128,256]{2,1,0:T(8,128)(2,1)S(1)}, f32[96,128]{1,0:T(8,128)...) custom-call(s32[3,64]{1,0:T(4,128)S(1)} %copy-done.4, ...), custom_call_target="tpu_custom_call" | custom-call | flops 1000000000 | bytes 1000000 | tf_op jit(solution)/shard_map/k_block/pallas_call | solution.py:457
  6.4 3.3 %collective-permute-start = (f32[3,136,128]{2,1,0:T(8,128)S(1)}, f32[3,136,128]{2,1,0:T(8,128)S(1)}, u32[]{:S(2)}, u32[]{:S(2)}) collective-permute-start(f32[3,136,128]{2,1,0:T(8,128)S(1)} %get-tuple-element.49.own_ref), channel_id=1, source_target_pairs={{0,1},{1,0},{2,3},{3,2},{4,5},{5,4},{6,7},{7,6},{8,9},{9,8},{10,11... | collective-permute-start | bytes 626696 | tf_op jit(solution)/shard_map/ppermute | solution.py:434
  9.8 1.1 %collective-permute-done.mate_ref = f32[3,136,128]{2,1,0:T(8,128)S(1)} collective-permute-done((f32[3,136,128]{2,1,0:T(8,128)S(1)}, f32[3,136,128]{2,1,0:T(8,128)S(1)}, u32[]{:S(2)}, u32[]{:S(2)}) %collective-permute-start) | collective-permute-done | bytes 208928 | tf_op jit(solution)/shard_map/ppermute | solution.py:434
  11.1 1.1 %collective-permute-start.3 = (f32[3,72,128]{2,1,0:T(8,128)S(1)}, f32[3,72,128]{2,1,0:T(8,128)S(1)}, u32[]{:S(2)}, u32[]{:S(2)}) collective-permute-start(f32[3,72,128]{2,1,0:T(8,128)S(1)} %get-tuple-element.52.chip_ref), channel_id=1, source_target_pairs={{0,6},{2,0},{4,2},{6,4},{1,7},{3,1},{5,3},{7,5},{8,14},{10,8},{12,... | collective-permute-start | bytes 331784 | tf_op jit(solution)/shard_map/ppermute | solution.py:434
  12.2 0.3 collective-permute-start.2
  12.5 0.7 %collective-permute-start.1 = (f32[3,72,128]{2,1,0:T(8,128)S(1)}, f32[3,72,128]{2,1,0:T(8,128)S(1)}, u32[]{:S(2)}, u32[]{:S(2)}) collective-permute-start(f32[3,72,128]{2,1,0:T(8,128)S(1)} %get-tuple-element.52.chip_ref), channel_id=1, source_target_pairs={{0,2},{2,4},{4,6},{6,0},{1,3},{3,5},{5,7},{7,1},{8,10},{10,12},{12... | collective-permute-start | bytes 331784 | tf_op jit(solution)/shard_map/ppermute | solution.py:434
  13.2 1.6 %k_prefix.1 = (f32[48,128,128]{2,1,0:T(8,128)S(1)}, f32[48,128]{1,0:T(8,128)S(1)}) custom-call(f32[3,72,128]{2,1,0:T(8,128)S(1)} %get-tuple-element.52.chip_ref, s32[3,64]{1,0:T(4,128)S(1)} %copy-done.4, bf16[16,128,256]{2,1,0:T(8,128)(2,1)S(1)} %get-tuple-element.53.table, bf16[42,128,256]{2,1,0:T(8,128)(2,1)S(1)} %get-tuple-element.54.nodes, ...), custom_call_target="tpu_custom_call" | custom-call | flops 3000000000 | bytes 10000000 | tf_op jit(solution)/shard_map/k_prefix/pallas_call | solution.py:490
  14.9 0.6 %collective-permute-done.3.r3 = f32[3,72,128]{2,1,0:T(8,128)S(1)} collective-permute-done((f32[3,72,128]{2,1,0:T(8,128)S(1)}, f32[3,72,128]{2,1,0:T(8,128)S(1)}, u32[]{:S(2)}, u32[]{:S(2)}) %collective-permute-start.3) | collective-permute-done | bytes 110624 | tf_op jit(solution)/shard_map/ppermute | solution.py:434
  15.4 2.2 %collective-permute-done.2.r2 = f32[3,72,128]{2,1,0:T(8,128)S(1)} collective-permute-done((f32[3,72,128]{2,1,0:T(8,128)S(1)}, f32[3,72,128]{2,1,0:T(8,128)S(1)}, u32[]{:S(2)}, u32[]{:S(2)}) %collective-permute-start.2) | collective-permute-done | bytes 110624 | tf_op jit(solution)/shard_map/ppermute | solution.py:434
  17.6 3.4 %collective-permute-done.1.r1 = f32[3,72,128]{2,1,0:T(8,128)S(1)} collective-permute-done((f32[3,72,128]{2,1,0:T(8,128)S(1)}, f32[3,72,128]{2,1,0:T(8,128)S(1)}, u32[]{:S(2)}, u32[]{:S(2)}) %collective-permute-start.1) | collective-permute-done | bytes 110624 | tf_op jit(solution)/shard_map/ppermute | solution.py:434
  21.0 0.5 collective-permute-start.4
  21.5 0.5 collective-permute-start.6
  22.0 0.4 collective-permute-done.4.m1
  22.5 0.4 collective-permute-done.5.m2
  23.0 0.8 %k_total.1 = (f32[3,72,128]{2,1,0:T(8,128)S(1)}, f32[3,3,136,128]{3,2,1,0:T(8,128)S(1)}) custom-call(f32[3,72,128]{2,1,0:T(8,128)S(1)} %get-tuple-element.50.low_ref, f32[3,72,128]{2,1,0:T(8,128)S(1)} %get-tuple-element.51.high_ref, f32[3,72,128]{2,1,0:T(8,128)S(1)} %collective-permute-done.1.r1, f32[3,72,128]{2,1,0:T(8,128)S(1)} %collective-permute-done.2.r2, ...), custom_call_target="tpu_custom_call" | custom-call | flops 100000000 | bytes 1000000 | tf_op jit(solution)/shard_map/k_total/pallas_call | solution.py:492
  23.8 2.6 %collective-permute-start.9 = (f32[3,72,128]{2,1,0:T(8,128)S(1)}, f32[3,72,128]{2,1,0:T(8,128)S(1)}, u32[]{:S(2)}, u32[]{:S(2)}) collective-permute-start(f32[3,72,128]{2,1,0:T(8,128)S(1)} %get-tuple-element.61.after_ref), channel_id=1, source_target_pairs={{0,24},{8,0},{16,8},{24,16},{1,25},{9,1},{17,9},{25,17},{2,26},{10... | collective-permute-start | bytes 331784 | tf_op jit(solution)/shard_map/ppermute | solution.py:434
  26.4 0.5 collective-permute-start.8
  26.9 0.6 %collective-permute-start.7 = (f32[3,72,128]{2,1,0:T(8,128)S(1)}, f32[3,72,128]{2,1,0:T(8,128)S(1)}, u32[]{:S(2)}, u32[]{:S(2)}) collective-permute-start(f32[3,72,128]{2,1,0:T(8,128)S(1)} %get-tuple-element.61.after_ref), channel_id=1, source_target_pairs={{0,8},{8,16},{16,24},{24,0},{1,9},{9,17},{17,25},{25,1},{2,10},{10... | collective-permute-start | bytes 331784 | tf_op jit(solution)/shard_map/ppermute | solution.py:434
  27.5 2.0 %k_powers.1 = (f32[16,128,128]{2,1,0:T(8,128)S(1)}, bf16[4,128,256]{2,1,0:T(8,128)(2,1)S(1)}, bf16[11,128,256]{2,1,0:T(8,128)(2,1)S(1)}) custom-call(f32[3,72,128]{2,1,0:T(8,128)S(1)} %get-tuple-element.61.after_ref, f32[128,128]{1,0:T(8,128)S(1)} %get-tuple-element.62.d4_ref), custom_call_target="tpu_custom_call" | custom-call | flops 3000000000 | bytes 10000000 | tf_op jit(solution)/shard_map/k_powers/pallas_call | solution.py:514
  29.5 1.1 %k_entry.1 = (f32[3,128,128]{2,1,0:T(8,128)S(1)}, f32[8,128]{1,0:T(8,128)S(1)}) custom-call(f32[3,72,128]{2,1,0:T(8,128)S(1)} %get-tuple-element.61.after_ref, f32[3,3,136,128]{3,2,1,0:T(8,128)S(1)} %get-tuple-element.66.full_ref, f32[3,136,128]{2,1,0:T(8,128)S(1)} %collective-permute-done.mate_ref), custom_call_target="tpu_custom_call" | custom-call | flops 1000000000 | bytes 10000000 | tf_op jit(solution)/shard_map/k_entry/pallas_call | solution.py:514
  30.7 1.2 %collective-permute-done.8.r2 = f32[3,72,128]{2,1,0:T(8,128)S(1)} collective-permute-done((f32[3,72,128]{2,1,0:T(8,128)S(1)}, f32[3,72,128]{2,1,0:T(8,128)S(1)}, u32[]{:S(2)}, u32[]{:S(2)}) %collective-permute-start.8) | collective-permute-done | bytes 110624 | tf_op jit(solution)/shard_map/ppermute | solution.py:434
  31.9 3.3 %collective-permute-done.7.r1 = f32[3,72,128]{2,1,0:T(8,128)S(1)} collective-permute-done((f32[3,72,128]{2,1,0:T(8,128)S(1)}, f32[3,72,128]{2,1,0:T(8,128)S(1)}, u32[]{:S(2)}, u32[]{:S(2)}) %collective-permute-start.7) | collective-permute-done | bytes 110624 | tf_op jit(solution)/shard_map/ppermute | solution.py:434
  35.2 0.6 %collective-permute-start.10 = (f32[3,72,128]{2,1,0:T(8,128)S(1)}, f32[3,72,128]{2,1,0:T(8,128)S(1)}, u32[]{:S(2)}, u32[]{:S(2)}) collective-permute-start(f32[3,72,128]{2,1,0:T(8,128)S(1)} %collective-permute-done.7.r1), channel_id=1, source_target_pairs={{0,1},{1,0},{2,3},{3,2},{4,5},{5,4},{6,7},{7,6},{8,9},{9,8},{10,11... | collective-permute-start | bytes 331784 | tf_op jit(solution)/shard_map/ppermute | solution.py:434
  35.7 0.5 collective-permute-start.12
  36.2 0.4 collective-permute-done.10.m1
  36.7 0.4 collective-permute-done.11.m2
  37.2 2.4 %k_filter.1 = (f32[32,8,128]{2,1,0:T(8,128)S(1)}, f32[4,48,128]{2,1,0:T(8,128)S(1)}, f32[48,128]{1,0:T(8,128)S(1)}, f32[8,128]{1,0:T(8,128)S(1)}) custom-call(f32[3,72,128]{2,1,0:T(8,128)S(1)} %collective-permute-done.7.r1, f32[3,72,128]{2,1,0:T(8,128)S(1)} %collective-permute-done.8.r2, f32[3,72,128]{2,1,0:T(8,128)S(1)} %collective-permute-done.9.r3, ...), custom_call_target="tpu_custom_call" | custom-call | flops 10000000 | bytes 1000000 | tf_op jit(solution)/shard_map/k_filter/pallas_call | solution.py:516
  39.6 10.8 %all_to_all.5.got_ref = f32[32,8,128]{2,1,0:T(8,128)S(1)} all-to-all(f32[32,8,128]{2,1,0:T(8,128)S(1)} %get-tuple-element.84), channel_id=1, replica_groups=mesh['cluster'=8,'tm_0'=4,'tm_1'=4,'tm_2'=2] {'tm_0','tm_1','tm_2'}, dimensions={0} | all-to-all | bytes 262144 | tf_op jit(solution)/shard_map/all_to_all | solution.py:528
  50.4 1.6 %k_smooth.1 = (f32[3,64,128]{2,1,0:T(8,128)}, f32[1,128]{1,0:T(1,128)}, f32[1,128]{1,0:T(1,128)}) custom-call(f32[32,8,128]{2,1,0:T(8,128)S(1)} %all_to_all.5.got_ref, f32[4,48,128]{2,1,0:T(8,128)S(1)} %get-tuple-element.85.local_ref, f32[48,128]{1,0:T(8,128)S(1)} %get-tuple-element.86.suffix_ref, f32[8,128]{1,0:T(8,128)S(1)} %get-tuple-element.87.final_ref, ...), custom_call_target="tpu_custom_call" | custom-call | flops 10000000 | bytes 1000000 | tf_op jit(solution)/shard_map/k_smooth/pallas_call | solution.py:529
  (18 shorter events, 0.6 us)
Async XLA Ops:
  1.3 0.8 %copy-start.2 = (f32[128,128]{1,0:T(8,128)S(1)}, f32[128,128]{1,0:T(8,128)}, u32[]{:S(2)}) copy-start(f32[128,128]{1,0:T(8,128)} %dyn_ref.1) | copy-start | bytes 196612
  2.1 0.9 %copy-start.1 = (f32[3,64,128]{2,1,0:T(8,128)S(1)}, f32[3,64,128]{2,1,0:T(8,128)}, u32[]{:S(2)}) copy-start(f32[3,64,128]{2,1,0:T(8,128)} %obs_raw.1) | copy-start | bytes 294916
  2.1 0.9 %copy-start.3 = (f32[128,128]{1,0:T(8,128)S(1)}, f32[128,128]{1,0:T(8,128)}, u32[]{:S(2)}) copy-start(f32[128,128]{1,0:T(8,128)} %map_ref.1) | copy-start | bytes 196612
  2.1 0.9 %copy-start.4 = (s32[3,64]{1,0:T(4,128)S(1)}, s32[3,64]{1,0:T(4,128)}, u32[]{:S(2)}) copy-start(s32[3,64]{1,0:T(4,128)} %flags.3) | copy-start | bytes 2308
  2.1 0.9 %copy-start.5 = (f32[128]{0:T(128)S(1)}, f32[128]{0:T(128)}, u32[]{:S(2)}) copy-start(f32[128]{0:T(128)} %param.11) | copy-start | bytes 1540
  2.1 0.9 %copy-start.6 = (f32[128]{0:T(128)S(1)}, f32[128]{0:T(128)}, u32[]{:S(2)}) copy-start(f32[128]{0:T(128)} %param.13) | copy-start | bytes 1540
  6.4 4.4 %collective-permute-start = (f32[3,136,128]{2,1,0:T(8,128)S(1)}, f32[3,136,128]{2,1,0:T(8,128)S(1)}, u32[]{:S(2)}, u32[]{:S(2)}) collective-permute-start(f32[3,136,128]{2,1,0:T(8,128)S(1)} %get-tuple-element.49.own_ref), channel_id=1, source_target_pairs={{0,1},{1,0},{2,3},{3,2},{4,5},{5,4},{6,7},{7,6},{8,9},{9,8},{10,11... | collective-permute-start | bytes 626696 | tf_op jit(solution)/shard_map/ppermute | solution.py:434
  11.1 4.3 %collective-permute-start.3 = (f32[3,72,128]{2,1,0:T(8,128)S(1)}, f32[3,72,128]{2,1,0:T(8,128)S(1)}, u32[]{:S(2)}, u32[]{:S(2)}) collective-permute-start(f32[3,72,128]{2,1,0:T(8,128)S(1)} %get-tuple-element.52.chip_ref), channel_id=1, source_target_pairs={{0,6},{2,0},{4,2},{6,4},{1,7},{3,1},{5,3},{7,5},{8,14},{10,8},{12,... | collective-permute-start | bytes 331784 | tf_op jit(solution)/shard_map/ppermute | solution.py:434
  12.2 5.5 %collective-permute-start.2 = (f32[3,72,128]{2,1,0:T(8,128)S(1)}, f32[3,72,128]{2,1,0:T(8,128)S(1)}, u32[]{:S(2)}, u32[]{:S(2)}) collective-permute-start(f32[3,72,128]{2,1,0:T(8,128)S(1)} %get-tuple-element.52.chip_ref), channel_id=1, source_target_pairs={{0,4},{2,6},{4,0},{6,2},{1,5},{3,7},{5,1},{7,3},{8,12},{10,14},{12... | collective-permute-start | bytes 331784 | tf_op jit(solution)/shard_map/ppermute | solution.py:434
  12.5 8.5 %collective-permute-start.1 = (f32[3,72,128]{2,1,0:T(8,128)S(1)}, f32[3,72,128]{2,1,0:T(8,128)S(1)}, u32[]{:S(2)}, u32[]{:S(2)}) collective-permute-start(f32[3,72,128]{2,1,0:T(8,128)S(1)} %get-tuple-element.52.chip_ref), channel_id=1, source_target_pairs={{0,2},{2,4},{4,6},{6,0},{1,3},{3,5},{5,7},{7,1},{8,10},{10,12},{12... | collective-permute-start | bytes 331784 | tf_op jit(solution)/shard_map/ppermute | solution.py:434
  21.0 1.5 %collective-permute-start.4 = (f32[3,72,128]{2,1,0:T(8,128)S(1)}, f32[3,72,128]{2,1,0:T(8,128)S(1)}, u32[]{:S(2)}, u32[]{:S(2)}) collective-permute-start(f32[3,72,128]{2,1,0:T(8,128)S(1)} %collective-permute-done.1.r1), channel_id=1, source_target_pairs={{0,1},{1,0},{2,3},{3,2},{4,5},{5,4},{6,7},{7,6},{8,9},{9,8},{10,11... | collective-permute-start | bytes 331784 | tf_op jit(solution)/shard_map/ppermute | solution.py:434
  21.5 1.3 %collective-permute-start.5 = (f32[3,72,128]{2,1,0:T(8,128)S(1)}, f32[3,72,128]{2,1,0:T(8,128)S(1)}, u32[]{:S(2)}, u32[]{:S(2)}) collective-permute-start(f32[3,72,128]{2,1,0:T(8,128)S(1)} %collective-permute-done.2.r2), channel_id=1, source_target_pairs={{0,1},{1,0},{2,3},{3,2},{4,5},{5,4},{6,7},{7,6},{8,9},{9,8},{10,11... | collective-permute-start | bytes 331784 | tf_op jit(solution)/shard_map/ppermute | solution.py:434
  21.5 1.5 %collective-permute-start.6 = (f32[3,72,128]{2,1,0:T(8,128)S(1)}, f32[3,72,128]{2,1,0:T(8,128)S(1)}, u32[]{:S(2)}, u32[]{:S(2)}) collective-permute-start(f32[3,72,128]{2,1,0:T(8,128)S(1)} %collective-permute-done.3.r3), channel_id=1, source_target_pairs={{0,1},{1,0},{2,3},{3,2},{4,5},{5,4},{6,7},{7,6},{8,9},{9,8},{10,11... | collective-permute-start | bytes 331784 | tf_op jit(solution)/shard_map/ppermute | solution.py:434
  23.8 6.9 %collective-permute-start.9 = (f32[3,72,128]{2,1,0:T(8,128)S(1)}, f32[3,72,128]{2,1,0:T(8,128)S(1)}, u32[]{:S(2)}, u32[]{:S(2)}) collective-permute-start(f32[3,72,128]{2,1,0:T(8,128)S(1)} %get-tuple-element.61.after_ref), channel_id=1, source_target_pairs={{0,24},{8,0},{16,8},{24,16},{1,25},{9,1},{17,9},{25,17},{2,26},{10... | collective-permute-start | bytes 331784 | tf_op jit(solution)/shard_map/ppermute | solution.py:434
  26.4 5.5 %collective-permute-start.8 = (f32[3,72,128]{2,1,0:T(8,128)S(1)}, f32[3,72,128]{2,1,0:T(8,128)S(1)}, u32[]{:S(2)}, u32[]{:S(2)}) collective-permute-start(f32[3,72,128]{2,1,0:T(8,128)S(1)} %get-tuple-element.61.after_ref), channel_id=1, source_target_pairs={{0,16},{8,24},{16,0},{24,8},{1,17},{9,25},{17,1},{25,9},{2,18},{10... | collective-permute-start | bytes 331784 | tf_op jit(solution)/shard_map/ppermute | solution.py:434
  26.9 8.3 %collective-permute-start.7 = (f32[3,72,128]{2,1,0:T(8,128)S(1)}, f32[3,72,128]{2,1,0:T(8,128)S(1)}, u32[]{:S(2)}, u32[]{:S(2)}) collective-permute-start(f32[3,72,128]{2,1,0:T(8,128)S(1)} %get-tuple-element.61.after_ref), channel_id=1, source_target_pairs={{0,8},{8,16},{16,24},{24,0},{1,9},{9,17},{17,25},{25,1},{2,10},{10... | collective-permute-start | bytes 331784 | tf_op jit(solution)/shard_map/ppermute | solution.py:434
  29.5 7.7 %copy-start = (f32[3,128]{1,0:T(4,128)S(1)}, f32[3,128]{1,0:T(4,128)}, u32[]{:S(2)}) copy-start(f32[3,128]{1,0:T(4,128)} %init_ref.1) | copy-start | bytes 4612
  35.2 1.5 %collective-permute-start.10 = (f32[3,72,128]{2,1,0:T(8,128)S(1)}, f32[3,72,128]{2,1,0:T(8,128)S(1)}, u32[]{:S(2)}, u32[]{:S(2)}) collective-permute-start(f32[3,72,128]{2,1,0:T(8,128)S(1)} %collective-permute-done.7.r1), channel_id=1, source_target_pairs={{0,1},{1,0},{2,3},{3,2},{4,5},{5,4},{6,7},{7,6},{8,9},{9,8},{10,11... | collective-permute-start | bytes 331784 | tf_op jit(solution)/shard_map/ppermute | solution.py:434
  35.7 1.3 %collective-permute-start.11 = (f32[3,72,128]{2,1,0:T(8,128)S(1)}, f32[3,72,128]{2,1,0:T(8,128)S(1)}, u32[]{:S(2)}, u32[]{:S(2)}) collective-permute-start(f32[3,72,128]{2,1,0:T(8,128)S(1)} %collective-permute-done.8.r2), channel_id=1, source_target_pairs={{0,1},{1,0},{2,3},{3,2},{4,5},{5,4},{6,7},{7,6},{8,9},{9,8},{10,11... | collective-permute-start | bytes 331784 | tf_op jit(solution)/shard_map/ppermute | solution.py:434
  35.7 1.5 %collective-permute-start.12 = (f32[3,72,128]{2,1,0:T(8,128)S(1)}, f32[3,72,128]{2,1,0:T(8,128)S(1)}, u32[]{:S(2)}, u32[]{:S(2)}) collective-permute-start(f32[3,72,128]{2,1,0:T(8,128)S(1)} %collective-permute-done.9.r3), channel_id=1, source_target_pairs={{0,1},{1,0},{2,3},{3,2},{4,5},{5,4},{6,7},{7,6},{8,9},{9,8},{10,11... | collective-permute-start | bytes 331784 | tf_op jit(solution)/shard_map/ppermute | solution.py:434

commit v2 on v1

--- a/solution.py
+++ b/solution.py
@@ -102,38 +102,32 @@
     return got[:N], got[N : N + 1] + right_off
 
 
+REACH = (1, 2, 3, 4, 8, 12)
 LEVELS = ((0, 24), (24, 12), (36, 6))
 OFFS = (0, 48, 72, 84)
-PART = HALF + 8
-
-
-def k_first(dyn_ref, dynt_ref, near_ref, d4_ref, resid_ref):
-    dyn = dyn_ref[...]
-    dyn_t = jnp.transpose(dyn)
-    dynt_ref[...] = dyn_t
-    resid_ref[...] = pair(identity() - mul_exact(dyn_t, dyn))
-    d2 = mul_exact(dyn, dyn)
-    d34 = mul_exact(d2, lanes(dyn, d2))
-    d4_ref[...] = d34[:, N:]
-    for i, a in enumerate((dyn, d2, d34[:, :N], d34[:, N:])):
-        near_ref[i] = pair(a)
+PART = SEQ * HALF + 8
+
+
+def k_first(eye_ref):
+    eye_ref[...] = identity()
 
 
 def k_block(
-    flags, sensors_ref, obs_raw, pres_ref, lp_ref, dynt_ref, pv_ref, map_ref,
-    root_ref, table, nodes, offs, step_ref, u_ref, mask_ref, obs_ref, rows_ref, mask_scr, u_scr,
+    flags, sensors_ref, eye_ref, obs_raw, pres_ref, lp_ref, dyn_ref, pv_ref, map_ref,
+    root_ref, dynt_ref, table, nodes, offs, step_ref, u_ref, mask_ref, obs_ref, rows_ref, mask_scr, u_scr,
 ):
     on = on_row(sensors_ref)
     weight = jnp.exp(lp_ref[...]) * on
     pv, obs_map = pv_ref[...], map_ref[...]
-    dyn_t = dynt_ref[...]
-    out_t = mul_exact(dyn_t, jnp.transpose(obs_map))
-    filt_t = dyn_t - mul_exact(out_t * weight, obs_map) * pv
+    dyn_t = jnp.transpose(dyn_ref[...])
+    dynt_ref[...] = dyn_t
+    y = pair(obs_map)
+    out_t = mul_pair(pair(dyn_t), pair(jnp.transpose(obs_map)))
+    filt_t = dyn_t - mul_pair(pair(out_t * weight), y) * pv
     rows_ref[...] = stacked(on, weight, lp_ref[...], jnp.zeros((5, N), F32))
     step_ref[...] = pair(lanes(dyn_t, filt_t, out_t))
     seen = pres_ref[...].astype(F32)
     seen = jnp.transpose(stacked(seen, jnp.zeros((8 - SEQ, STEPS), F32)))
-    y = pair(obs_map)
     for b in range(SEQ):
         mask = jnp.broadcast_to(seen[:, b : b + 1], (STEPS, N))
         mask_scr[b] = mask
@@ -178,22 +172,27 @@
             get = lambda k, level=level: nodes[LEVELS[level][0] + k]
 
 
-def put_halves(refs, b, matrix, off):
-    off = jnp.broadcast_to(off, (8, N))
-    for c, ref in enumerate(refs):
-        ref[b, 0:HALF, :] = matrix[c * HALF : (c + 1) * HALF]
-        ref[b, HALF:PART, :] = off
+def put_offsets(ref, offs):
+    ref[SEQ * HALF : PART, :] = stacked(*offs, jnp.zeros((8 - SEQ, N), F32))
+
+
+def half_of(ref, b):
+    return ref[b * HALF : (b + 1) * HALF, :]
+
+
+def offset_of(ref, b):
+    return ref[SEQ * HALF + b : SEQ * HALF + b + 1, :]
 
 
 def from_halves(low_ref, high_ref, b):
-    return stacked(low_ref[b, 0:HALF, :], high_ref[b, 0:HALF, :]), low_ref[b, HALF : HALF + 1, :]
+    return stacked(half_of(low_ref, b), half_of(high_ref, b)), offset_of(low_ref, b)
 
 
 def in_order(mine_ref, mate_ref, b):
     first = lax.axis_index("tm_2") == 0
-    mine, mate = mine_ref[b, 0:HALF, :], mate_ref[b, 0:HALF, :]
+    mine, mate = half_of(mine_ref, b), half_of(mate_ref, b)
     matrix = stacked(pick(first, mine, mate), pick(first, mate, mine))
-    return matrix, mine_ref[b, HALF : HALF + 1, :]
+    return matrix, offset_of(mine_ref, b)
 
 
 def then(p, q):
@@ -202,22 +201,24 @@
 
 def then_half(p, q, ref, b):
     left = pick(lax.axis_index("tm_2") == 0, p[0][:HALF], p[0][HALF:])
-    got = mul_pair(
-        stacked(pair(left), pair(jnp.broadcast_to(p[1], (16, N)))), pair(q[0])
-    )
-    ref[b, 0:HALF, :] = got[:HALF]
-    ref[b, HALF:PART, :] = got[HALF:PART] + q[1]
+    got = mul_pair(stacked(pair(left), pair(jnp.broadcast_to(p[1], (16, N)))), pair(q[0]))
+    ref[b * HALF : (b + 1) * HALF, :] = got[:HALF]
+    return got[HALF : HALF + 1] + q[1]
 
 
 def k_core(own_ref, mate_ref, mine_ref, low_ref, high_ref):
     first = lax.axis_index("tm_2") == 0
+    offs = []
     for b in range(SEQ):
         own, mate = own_ref[b], mate_ref[b]
         p, q = pick(first, own, mate), pick(first, mate, own)
         matrix, off = then((p[:N], p[N : N + 1]), (q[:N], q[N : N + 1]))
-        put_halves((low_ref, high_ref), b, matrix, off)
-        mine_ref[b, 0:HALF, :] = pick(first, matrix[:HALF], matrix[HALF:])
-        mine_ref[b, HALF:PART, :] = jnp.broadcast_to(off, (8, N))
+        low, high = matrix[:HALF], matrix[HALF:]
+        for ref, half in ((low_ref, low), (high_ref, high), (mine_ref, pick(first, low, high))):
+            ref[b * HALF : (b + 1) * HALF, :] = half
+        offs.append(off)
+    for ref in (low_ref, high_ref, mine_ref):
+        put_offsets(ref, offs)
 
 
 def k_total(low_ref, high_ref, r1, r2, r3, m1, m2, m3, out_ref, full_ref, maps, offs):
@@ -233,9 +234,11 @@
         matrix, off = from_halves(low_ref, high_ref, b)
         maps[me, b] = matrix
         offs[me, b] = jnp.broadcast_to(off, (8, N))
+    ends = []
     for b in range(SEQ):
         p = [(maps[k, b], offs[k, b, 0:1, :]) for k in range(4)]
-        then_half(then(p[0], p[1]), then(p[2], p[3]), out_ref, b)
+        ends.append(then_half(then(p[0], p[1]), then(p[2], p[3]), out_ref, b))
+    put_offsets(out_ref, ends)
 
 
 def k_prefix(chip_ref, flags, table, nodes, offs, pre_ref, preoff_ref):
@@ -264,17 +267,29 @@
                 preoff_ref[to : to + 1, :] = off
 
 
-def k_powers(after_ref, d4_ref, far_ref, reach_ref, cross_ref):
-    eye = identity()
+def k_powers(
+    after_ref, eye_ref, dyn_ref, dynt_ref, near_ref, far_ref, reach_ref, cross_ref, resid_ref
+):
+    eye, dyn = eye_ref[...], dyn_ref[...]
+    d2 = mul_exact(dyn, dyn)
+    d34 = mul_exact(d2, lanes(dyn, d2))
+    d3, d4 = d34[:, :N], d34[:, N:]
+    for i, a in enumerate((dyn, d2, d3, d4)):
+        near_ref[i] = pair(a)
+    resid = eye - mul_exact(dynt_ref[...], dyn)
+    resid_ref[0] = pair(resid)
+    more = mul_exact(resid, lanes(dyn, d2, d3))
+    for i in range(3):
+        resid_ref[i + 1] = pair(more[:, i * N : (i + 1) * N])
     far_ref[0] = eye
-    far_ref[1] = d4_ref[...]
+    far_ref[1] = d4
     for have in (1, 2, 4, 8):
         last = far_ref[have]
         for k in range(1, have + 1):
             got = mul_exact(last, far_ref[k])
             if have + k < LEAVES:
                 far_ref[have + k] = got
-    for i, k in enumerate((1, 2, 4, 8)):
+    for i, k in enumerate(REACH):
         reach_ref[i] = pair(far_ref[k])
     cross_ref[0] = pair(eye)
     powers = [None, got]
@@ -305,8 +320,8 @@
 
 def k_filter(
     r1, r2, r3, m1, m2, m3, entry_ref, entryoff_ref, init_ref, obs_ref,
-    rows_ref, dynt_ref, pre_ref, preoff_ref, step_ref, u_ref, mask_ref, near_ref, reach_ref,
-    resid_ref, send_ref, local_ref, suffix_ref, final_ref,
+    rows_ref, dynt_ref, pre_ref, preoff_ref, step_ref, u_ref, mask_ref, reach_ref,
+    resid_ref, cross_ref, send_ref, local_ref, suffix_ref, final_ref,
 ):
     group = lax.axis_index("tm_0")
     last = (group == 3) & (lax.axis_index("tm_1") == 3) & (lax.axis_index("tm_2") == 1)
@@ -329,10 +344,9 @@
     state = stacked(*rows)
     weight = rows_ref[1:2, :]
     step = step_ref[...]
-    resid = resid_ref[...]
     square = jnp.zeros((ROWS, N), F32)
     seen = jnp.zeros((ROWS, N), F32)
-    residuals = []
+    sums = [None] * SUB
     for i in range(SUB):
         d = mul_pair(pair(state), step)
         mask = mask_ref[i]
@@ -340,29 +354,30 @@
         square = square + mask * (error * error)
         seen = seen + mask
         state = pick(mask > 0.5, d[:, N : 2 * N], d[:, :N]) + u_ref[i]
-        residuals.append(mul_pair(pair(state), resid))
+        x = pair(state)
+        for k in range(i + 1):
+            add = mul_pair(x, resid_ref[i - k])
+            sums[k] = add if k == i else sums[k] + add
     square = jnp.sum(square, axis=0, keepdims=True) * weight
     seen = jnp.sum(seen, axis=0, keepdims=True)
     ends = stacked(*(state[(b + 1) * LEAVES - 1 : (b + 1) * LEAVES, :] for b in range(SEQ)))
     ends = stacked(ends, jnp.zeros((8 - SEQ, N), F32))
     final = mul_pair(pair(ends), pair(dynt_ref[...]))
     final_ref[...] = final
-    y = near_ref[0]
-    run = residuals[SUB - 1]
-    local_ref[SUB - 1] = run
-    for i in reversed(range(SUB - 1)):
-        run = mul_pair(pair(run), y) + residuals[i]
-        local_ref[i] = run
     place = lax.broadcasted_iota(jnp.int32, (ROWS, N), 0) % LEAVES
-    for k, reach in enumerate((1, 2, 4, 8)):
-        moved = mul_pair(pair(run), reach_ref[k])
-        moved = pltpu.roll(moved, ROWS - reach, 0)
-        run = run + pick(place < LEAVES - reach, moved, 0.0)
+    run = sums[0]
+    for first in (0, 3):
+        total = run
+        for k in range(first, first + 3):
+            moved = pltpu.roll(mul_pair(pair(run), reach_ref[k]), ROWS - REACH[k], 0)
+            total = total + pick(place < LEAVES - REACH[k], moved, 0.0)
+        run = total
+    for i in range(SUB):
+        local_ref[i] = sums[i]
     suffix_ref[...] = run
     offsets = stacked(*(run[b * LEAVES : b * LEAVES + 1, :] for b in range(SEQ)))
     offsets = stacked(offsets, jnp.zeros((8 - SEQ, N), F32))
-    half = mul_pair(pair(final), reach_ref[3])
-    through = mul_pair(pair(half), reach_ref[3])
+    through = mul_pair(pair(final), cross_ref[1])
     offsets = offsets + pick(last, through, 0.0)
     packed = stacked(offsets[:SEQ], square, seen, jnp.zeros((8 - SEQ - 2, N), F32))
     send_ref[...] = jnp.broadcast_to(packed[None], (BLOCKS, 8, N))
@@ -400,8 +415,8 @@
         got = mul_pair(x, near_ref[SUB - 1 - i]) + local_ref[i]
         for b in range(SEQ):
             out_ref[b, pl.ds(i, LEAVES, stride=SUB), :] = got[b * LEAVES : (b + 1) * LEAVES]
-    sums = jnp.sum(got_ref[...], axis=0)
-    square, seen = sums[SEQ : SEQ + 1], sums[SEQ + 1 : SEQ + 2]
+    both = jnp.sum(got_ref[...], axis=0)
+    square, seen = both[SEQ : SEQ + 1], both[SEQ + 1 : SEQ + 2]
     total = float(SEQ * STEPS * BLOCKS)
     prec_ref[...] = lp + (0.5 / total) * on * (seen - square)
     lik = jnp.sum(on * (seen * lp - square), axis=1, keepdims=True) * (0.5 / (total * N))
@@ -437,29 +452,23 @@
 def exchanged(mine, axis, work):
     got = [shifted(mine, axis, d) for d in (1, 2, 3)]
     done = work(mine)
-    tied, done = lax.optimization_barrier((got, done))
-    return got, [shifted(a, "tm_2", 1) for a in tied], done
+    swaps = [shifted(lax.optimization_barrier((a, done[-1]))[0], "tm_2", 1) for a in got]
+    return got, swaps, done
 
 
 def local(obs, present, sensors, log_prec, dynamics, prior_var, obs_map, init_state):
     lp, pv = log_prec.reshape(1, N), prior_var.reshape(1, N)
-    part = out((SEQ, PART, N))
+    part = out((PART, N))
     square = out((N, N))
-    dyn_t, near, d4, resid = call(
-        k_first,
-        "k_first",
-        [VM],
-        (square, out((4, N, 2 * N), BF16), square, out((N, 2 * N), BF16)),
-        (),
-        4 * 10**9,
-        10**7,
-    )(dynamics)
-    root, table, nodes, offs, step, u, mask, obs_s, rows = call(
+    square = out((N, N))
+    eye = call(k_first, "k_first", [], square, (), 4 * 10**9, 10**7)()
+    root, dyn_t, table, nodes, offs, step, u, mask, obs_s, rows = call(
         k_block,
         "k_block",
-        [SM] * 2 + [VM] * 6,
+        [SM] * 2 + [VM] * 7,
         (
             out((SEQ, N + 8, N)),
+            square,
             out((16, N, 2 * N), BF16),
             out((42, N, 2 * N), BF16),
             out((96, N)),
@@ -472,7 +481,7 @@
         [pltpu.VMEM((SEQ, STEPS, N), F32), pltpu.VMEM((SEQ, STEPS, N), F32)],
         10**9,
         10**6,
-    )(present, sensors, obs, present, lp, dyn_t, pv, obs_map)
+    )(present, sensors, eye, obs, present, lp, dynamics, pv, obs_map)
     mate = shifted(root, "tm_2", 1)
     chip, low, high = call(k_core, "k_core", [VM] * 2, (part, part, part), (), 10**7, 10**6)(
         root, mate
@@ -501,8 +510,14 @@
     powers = call(
         k_powers,
         "k_powers",
-        [VM] * 2,
-        (out((LEAVES, N, N)), out((4, N, 2 * N), BF16), out((11, N, 2 * N), BF16)),
+        [VM] * 4,
+        (
+            out((SUB, N, 2 * N), BF16),
+            out((LEAVES, N, N)),
+            out((len(REACH), N, 2 * N), BF16),
+            out((11, N, 2 * N), BF16),
+            out((SUB, N, 2 * N), BF16),
+        ),
         (),
         3 * 10**9,
         10**7,
@@ -510,9 +525,12 @@
     entries = call(
         k_entry, "k_entry", [VM] * 3, (out((SEQ, N, N)), out((8, N))), (), 10**9, 10**7
     )
-    got, mates, ((far, reach, cross), (entry, entryoff)) = exchanged(
-        group, "tm_0", lambda a: (powers(a, d4), entries(a, full, mate))
-    )
+
+    def work(a):
+        tables = powers(a, eye, dynamics, dyn_t)
+        return (*tables, *entries(tables[-1], full, mate))
+
+    got, mates, (near, far, reach, cross, resid, entry, entryoff) = exchanged(group, "tm_0", work)
     send, near_sums, suffix, final = call(
         k_filter,
         "k_filter",
@@ -523,7 +541,7 @@
         10**6,
     )(
         *got, *mates, entry, entryoff, init_state, obs_s, rows, dyn_t, pre, preoff, step, u,
-        mask, near, reach, resid,
+        mask, reach, resid, cross,
     )
     got = lax.all_to_all(send, TM, 0, 0, tiled=True)
     smoothed, prec, lik = call(

time: 52.2 us -> 49.1 us (0.941)
  waiting for transfers between devices: 13.7 us -> 7.5 us
  starting transfers between devices: 11.2 us -> 15.6 us
  local copies, waits for them, and re-layouts: 1.17 us -> 0.23 us
  Pallas kernels: 13.8 us -> 13.2 us
    ppermute x13, waiting for transfers between devices: 13.7 us -> 7.5 us  [shifted(): return lax.ppermute(a, axis, [(i, (i + by) % count) for i in range(count)])]
    ppermute x13, starting transfers between devices: 11.2 us -> 15.6 us  [shifted(): return lax.ppermute(a, axis, [(i, (i + by) % count) for i in range(count)])]
    unnamed x14, local copies, waits for them, and re-layouts: 1.17 us -> 0.23 us
  transfers between devices with their start and end apart: 13 -> 13, of which waited for: 13 -> 9; matrix products, arithmetic and copies ran while one was open for 0% -> 0% of each run, Pallas kernels for 9% -> 11%
where the time goes in v2:
time: 49.1 us; the launch traced here: 48.9 us
  starting transfers between devices  15.6 us (32%)
  Pallas kernels  13.2 us (27%)
  blocking collectives  10.8 us (22%)
  waiting for transfers between devices  7.5 us (15%)
  between operations  1.5 us (3%)
    ppermute x13, starting transfers between devices, shifted(): return lax.ppermute(a, axis, [(i, (i + by) % count) for i in range(count)])  15.6 us
    all_to_all x1, blocking collectives, local(): got = lax.all_to_all(send, TM, 0, 0, tiled=True)  10.8 us
    ppermute x13, waiting for transfers between devices, shifted(): return lax.ppermute(a, axis, [(i, (i + by) % count) for i in range(count)])  7.5 us
    pallas_call x1, Pallas kernels, local(): call(k_block, 'k_block', [SM] * 2 + [VM] * 7, (out((SEQ, N + 8, N)), squa...  3.31 us
    pallas_call x1, Pallas kernels, work(): tables = powers(a, eye, dynamics, dyn_t)  2.48 us
    pallas_call x1, Pallas kernels, local(): call(k_filter, 'k_filter', [VM] * 20, (out((BLOCKS, 8, N)), out((SUB, ROW...  1.98 us
    pallas_call x1, Pallas kernels, local(): prefix(a, present, table, nodes, offs)  1.65 us
    pallas_call x1, Pallas kernels, local(): call(k_smooth, 'k_smooth', [VM] * 8, (out((SEQ, STEPS, N)), out((1, N)),...  1.6 us
  transfers between devices with their start and end apart: 13, of which 9 were waited for; matrix products, arithmetic and copies ran while one was open for 0% of the time, Pallas kernels for 11%

profile of v2, /device:TPU:1, one launch (start us, length us, event | category | flops | bytes accessed | tf_op | source)
XLA Modules:
  0.0 48.9 jit_solution(13191682947610595455)
XLA Ops:
  1.5 0.0 copy-done.2
  1.5 0.1 copy-done.1
  1.7 3.3 %k_block.1 = (f32[3,136,128]{2,1,0:T(8,128)S(1)}, f32[128,128]{1,0:T(8,128)S(1)}, bf16[16,128,256]{2,1,0:T(8,128)(2,1)S(1)}, bf16[42,128,256]{2,1,0:T(8,128)(2,1...) custom-call(s32[3,64]{1,0:T(4,128)S(1)} %copy-done.4, ...), custom_call_target="tpu_custom_call" | custom-call | flops 1000000000 | bytes 1000000 | tf_op jit(solution)/shard_map/k_block/pallas_call | solution.py:465
  5.0 3.3 %collective-permute-start = (f32[3,136,128]{2,1,0:T(8,128)S(1)}, f32[3,136,128]{2,1,0:T(8,128)S(1)}, u32[]{:S(2)}, u32[]{:S(2)}) collective-permute-start(f32[3,136,128]{2,1,0:T(8,128)S(1)} %get-tuple-element.40.own_ref), channel_id=1, source_target_pairs={{0,1},{1,0},{2,3},{3,2},{4,5},{5,4},{6,7},{7,6},{8,9},{9,8},{10,11... | collective-permute-start | bytes 626696 | tf_op jit(solution)/shard_map/ppermute | solution.py:449
  8.3 1.1 %collective-permute-done.mate_ref = f32[3,136,128]{2,1,0:T(8,128)S(1)} collective-permute-done((f32[3,136,128]{2,1,0:T(8,128)S(1)}, f32[3,136,128]{2,1,0:T(8,128)S(1)}, u32[]{:S(2)}, u32[]{:S(2)}) %collective-permute-start) | collective-permute-done | bytes 208928 | tf_op jit(solution)/shard_map/ppermute | solution.py:449
  9.4 0.2 k_core.1
  9.6 1.1 %collective-permute-start.3 = (f32[200,128]{1,0:T(8,128)S(1)}, f32[200,128]{1,0:T(8,128)S(1)}, u32[]{:S(2)}, u32[]{:S(2)}) collective-permute-start(f32[200,128]{1,0:T(8,128)S(1)} %get-tuple-element.43.chip_ref), channel_id=1, source_target_pairs={{0,6},{2,0},{4,2},{6,4},{1,7},{3,1},{5,3},{7,5},{8,14},{10,8},{12,... | collective-permute-start | bytes 307208 | tf_op jit(solution)/shard_map/ppermute | solution.py:449
  10.7 0.4 collective-permute-start.2
  11.1 0.7 %collective-permute-start.1 = (f32[200,128]{1,0:T(8,128)S(1)}, f32[200,128]{1,0:T(8,128)S(1)}, u32[]{:S(2)}, u32[]{:S(2)}) collective-permute-start(f32[200,128]{1,0:T(8,128)S(1)} %get-tuple-element.43.chip_ref), channel_id=1, source_target_pairs={{0,2},{2,4},{4,6},{6,0},{1,3},{3,5},{5,7},{7,1},{8,10},{10,12},{12... | collective-permute-start | bytes 307208 | tf_op jit(solution)/shard_map/ppermute | solution.py:449
  11.8 1.6 %k_prefix.1 = (f32[48,128,128]{2,1,0:T(8,128)S(1)}, f32[48,128]{1,0:T(8,128)S(1)}) custom-call(f32[200,128]{1,0:T(8,128)S(1)} %get-tuple-element.43.chip_ref, s32[3,64]{1,0:T(4,128)S(1)} %copy-done.4, bf16[16,128,256]{2,1,0:T(8,128)(2,1)S(1)} %get-tuple-element.44.table, bf16[42,128,256]{2,1,0:T(8,128)(2,1)S(1)} %get-tuple-element.45.nodes, ...), custom_call_target="tpu_custom_call" | custom-call | flops 3000000000 | bytes 10000000 | tf_op jit(solution)/shard_map/k_prefix/pallas_call | solution.py:499
  13.4 0.4 collective-permute-done.3.r3
  13.8 2.0 %collective-permute-start.6 = (f32[200,128]{1,0:T(8,128)S(1)}, f32[200,128]{1,0:T(8,128)S(1)}, u32[]{:S(2)}, u32[]{:S(2)}) collective-permute-start(f32[200,128]{1,0:T(8,128)S(1)} %collective-permute-done.3.r3), channel_id=1, source_target_pairs={{0,1},{1,0},{2,3},{3,2},{4,5},{5,4},{6,7},{7,6},{8,9},{9,8},{10,11... | collective-permute-start | bytes 307208 | tf_op jit(solution)/shard_map/ppermute | solution.py:449
  15.8 2.8 %collective-permute-start.5 = (f32[200,128]{1,0:T(8,128)S(1)}, f32[200,128]{1,0:T(8,128)S(1)}, u32[]{:S(2)}, u32[]{:S(2)}) collective-permute-start(f32[200,128]{1,0:T(8,128)S(1)} %collective-permute-done.2.r2), channel_id=1, source_target_pairs={{0,1},{1,0},{2,3},{3,2},{4,5},{5,4},{6,7},{7,6},{8,9},{9,8},{10,11... | collective-permute-start | bytes 307208 | tf_op jit(solution)/shard_map/ppermute | solution.py:449
  18.6 0.5 %collective-permute-done.1.r1 = f32[200,128]{1,0:T(8,128)S(1)} collective-permute-done((f32[200,128]{1,0:T(8,128)S(1)}, f32[200,128]{1,0:T(8,128)S(1)}, u32[]{:S(2)}, u32[]{:S(2)}) %collective-permute-start.1) | collective-permute-done | bytes 102432 | tf_op jit(solution)/shard_map/ppermute | solution.py:449
  19.1 0.6 %collective-permute-start.4 = (f32[200,128]{1,0:T(8,128)S(1)}, f32[200,128]{1,0:T(8,128)S(1)}, u32[]{:S(2)}, u32[]{:S(2)}) collective-permute-start(f32[200,128]{1,0:T(8,128)S(1)} %collective-permute-done.1.r1), channel_id=1, source_target_pairs={{0,1},{1,0},{2,3},{3,2},{4,5},{5,4},{6,7},{7,6},{8,9},{9,8},{10,11... | collective-permute-start | bytes 307208 | tf_op jit(solution)/shard_map/ppermute | solution.py:449
  19.7 0.9 %collective-permute-done.4.m1 = f32[200,128]{1,0:T(8,128)S(1)} collective-permute-done((f32[200,128]{1,0:T(8,128)S(1)}, f32[200,128]{1,0:T(8,128)S(1)}, u32[]{:S(2)}, u32[]{:S(2)}) %collective-permute-start.4) | collective-permute-done | bytes 102432 | tf_op jit(solution)/shard_map/ppermute | solution.py:449
  20.7 0.8 %k_total.1 = (f32[200,128]{1,0:T(8,128)S(1)}, f32[3,3,136,128]{3,2,1,0:T(8,128)S(1)}) custom-call(f32[200,128]{1,0:T(8,128)S(1)} %get-tuple-element.41.low_ref, f32[200,128]{1,0:T(8,128)S(1)} %get-tuple-element.42.high_ref, f32[200,128]{1,0:T(8,128)S(1)} %collective-permute-done.1.r1, f32[200,128]{1,0:T(8,128)S(1)} %collective-permute-done.2.r2, ...), custom_call_target="tpu_custom_call" | custom-call | flops 100000000 | bytes 1000000 | tf_op jit(solution)/shard_map/k_total/pallas_call | solution.py:501
  21.5 2.6 %collective-permute-start.9 = (f32[200,128]{1,0:T(8,128)S(1)}, f32[200,128]{1,0:T(8,128)S(1)}, u32[]{:S(2)}, u32[]{:S(2)}) collective-permute-start(f32[200,128]{1,0:T(8,128)S(1)} %get-tuple-element.51.after_ref), channel_id=1, source_target_pairs={{0,24},{8,0},{16,8},{24,16},{1,25},{9,1},{17,9},{25,17},{2,26},{10... | collective-permute-start | bytes 307208 | tf_op jit(solution)/shard_map/ppermute | solution.py:449
  24.0 0.5 %collective-permute-start.8 = (f32[200,128]{1,0:T(8,128)S(1)}, f32[200,128]{1,0:T(8,128)S(1)}, u32[]{:S(2)}, u32[]{:S(2)}) collective-permute-start(f32[200,128]{1,0:T(8,128)S(1)} %get-tuple-element.51.after_ref), channel_id=1, source_target_pairs={{0,16},{8,24},{16,0},{24,8},{1,17},{9,25},{17,1},{25,9},{2,18},{10... | collective-permute-start | bytes 307208 | tf_op jit(solution)/shard_map/ppermute | solution.py:449
  24.5 0.6 %collective-permute-start.7 = (f32[200,128]{1,0:T(8,128)S(1)}, f32[200,128]{1,0:T(8,128)S(1)}, u32[]{:S(2)}, u32[]{:S(2)}) collective-permute-start(f32[200,128]{1,0:T(8,128)S(1)} %get-tuple-element.51.after_ref), channel_id=1, source_target_pairs={{0,8},{8,16},{16,24},{24,0},{1,9},{9,17},{17,25},{25,1},{2,10},{10... | collective-permute-start | bytes 307208 | tf_op jit(solution)/shard_map/ppermute | solution.py:449
  25.1 2.5 %k_powers.1 = (bf16[4,128,256]{2,1,0:T(8,128)(2,1)S(1)}, f32[16,128,128]{2,1,0:T(8,128)S(1)}, bf16[6,128,256]{2,1,0:T(8,128)(2,1)S(1)}, bf16[11,128,256]{2,1,0:T(8,128)(2,1)S(1)}, bf16[4,128,256]{2,1,0:T(8,128)(2,1)S(1)}) custom-call(f32[200,128]{1,0:T(8,128)S(1)} %get-tuple-element.51.after_ref, f32[128,128]{1,0:T(8,128)S(1)} %k_first.1.eye_ref, ...), custom_call_target="tpu_custom_call" | custom-call | flops 3000000000 | bytes 10000000 | tf_op jit(solution)/shard_map/k_powers/pallas_call | solution.py:530
  27.6 1.1 %k_entry.1 = (f32[3,128,128]{2,1,0:T(8,128)S(1)}, f32[8,128]{1,0:T(8,128)S(1)}) custom-call(bf16[4,128,256]{2,1,0:T(8,128)(2,1)S(1)} %get-tuple-element.53.after_ref.resid_ref, f32[3,3,136,128]{3,2,1,0:T(8,128)S(1)} %get-tuple-element.54.full_ref, f32[3,136,128]{2,1,0:T(8,128)S(1)} %collective-permute-done.mate_ref), custom_call_target="tpu_custom_call" | custom-call | flops 1000000000 | bytes 10000000 | tf_op jit(solution)/shard_map/k_entry/pallas_call | solution.py:531
  28.8 0.4 collective-permute-done.8.r2
  29.2 3.2 %collective-permute-done.7.r1 = f32[200,128]{1,0:T(8,128)S(1)} collective-permute-done((f32[200,128]{1,0:T(8,128)S(1)}, f32[200,128]{1,0:T(8,128)S(1)}, u32[]{:S(2)}, u32[]{:S(2)}) %collective-permute-start.7) | collective-permute-done | bytes 102432 | tf_op jit(solution)/shard_map/ppermute | solution.py:449
  32.4 0.6 %collective-permute-start.10 = (f32[200,128]{1,0:T(8,128)S(1)}, f32[200,128]{1,0:T(8,128)S(1)}, u32[]{:S(2)}, u32[]{:S(2)}) collective-permute-start(f32[200,128]{1,0:T(8,128)S(1)} %collective-permute-done.7.r1), channel_id=1, source_target_pairs={{0,1},{1,0},{2,3},{3,2},{4,5},{5,4},{6,7},{7,6},{8,9},{9,8},{10,11... | collective-permute-start | bytes 307208 | tf_op jit(solution)/shard_map/ppermute | solution.py:449
  33.0 0.5 %collective-permute-start.12 = (f32[200,128]{1,0:T(8,128)S(1)}, f32[200,128]{1,0:T(8,128)S(1)}, u32[]{:S(2)}, u32[]{:S(2)}) collective-permute-start(f32[200,128]{1,0:T(8,128)S(1)} %collective-permute-done.9.r3), channel_id=1, source_target_pairs={{0,1},{1,0},{2,3},{3,2},{4,5},{5,4},{6,7},{7,6},{8,9},{9,8},{10,11... | collective-permute-start | bytes 307208 | tf_op jit(solution)/shard_map/ppermute | solution.py:449
  33.6 0.4 collective-permute-done.10.m1
  34.0 0.4 collective-permute-done.11.m2
  34.4 0.2 collective-permute-done.12.m3
  34.5 2.0 %k_filter.1 = (f32[32,8,128]{2,1,0:T(8,128)S(1)}, f32[4,48,128]{2,1,0:T(8,128)S(1)}, f32[48,128]{1,0:T(8,128)S(1)}, f32[8,128]{1,0:T(8,128)S(1)}) custom-call(f32[200,128]{1,0:T(8,128)S(1)} %collective-permute-done.7.r1, f32[200,128]{1,0:T(8,128)S(1)} %collective-permute-done.8.r2, f32[200,128]{1,0:T(8,128)S(1)} %collective-permute-done.9.r3, ...), custom_call_target="tpu_custom_call" | custom-call | flops 10000000 | bytes 1000000 | tf_op jit(solution)/shard_map/k_filter/pallas_call | solution.py:534
  36.5 10.8 %all_to_all.5.got_ref = f32[32,8,128]{2,1,0:T(8,128)S(1)} all-to-all(f32[32,8,128]{2,1,0:T(8,128)S(1)} %get-tuple-element.68), channel_id=1, replica_groups=mesh['cluster'=8,'tm_0'=4,'tm_1'=4,'tm_2'=2] {'tm_0','tm_1','tm_2'}, dimensions={0} | all-to-all | bytes 262144 | tf_op jit(solution)/shard_map/all_to_all | solution.py:546
  47.3 1.6 %k_smooth.1 = (f32[3,64,128]{2,1,0:T(8,128)}, f32[1,128]{1,0:T(1,128)}, f32[1,128]{1,0:T(1,128)}) custom-call(f32[32,8,128]{2,1,0:T(8,128)S(1)} %all_to_all.5.got_ref, f32[4,48,128]{2,1,0:T(8,128)S(1)} %get-tuple-element.69.local_ref, f32[48,128]{1,0:T(8,128)S(1)} %get-tuple-element.70.suffix_ref, f32[8,128]{1,0:T(8,128)S(1)} %get-tuple-element.71.final_ref, ...), custom_call_target="tpu_custom_call" | custom-call | flops 10000000 | bytes 1000000 | tf_op jit(solution)/shard_map/k_smooth/pallas_call | solution.py:547
  (18 shorter events, 0.1 us)
Async XLA Ops:
  0.6 0.8 %copy-start.3 = (f32[128,128]{1,0:T(8,128)S(1)}, f32[128,128]{1,0:T(8,128)}, u32[]{:S(2)}) copy-start(f32[128,128]{1,0:T(8,128)} %dyn_ref.3) | copy-start | bytes 196612
  0.6 0.8 %copy-start.4 = (s32[3,64]{1,0:T(4,128)S(1)}, s32[3,64]{1,0:T(4,128)}, u32[]{:S(2)}) copy-start(s32[3,64]{1,0:T(4,128)} %flags.3) | copy-start | bytes 2308
  0.7 0.9 %copy-start.2 = (f32[128,128]{1,0:T(8,128)S(1)}, f32[128,128]{1,0:T(8,128)}, u32[]{:S(2)}) copy-start(f32[128,128]{1,0:T(8,128)} %map_ref.1) | copy-start | bytes 196612
  0.7 0.9 %copy-start.6 = (f32[128]{0:T(128)S(1)}, f32[128]{0:T(128)}, u32[]{:S(2)}) copy-start(f32[128]{0:T(128)} %param.13) | copy-start | bytes 1540
  0.7 0.9 %copy-start.5 = (f32[128]{0:T(128)S(1)}, f32[128]{0:T(128)}, u32[]{:S(2)}) copy-start(f32[128]{0:T(128)} %param.11) | copy-start | bytes 1540
  0.7 1.0 %copy-start.1 = (f32[3,64,128]{2,1,0:T(8,128)S(1)}, f32[3,64,128]{2,1,0:T(8,128)}, u32[]{:S(2)}) copy-start(f32[3,64,128]{2,1,0:T(8,128)} %obs_raw.1) | copy-start | bytes 294916
  5.0 4.4 %collective-permute-start = (f32[3,136,128]{2,1,0:T(8,128)S(1)}, f32[3,136,128]{2,1,0:T(8,128)S(1)}, u32[]{:S(2)}, u32[]{:S(2)}) collective-permute-start(f32[3,136,128]{2,1,0:T(8,128)S(1)} %get-tuple-element.40.own_ref), channel_id=1, source_target_pairs={{0,1},{1,0},{2,3},{3,2},{4,5},{5,4},{6,7},{7,6},{8,9},{9,8},{10,11... | collective-permute-start | bytes 626696 | tf_op jit(solution)/shard_map/ppermute | solution.py:449
  9.6 4.2 %collective-permute-start.3 = (f32[200,128]{1,0:T(8,128)S(1)}, f32[200,128]{1,0:T(8,128)S(1)}, u32[]{:S(2)}, u32[]{:S(2)}) collective-permute-start(f32[200,128]{1,0:T(8,128)S(1)} %get-tuple-element.43.chip_ref), channel_id=1, source_target_pairs={{0,6},{2,0},{4,2},{6,4},{1,7},{3,1},{5,3},{7,5},{8,14},{10,8},{12,... | collective-permute-start | bytes 307208 | tf_op jit(solution)/shard_map/ppermute | solution.py:449
  10.7 5.1 %collective-permute-start.2 = (f32[200,128]{1,0:T(8,128)S(1)}, f32[200,128]{1,0:T(8,128)S(1)}, u32[]{:S(2)}, u32[]{:S(2)}) collective-permute-start(f32[200,128]{1,0:T(8,128)S(1)} %get-tuple-element.43.chip_ref), channel_id=1, source_target_pairs={{0,4},{2,6},{4,0},{6,2},{1,5},{3,7},{5,1},{7,3},{8,12},{10,14},{12... | collective-permute-start | bytes 307208 | tf_op jit(solution)/shard_map/ppermute | solution.py:449
  11.1 8.0 %collective-permute-start.1 = (f32[200,128]{1,0:T(8,128)S(1)}, f32[200,128]{1,0:T(8,128)S(1)}, u32[]{:S(2)}, u32[]{:S(2)}) collective-permute-start(f32[200,128]{1,0:T(8,128)S(1)} %get-tuple-element.43.chip_ref), channel_id=1, source_target_pairs={{0,2},{2,4},{4,6},{6,0},{1,3},{3,5},{5,7},{7,1},{8,10},{10,12},{12... | collective-permute-start | bytes 307208 | tf_op jit(solution)/shard_map/ppermute | solution.py:449
  13.8 5.9 %collective-permute-start.6 = (f32[200,128]{1,0:T(8,128)S(1)}, f32[200,128]{1,0:T(8,128)S(1)}, u32[]{:S(2)}, u32[]{:S(2)}) collective-permute-start(f32[200,128]{1,0:T(8,128)S(1)} %collective-permute-done.3.r3), channel_id=1, source_target_pairs={{0,1},{1,0},{2,3},{3,2},{4,5},{5,4},{6,7},{7,6},{8,9},{9,8},{10,11... | collective-permute-start | bytes 307208 | tf_op jit(solution)/shard_map/ppermute | solution.py:449
  15.8 3.9 %collective-permute-start.5 = (f32[200,128]{1,0:T(8,128)S(1)}, f32[200,128]{1,0:T(8,128)S(1)}, u32[]{:S(2)}, u32[]{:S(2)}) collective-permute-start(f32[200,128]{1,0:T(8,128)S(1)} %collective-permute-done.2.r2), channel_id=1, source_target_pairs={{0,1},{1,0},{2,3},{3,2},{4,5},{5,4},{6,7},{7,6},{8,9},{9,8},{10,11... | collective-permute-start | bytes 307208 | tf_op jit(solution)/shard_map/ppermute | solution.py:449
  19.1 1.5 %collective-permute-start.4 = (f32[200,128]{1,0:T(8,128)S(1)}, f32[200,128]{1,0:T(8,128)S(1)}, u32[]{:S(2)}, u32[]{:S(2)}) collective-permute-start(f32[200,128]{1,0:T(8,128)S(1)} %collective-permute-done.1.r1), channel_id=1, source_target_pairs={{0,1},{1,0},{2,3},{3,2},{4,5},{5,4},{6,7},{7,6},{8,9},{9,8},{10,11... | collective-permute-start | bytes 307208 | tf_op jit(solution)/shard_map/ppermute | solution.py:449
  21.5 7.3 %collective-permute-start.9 = (f32[200,128]{1,0:T(8,128)S(1)}, f32[200,128]{1,0:T(8,128)S(1)}, u32[]{:S(2)}, u32[]{:S(2)}) collective-permute-start(f32[200,128]{1,0:T(8,128)S(1)} %get-tuple-element.51.after_ref), channel_id=1, source_target_pairs={{0,24},{8,0},{16,8},{24,16},{1,25},{9,1},{17,9},{25,17},{2,26},{10... | collective-permute-start | bytes 307208 | tf_op jit(solution)/shard_map/ppermute | solution.py:449
  24.0 5.1 %collective-permute-start.8 = (f32[200,128]{1,0:T(8,128)S(1)}, f32[200,128]{1,0:T(8,128)S(1)}, u32[]{:S(2)}, u32[]{:S(2)}) collective-permute-start(f32[200,128]{1,0:T(8,128)S(1)} %get-tuple-element.51.after_ref), channel_id=1, source_target_pairs={{0,16},{8,24},{16,0},{24,8},{1,17},{9,25},{17,1},{25,9},{2,18},{10... | collective-permute-start | bytes 307208 | tf_op jit(solution)/shard_map/ppermute | solution.py:449
  24.5 7.8 %collective-permute-start.7 = (f32[200,128]{1,0:T(8,128)S(1)}, f32[200,128]{1,0:T(8,128)S(1)}, u32[]{:S(2)}, u32[]{:S(2)}) collective-permute-start(f32[200,128]{1,0:T(8,128)S(1)} %get-tuple-element.51.after_ref), channel_id=1, source_target_pairs={{0,8},{8,16},{16,24},{24,0},{1,9},{9,17},{17,25},{25,1},{2,10},{10... | collective-permute-start | bytes 307208 | tf_op jit(solution)/shard_map/ppermute | solution.py:449
  27.6 6.9 %copy-start = (f32[3,128]{1,0:T(4,128)S(1)}, f32[3,128]{1,0:T(4,128)}, u32[]{:S(2)}) copy-start(f32[3,128]{1,0:T(4,128)} %init_ref.1) | copy-start | bytes 4612
  32.4 1.6 %collective-permute-start.10 = (f32[200,128]{1,0:T(8,128)S(1)}, f32[200,128]{1,0:T(8,128)S(1)}, u32[]{:S(2)}, u32[]{:S(2)}) collective-permute-start(f32[200,128]{1,0:T(8,128)S(1)} %collective-permute-done.7.r1), channel_id=1, source_target_pairs={{0,1},{1,0},{2,3},{3,2},{4,5},{5,4},{6,7},{7,6},{8,9},{9,8},{10,11... | collective-permute-start | bytes 307208 | tf_op jit(solution)/shard_map/ppermute | solution.py:449
  33.0 1.3 %collective-permute-start.11 = (f32[200,128]{1,0:T(8,128)S(1)}, f32[200,128]{1,0:T(8,128)S(1)}, u32[]{:S(2)}, u32[]{:S(2)}) collective-permute-start(f32[200,128]{1,0:T(8,128)S(1)} %collective-permute-done.8.r2), channel_id=1, source_target_pairs={{0,1},{1,0},{2,3},{3,2},{4,5},{5,4},{6,7},{7,6},{8,9},{9,8},{10,11... | collective-permute-start | bytes 307208 | tf_op jit(solution)/shard_map/ppermute | solution.py:449
  33.0 1.5 %collective-permute-start.12 = (f32[200,128]{1,0:T(8,128)S(1)}, f32[200,128]{1,0:T(8,128)S(1)}, u32[]{:S(2)}, u32[]{:S(2)}) collective-permute-start(f32[200,128]{1,0:T(8,128)S(1)} %collective-permute-done.9.r3), channel_id=1, source_target_pairs={{0,1},{1,0},{2,3},{3,2},{4,5},{5,4},{6,7},{7,6},{8,9},{9,8},{10,11... | collective-permute-start | bytes 307208 | tf_op jit(solution)/shard_map/ppermute | solution.py:449

commit v3 on v2

--- a/solution.py
+++ b/solution.py
@@ -106,6 +106,7 @@
 LEVELS = ((0, 24), (24, 12), (36, 6))
 OFFS = (0, 48, 72, 84)
 PART = SEQ * HALF + 8
+FULL = SEQ * N + 8
 
 
 def k_first(eye_ref):
@@ -172,20 +173,27 @@
             get = lambda k, level=level: nodes[LEVELS[level][0] + k]
 
 
+def put(ref, b, matrix):
+    rows = matrix.shape[0]
+    ref[b * rows : (b + 1) * rows, :] = matrix
+
+
 def put_offsets(ref, offs):
-    ref[SEQ * HALF : PART, :] = stacked(*offs, jnp.zeros((8 - SEQ, N), F32))
+    rows = ref.shape[0]
+    ref[rows - 8 : rows, :] = stacked(*offs, jnp.zeros((8 - SEQ, N), F32))
+
+
+def offset_of(ref, b):
+    at = ref.shape[0] - 8 + b
+    return ref[at : at + 1, :]
 
 
 def half_of(ref, b):
     return ref[b * HALF : (b + 1) * HALF, :]
 
 
-def offset_of(ref, b):
-    return ref[SEQ * HALF + b : SEQ * HALF + b + 1, :]
-
-
-def from_halves(low_ref, high_ref, b):
-    return stacked(half_of(low_ref, b), half_of(high_ref, b)), offset_of(low_ref, b)
+def full_of(ref, b):
+    return ref[b * N : (b + 1) * N, :]
 
 
 def in_order(mine_ref, mate_ref, b):
@@ -195,50 +203,63 @@
     return matrix, offset_of(mine_ref, b)
 
 
+def chosen(flag, p_ref, q_ref, b):
+    return (
+        pick(flag, full_of(p_ref, b), full_of(q_ref, b)),
+        pick(flag, offset_of(p_ref, b), offset_of(q_ref, b)),
+    )
+
+
+def around(refs, b):
+    near, near_mate, two, two_mate = refs
+    first = lax.axis_index("tm_2") == 0
+    return (
+        chosen(first, near, near_mate, b),
+        in_order(two, two_mate, b),
+        chosen(first, near_mate, near, b),
+    )
+
+
 def then(p, q):
     return joined(pair(p[0]), p[1], pair(q[0]), q[1])
 
 
-def then_half(p, q, ref, b):
-    left = pick(lax.axis_index("tm_2") == 0, p[0][:HALF], p[0][HALF:])
-    got = mul_pair(stacked(pair(left), pair(jnp.broadcast_to(p[1], (16, N)))), pair(q[0]))
-    ref[b * HALF : (b + 1) * HALF, :] = got[:HALF]
-    return got[HALF : HALF + 1] + q[1]
-
-
-def k_core(own_ref, mate_ref, mine_ref, low_ref, high_ref):
+def put_both(full_ref, mine_ref, maps):
     first = lax.axis_index("tm_2") == 0
-    offs = []
+    for b, (matrix, off) in enumerate(maps):
+        put(full_ref, b, matrix)
+        put(mine_ref, b, pick(first, matrix[:HALF], matrix[HALF:]))
+    for ref in (full_ref, mine_ref):
+        put_offsets(ref, [off for _, off in maps])
+
+
+def k_core(own_ref, mate_ref, out_ref, mine_ref):
+    first = lax.axis_index("tm_2") == 0
+    maps = []
     for b in range(SEQ):
         own, mate = own_ref[b], mate_ref[b]
         p, q = pick(first, own, mate), pick(first, mate, own)
-        matrix, off = then((p[:N], p[N : N + 1]), (q[:N], q[N : N + 1]))
-        low, high = matrix[:HALF], matrix[HALF:]
-        for ref, half in ((low_ref, low), (high_ref, high), (mine_ref, pick(first, low, high))):
-            ref[b * HALF : (b + 1) * HALF, :] = half
-        offs.append(off)
-    for ref in (low_ref, high_ref, mine_ref):
-        put_offsets(ref, offs)
-
-
-def k_total(low_ref, high_ref, r1, r2, r3, m1, m2, m3, out_ref, full_ref, maps, offs):
+        maps.append(then((p[:N], p[N : N + 1]), (q[:N], q[N : N + 1])))
+    put_both(out_ref, mine_ref, maps)
+
+
+def k_total(own_ref, near, near_mate, two, two_mate, out_ref, mine_ref, ahead_ref, maps, offs):
     me = lax.axis_index("tm_1")
     for b in range(SEQ):
-        for d, (r, m) in enumerate(((r1, m1), (r2, m2), (r3, m3))):
-            matrix, off = in_order(r, m, b)
+        for d, (matrix, off) in enumerate(around((near, near_mate, two, two_mate), b)):
             slot = lax.rem(me + 3 - d, 4)
+            off = jnp.broadcast_to(off, (8, N))
             maps[slot, b] = matrix
-            offs[slot, b] = jnp.broadcast_to(off, (8, N))
-            full_ref[d, b, 0:N, :] = matrix
-            full_ref[d, b, N : N + 8, :] = jnp.broadcast_to(off, (8, N))
-        matrix, off = from_halves(low_ref, high_ref, b)
-        maps[me, b] = matrix
-        offs[me, b] = jnp.broadcast_to(off, (8, N))
+            offs[slot, b] = off
+            ahead_ref[d, b, 0:N, :] = matrix
+            ahead_ref[d, b, N : N + 8, :] = off
+        maps[me, b] = full_of(own_ref, b)
+        offs[me, b] = jnp.broadcast_to(offset_of(own_ref, b), (8, N))
     ends = []
     for b in range(SEQ):
         p = [(maps[k, b], offs[k, b, 0:1, :]) for k in range(4)]
-        ends.append(then_half(then(p[0], p[1]), then(p[2], p[3]), out_ref, b))
-    put_offsets(out_ref, ends)
+        ends.append(then(then(p[0], p[1]), then(p[2], p[3])))
+    put_both(out_ref, mine_ref, ends)
 
 
 def k_prefix(chip_ref, flags, table, nodes, offs, pre_ref, preoff_ref):
@@ -268,7 +289,7 @@
 
 
 def k_powers(
-    after_ref, eye_ref, dyn_ref, dynt_ref, near_ref, far_ref, reach_ref, cross_ref, resid_ref
+    eye_ref, dyn_ref, dynt_ref, near_ref, far_ref, reach_ref, cross_ref, resid_ref
 ):
     eye, dyn = eye_ref[...], dyn_ref[...]
     d2 = mul_exact(dyn, dyn)
@@ -303,13 +324,13 @@
     cross_ref[10] = pair(mul_exact(w16, powers[8]))
 
 
-def k_entry(after_ref, full_ref, mate_ref, entry_ref, entryoff_ref):
+def k_entry(ahead_ref, mate_ref, entry_ref, entryoff_ref):
     me, second = lax.axis_index("tm_1"), lax.axis_index("tm_2") == 1
     entryoff_ref[...] = jnp.zeros_like(entryoff_ref)
     for b in range(SEQ):
         so_far = (identity(), jnp.zeros((1, N), F32))
         for source, flag in (
-            (full_ref.at[2], me >= 3), (full_ref.at[1], me >= 2), (full_ref.at[0], me >= 1),
+            (ahead_ref.at[2], me >= 3), (ahead_ref.at[1], me >= 2), (ahead_ref.at[0], me >= 1),
             (mate_ref, second),
         ):
             got = then(so_far, (source[b, 0:N, :], source[b, N : N + 1, :]))
@@ -318,8 +339,16 @@
         entryoff_ref[b : b + 1, :] = so_far[1]
 
 
+def k_tables(
+    after_ref, eye_ref, dyn_ref, dynt_ref, ahead_ref, mate_ref,
+    near_ref, far_ref, reach_ref, cross_ref, resid_ref, entry_ref, entryoff_ref,
+):
+    k_entry(ahead_ref, mate_ref, entry_ref, entryoff_ref)
+    k_powers(eye_ref, dyn_ref, dynt_ref, near_ref, far_ref, reach_ref, cross_ref, resid_ref)
+
+
 def k_filter(
-    r1, r2, r3, m1, m2, m3, entry_ref, entryoff_ref, init_ref, obs_ref,
+    near, near_mate, two, two_mate, entry_ref, entryoff_ref, init_ref, obs_ref,
     rows_ref, dynt_ref, pre_ref, preoff_ref, step_ref, u_ref, mask_ref, reach_ref,
     resid_ref, cross_ref, send_ref, local_ref, suffix_ref, final_ref,
 ):
@@ -328,8 +357,9 @@
     starts = []
     for b in range(SEQ):
         row = init_ref[b : b + 1, :]
-        for d, r, m in ((3, r3, m3), (2, r2, m2), (1, r1, m1)):
-            matrix, off = in_order(r, m, b)
+        ahead = around((near, near_mate, two, two_mate), b)
+        for d in (3, 2, 1):
+            matrix, off = ahead[d - 1]
             row = pick(group >= d, apply_row(row, matrix) + off, row)
         starts.append(apply_row(row, entry_ref[b]) + entryoff_ref[b : b + 1, :])
     rows = []
@@ -449,16 +479,19 @@
     return lax.ppermute(a, axis, [(i, (i + by) % count) for i in range(count)])
 
 
-def exchanged(mine, axis, work):
-    got = [shifted(mine, axis, d) for d in (1, 2, 3)]
-    done = work(mine)
+def exchanged(full, mine, axis, work):
+    ring = [(2 * i, (2 * i + 2) % 8) for i in range(4)] + [
+        (2 * i + 1, (2 * i + 7) % 8) for i in range(4)
+    ]
+    got = [lax.ppermute(full, (axis, "tm_2"), ring), shifted(mine, axis, 2)]
+    done = work(full)
     swaps = [shifted(lax.optimization_barrier((a, done[-1]))[0], "tm_2", 1) for a in got]
-    return got, swaps, done
+    return (got[0], swaps[0], got[1], swaps[1]), done
 
 
 def local(obs, present, sensors, log_prec, dynamics, prior_var, obs_map, init_state):
     lp, pv = log_prec.reshape(1, N), prior_var.reshape(1, N)
-    part = out((PART, N))
+    both = (out((FULL, N)), out((PART, N)))
     square = out((N, N))
     square = out((N, N))
     eye = call(k_first, "k_first", [], square, (), 4 * 10**9, 10**7)()
@@ -483,9 +516,7 @@
         10**6,
     )(present, sensors, eye, obs, present, lp, dynamics, pv, obs_map)
     mate = shifted(root, "tm_2", 1)
-    chip, low, high = call(k_core, "k_core", [VM] * 2, (part, part, part), (), 10**7, 10**6)(
-        root, mate
-    )
+    chip, mine = call(k_core, "k_core", [VM] * 2, both, (), 10**7, 10**6)(root, mate)
     prefix = call(
         k_prefix,
         "k_prefix",
@@ -495,52 +526,48 @@
         3 * 10**9,
         10**7,
     )
-    got, mates, (pre, preoff) = exchanged(
-        chip, "tm_1", lambda a: prefix(a, present, table, nodes, offs)
-    )
-    group, full = call(
+    got, (pre, preoff) = exchanged(
+        chip, mine, "tm_1", lambda a: prefix(a, present, table, nodes, offs)
+    )
+    group, mine, ahead = call(
         k_total,
         "k_total",
-        [VM] * 8,
-        (part, out((3, SEQ, N + 8, N))),
+        [VM] * 5,
+        (*both, out((3, SEQ, N + 8, N))),
         [pltpu.VMEM((4, SEQ, N, N), F32), pltpu.VMEM((4, SEQ, 8, N), F32)],
         10**8,
         10**6,
-    )(low, high, *got, *mates)
-    powers = call(
-        k_powers,
-        "k_powers",
-        [VM] * 4,
+    )(chip, *got)
+    tables = call(
+        k_tables,
+        "k_tables",
+        [VM] * 6,
         (
             out((SUB, N, 2 * N), BF16),
             out((LEAVES, N, N)),
             out((len(REACH), N, 2 * N), BF16),
             out((11, N, 2 * N), BF16),
             out((SUB, N, 2 * N), BF16),
+            out((SEQ, N, N)),
+            out((8, N)),
         ),
         (),
-        3 * 10**9,
+        4 * 10**9,
         10**7,
     )
-    entries = call(
-        k_entry, "k_entry", [VM] * 3, (out((SEQ, N, N)), out((8, N))), (), 10**9, 10**7
-    )
-
-    def work(a):
-        tables = powers(a, eye, dynamics, dyn_t)
-        return (*tables, *entries(tables[-1], full, mate))
-
-    got, mates, (near, far, reach, cross, resid, entry, entryoff) = exchanged(group, "tm_0", work)
+    got, (near, far, reach, cross, resid, entry, entryoff) = exchanged(
+        group, mine, "tm_0", lambda a: tables(a, eye, dynamics, dyn_t, ahead, mate)
+    )
     send, near_sums, suffix, final = call(
         k_filter,
         "k_filter",
-        [VM] * 20,
+        [VM] * 18,
         (out((BLOCKS, 8, N)), out((SUB, ROWS, N)), out((ROWS, N)), out((8, N))),
         (),
         10**7,
         10**6,
     )(
-        *got, *mates, entry, entryoff, init_state, obs_s, rows, dyn_t, pre, preoff, step, u,
+        *got, entry, entryoff, init_state, obs_s, rows, dyn_t, pre, preoff, step, u,
         mask, reach, resid, cross,
     )
     got = lax.all_to_all(send, TM, 0, 0, tiled=True)

time: 49.1 us -> 47.9 us (0.976)
  starting transfers between devices: 15.6 us -> 12.3 us
  waiting for transfers between devices: 7.5 us -> 8.84 us
  blocking collectives: 10.8 us -> 11.9 us
    ppermute x0 -> x2, waiting for transfers between devices: none -> 5.13 us  [exchanged(): got = [lax.ppermute(full, (axis, 'tm_2'), ring), shifted(mine, axis, 2)]]
    ppermute x13 -> x7, starting transfers between devices: 15.6 us -> 10.6 us  [shifted(): return lax.ppermute(a, axis, [(i, (i + by) % count) for i in range(count)])]
    ppermute x13 -> x7, waiting for transfers between devices: 7.5 us -> 3.7 us  [shifted(): return lax.ppermute(a, axis, [(i, (i + by) % count) for i in range(count)])]
    ppermute x0 -> x2, starting transfers between devices: none -> 1.65 us  [exchanged(): got = [lax.ppermute(full, (axis, 'tm_2'), ring), shifted(mine, axis, 2)]]
    all_to_all x1, blocking collectives: 10.8 us -> 11.9 us  [local(): got = lax.all_to_all(send, TM, 0, 0, tiled=True)]
    pallas_call x5 -> x4, Pallas kernels: 6.66 us -> 6.53 us  [the longest x1 3.45 us: local(): tables(a, eye, dynamics, dyn_t, ahead, mate)]
  transfers between devices with their start and end apart: 13 -> 9, of which waited for: 9 -> 5; matrix products, arithmetic and copies ran while one was open for 0% -> 0% of each run, Pallas kernels for 11% -> 11%
where the time goes in v3:
time: 47.9 us; the launch traced here: 47.8 us
  Pallas kernels  13.1 us (27%)
  starting transfers between devices  12.3 us (26%)
  blocking collectives  11.9 us (25%)
  waiting for transfers between devices  8.84 us (18%)
  between operations  1.47 us (3%)
    all_to_all x1, blocking collectives, local(): got = lax.all_to_all(send, TM, 0, 0, tiled=True)  11.9 us
    ppermute x7, starting transfers between devices, shifted(): return lax.ppermute(a, axis, [(i, (i + by) % count) for i in range(count)])  10.6 us
    ppermute x2, waiting for transfers between devices, exchanged(): got = [lax.ppermute(full, (axis, 'tm_2'), ring), shifted(mine, axis, 2)]  5.13 us
    ppermute x7, waiting for transfers between devices, shifted(): return lax.ppermute(a, axis, [(i, (i + by) % count) for i in range(count)])  3.7 us
    pallas_call x1, Pallas kernels, local(): tables(a, eye, dynamics, dyn_t, ahead, mate)  3.45 us
    pallas_call x1, Pallas kernels, local(): call(k_block, 'k_block', [SM] * 2 + [VM] * 7, (out((SEQ, N + 8, N)), squa...  3.3 us
    pallas_call x1, Pallas kernels, local(): call(k_filter, 'k_filter', [VM] * 18, (out((BLOCKS, 8, N)), out((SUB, ROW...  1.98 us
    ppermute x2, starting transfers between devices, exchanged(): got = [lax.ppermute(full, (axis, 'tm_2'), ring), shifted(mine, axis, 2)]  1.65 us
  transfers between devices with their start and end apart: 9, of which 5 were waited for; matrix products, arithmetic and copies ran while one was open for 0% of the time, Pallas kernels for 11%

profile of v3, /device:TPU:1, one launch (start us, length us, event | category | flops | bytes accessed | tf_op | source)
XLA Modules:
  0.0 47.8 jit_solution(668258108034883466)
XLA Ops:
  0.6 0.0 copy-start.3
  0.6 0.0 copy-start.4
  1.4 0.0 copy-done.3
  1.5 0.0 copy-done.4
  1.5 0.0 copy-done.2
  1.5 0.1 copy-done.1
  1.7 3.3 %k_block.1 = (f32[3,136,128]{2,1,0:T(8,128)S(1)}, f32[128,128]{1,0:T(8,128)S(1)}, bf16[16,128,256]{2,1,0:T(8,128)(2,1)S(1)}, bf16[42,128,256]{2,1,0:T(8,128)(2,1...) custom-call(s32[3,64]{1,0:T(4,128)S(1)} %copy-done.4, ...), custom_call_target="tpu_custom_call" | custom-call | flops 1000000000 | bytes 1000000 | tf_op jit(solution)/shard_map/k_block/pallas_call | solution.py:498
  5.0 3.4 %collective-permute-start = (f32[3,136,128]{2,1,0:T(8,128)S(1)}, f32[3,136,128]{2,1,0:T(8,128)S(1)}, u32[]{:S(2)}, u32[]{:S(2)}) collective-permute-start(f32[3,136,128]{2,1,0:T(8,128)S(1)} %get-tuple-element.38.own_ref), channel_id=1, source_target_pairs={{0,1},{1,0},{2,3},{3,2},{4,5},{5,4},{6,7},{7,6},{8,9},{9,8},{10,11... | collective-permute-start | bytes 626696 | tf_op jit(solution)/shard_map/ppermute | solution.py:479
  8.3 1.1 %collective-permute-done.mate_ref = f32[3,136,128]{2,1,0:T(8,128)S(1)} collective-permute-done((f32[3,136,128]{2,1,0:T(8,128)S(1)}, f32[3,136,128]{2,1,0:T(8,128)S(1)}, u32[]{:S(2)}, u32[]{:S(2)}) %collective-permute-start) | collective-permute-done | bytes 208928 | tf_op jit(solution)/shard_map/ppermute | solution.py:479
  9.4 0.2 k_core.1
  9.6 1.3 %collective-permute-start.3 = (f32[200,128]{1,0:T(8,128)S(1)}, f32[200,128]{1,0:T(8,128)S(1)}, u32[]{:S(2)}, u32[]{:S(2)}) collective-permute-start(f32[200,128]{1,0:T(8,128)S(1)} %get-tuple-element.45), channel_id=1, source_target_pairs={{0,4},{2,6},{4,0},{6,2},{1,5},{3,7},{5,1},{7,3},{8,12},{10,14},{12... | collective-permute-start | bytes 307208 | tf_op jit(solution)/shard_map/ppermute | solution.py:479
  10.9 0.8 %collective-permute-start.1 = (f32[392,128]{1,0:T(8,128)S(1)}, f32[392,128]{1,0:T(8,128)S(1)}, u32[]{:S(2)}, u32[]{:S(2)}) collective-permute-start(f32[392,128]{1,0:T(8,128)S(1)} %get-tuple-element.39.chip_ref.own_ref), channel_id=1, source_target_pairs={{0,2},{2,4},{4,6},{6,0},{1,7},{3,1},{5,3},{7,5},{8,10},{10,12},{12... | collective-permute-start | bytes 602120 | tf_op jit(solution)/shard_map/ppermute | solution.py:486
  11.7 1.6 %k_prefix.1 = (f32[48,128,128]{2,1,0:T(8,128)S(1)}, f32[48,128]{1,0:T(8,128)S(1)}) custom-call(f32[392,128]{1,0:T(8,128)S(1)} %get-tuple-element.39.chip_ref.own_ref, s32[3,64]{1,0:T(4,128)S(1)} %copy-done.4, bf16[16,128,256]{2,1,0:T(8,128)(2,1)S(1)} %get-tuple-element.40.table, bf16[42,128,256]{2,1,0:T(8,128)(2,1)S(1)} %get-tuple-element.41.nodes, ...), custom_call_target="tpu_custom_call" | custom-call | flops 3000000000 | bytes 10000000 | tf_op jit(solution)/shard_map/k_prefix/pallas_call | solution.py:530
  13.3 3.6 %collective-permute-done.1.near = f32[392,128]{1,0:T(8,128)S(1)} collective-permute-done((f32[392,128]{1,0:T(8,128)S(1)}, f32[392,128]{1,0:T(8,128)S(1)}, u32[]{:S(2)}, u32[]{:S(2)}) %collective-permute-start.1) | collective-permute-done | bytes 200736 | tf_op jit(solution)/shard_map/ppermute | solution.py:486
  16.9 1.8 %collective-permute-start.2 = (f32[392,128]{1,0:T(8,128)S(1)}, f32[392,128]{1,0:T(8,128)S(1)}, u32[]{:S(2)}, u32[]{:S(2)}) collective-permute-start(f32[392,128]{1,0:T(8,128)S(1)} %collective-permute-done.1.near), channel_id=1, source_target_pairs={{0,1},{1,0},{2,3},{3,2},{4,5},{5,4},{6,7},{7,6},{8,9},{9,8},{10,11... | collective-permute-start | bytes 602120 | tf_op jit(solution)/shard_map/ppermute | solution.py:479
  18.7 0.0 collective-permute-done.3.two
  18.7 0.0 collective-permute-start.4
  18.7 1.3 %collective-permute-done.4.two_mate = f32[200,128]{1,0:T(8,128)S(1)} collective-permute-done((f32[200,128]{1,0:T(8,128)S(1)}, f32[200,128]{1,0:T(8,128)S(1)}, u32[]{:S(2)}, u32[]{:S(2)}) %collective-permute-start.4) | collective-permute-done | bytes 102432 | tf_op jit(solution)/shard_map/ppermute | solution.py:479
  20.0 0.0 collective-permute-done.2.near_mate
  20.0 0.9 %k_total.1 = (f32[392,128]{1,0:T(8,128)S(1)}, f32[200,128]{1,0:T(8,128)S(1)}, f32[3,3,136,128]{3,2,1,0:T(8,128)S(1)}) custom-call(f32[392,128]{1,0:T(8,128)S(1)} %get-tuple-element.39.chip_ref.own_ref, f32[392,128]{1,0:T(8,128)S(1)} %collective-permute-done.1.near, f32[392,128]{1,0:T(8,128)S(1)} %collective-permute-done.2.near_mate, ...), custom_call_target="tpu_custom_call" | custom-call | flops 100000000 | bytes 1000000 | tf_op jit(solution)/shard_map/k_total/pallas_call | solution.py:532
  20.9 2.6 %collective-permute-start.7 = (f32[200,128]{1,0:T(8,128)S(1)}, f32[200,128]{1,0:T(8,128)S(1)}, u32[]{:S(2)}, u32[]{:S(2)}) collective-permute-start(f32[200,128]{1,0:T(8,128)S(1)} %get-tuple-element.52), channel_id=1, source_target_pairs={{0,16},{8,24},{16,0},{24,8},{1,17},{9,25},{17,1},{25,9},{2,18},{10... | collective-permute-start | bytes 307208 | tf_op jit(solution)/shard_map/ppermute | solution.py:479
  23.5 0.9 %collective-permute-start.5 = (f32[392,128]{1,0:T(8,128)S(1)}, f32[392,128]{1,0:T(8,128)S(1)}, u32[]{:S(2)}, u32[]{:S(2)}) collective-permute-start(f32[392,128]{1,0:T(8,128)S(1)} %get-tuple-element.47.after_ref), channel_id=1, source_target_pairs={{0,8},{8,16},{16,24},{24,0},{1,25},{9,1},{17,9},{25,17},{2,10},{10... | collective-permute-start | bytes 602120 | tf_op jit(solution)/shard_map/ppermute | solution.py:486
  24.4 3.5 %k_tables.1 = (bf16[4,128,256]{2,1,0:T(8,128)(2,1)S(1)}, f32[16,128,128]{2,1,0:T(8,128)S(1)}, bf16[6,128,256]{2,1,0:T(8,128)(2,1)S(1)}, bf16[11,128,256]{2,1,0:T...) custom-call(f32[392,128]{1,0:T(8,128)S(1)} %get-tuple-element.47.after_ref, ...), custom_call_target="tpu_custom_call" | custom-call | flops 4000000000 | bytes 10000000 | tf_op jit(solution)/shard_map/k_tables/pallas_call | solution.py:559
  27.8 1.6 %collective-permute-done.5.near = f32[392,128]{1,0:T(8,128)S(1)} collective-permute-done((f32[392,128]{1,0:T(8,128)S(1)}, f32[392,128]{1,0:T(8,128)S(1)}, u32[]{:S(2)}, u32[]{:S(2)}) %collective-permute-start.5) | collective-permute-done | bytes 200736 | tf_op jit(solution)/shard_map/ppermute | solution.py:486
  29.4 1.6 %collective-permute-start.6 = (f32[392,128]{1,0:T(8,128)S(1)}, f32[392,128]{1,0:T(8,128)S(1)}, u32[]{:S(2)}, u32[]{:S(2)}) collective-permute-start(f32[392,128]{1,0:T(8,128)S(1)} %collective-permute-done.5.near), channel_id=1, source_target_pairs={{0,1},{1,0},{2,3},{3,2},{4,5},{5,4},{6,7},{7,6},{8,9},{9,8},{10,11... | collective-permute-start | bytes 602120 | tf_op jit(solution)/shard_map/ppermute | solution.py:479
  31.0 0.0 collective-permute-done.7.two
  31.0 0.0 collective-permute-start.8
  31.0 1.3 %collective-permute-done.8.two_mate = f32[200,128]{1,0:T(8,128)S(1)} collective-permute-done((f32[200,128]{1,0:T(8,128)S(1)}, f32[200,128]{1,0:T(8,128)S(1)}, u32[]{:S(2)}, u32[]{:S(2)}) %collective-permute-start.8) | collective-permute-done | bytes 102432 | tf_op jit(solution)/shard_map/ppermute | solution.py:479
  32.3 0.0 collective-permute-done.6.near_mate
  32.3 2.0 %k_filter.1 = (f32[32,8,128]{2,1,0:T(8,128)S(1)}, f32[4,48,128]{2,1,0:T(8,128)S(1)}, f32[48,128]{1,0:T(8,128)S(1)}, f32[8,128]{1,0:T(8,128)S(1)}) custom-call(f32[392,128]{1,0:T(8,128)S(1)} %collective-permute-done.5.near, f32[392,128]{1,0:T(8,128)S(1)} %collective-permute-done.6.near_mate, f32[200,128]{1,0:T(8,128)S(1)} %collective-permute-done.7.two, ...), custom_call_target="tpu_custom_call" | custom-call | flops 10000000 | bytes 1000000 | tf_op jit(solution)/shard_map/k_filter/pallas_call | solution.py:561
  34.3 11.9 %all_to_all.5.got_ref = f32[32,8,128]{2,1,0:T(8,128)S(1)} all-to-all(f32[32,8,128]{2,1,0:T(8,128)S(1)} %get-tuple-element.64), channel_id=1, replica_groups=mesh['cluster'=8,'tm_0'=4,'tm_1'=4,'tm_2'=2] {'tm_0','tm_1','tm_2'}, dimensions={0} | all-to-all | bytes 262144 | tf_op jit(solution)/shard_map/all_to_all | solution.py:573
  46.2 1.6 %k_smooth.1 = (f32[3,64,128]{2,1,0:T(8,128)}, f32[1,128]{1,0:T(1,128)}, f32[1,128]{1,0:T(1,128)}) custom-call(f32[32,8,128]{2,1,0:T(8,128)S(1)} %all_to_all.5.got_ref, f32[4,48,128]{2,1,0:T(8,128)S(1)} %get-tuple-element.65.local_ref, f32[48,128]{1,0:T(8,128)S(1)} %get-tuple-element.66.suffix_ref, f32[8,128]{1,0:T(8,128)S(1)} %get-tuple-element.67.final_ref, ...), custom_call_target="tpu_custom_call" | custom-call | flops 10000000 | bytes 1000000 | tf_op jit(solution)/shard_map/k_smooth/pallas_call | solution.py:574
  (9 shorter events, 0.0 us)
Async XLA Ops:
  0.6 0.8 %copy-start.3 = (f32[128,128]{1,0:T(8,128)S(1)}, f32[128,128]{1,0:T(8,128)}, u32[]{:S(2)}) copy-start(f32[128,128]{1,0:T(8,128)} %dyn_ref.3) | copy-start | bytes 196612
  0.6 0.8 %copy-start.4 = (s32[3,64]{1,0:T(4,128)S(1)}, s32[3,64]{1,0:T(4,128)}, u32[]{:S(2)}) copy-start(s32[3,64]{1,0:T(4,128)} %flags.3) | copy-start | bytes 2308
  0.7 0.9 %copy-start.2 = (f32[128,128]{1,0:T(8,128)S(1)}, f32[128,128]{1,0:T(8,128)}, u32[]{:S(2)}) copy-start(f32[128,128]{1,0:T(8,128)} %map_ref.1) | copy-start | bytes 196612
  0.7 0.9 %copy-start.6 = (f32[128]{0:T(128)S(1)}, f32[128]{0:T(128)}, u32[]{:S(2)}) copy-start(f32[128]{0:T(128)} %param.13) | copy-start | bytes 1540
  0.7 0.9 %copy-start.5 = (f32[128]{0:T(128)S(1)}, f32[128]{0:T(128)}, u32[]{:S(2)}) copy-start(f32[128]{0:T(128)} %param.11) | copy-start | bytes 1540
  0.7 1.0 %copy-start.1 = (f32[3,64,128]{2,1,0:T(8,128)S(1)}, f32[3,64,128]{2,1,0:T(8,128)}, u32[]{:S(2)}) copy-start(f32[3,64,128]{2,1,0:T(8,128)} %obs_raw.1) | copy-start | bytes 294916
  5.0 4.4 %collective-permute-start = (f32[3,136,128]{2,1,0:T(8,128)S(1)}, f32[3,136,128]{2,1,0:T(8,128)S(1)}, u32[]{:S(2)}, u32[]{:S(2)}) collective-permute-start(f32[3,136,128]{2,1,0:T(8,128)S(1)} %get-tuple-element.38.own_ref), channel_id=1, source_target_pairs={{0,1},{1,0},{2,3},{3,2},{4,5},{5,4},{6,7},{7,6},{8,9},{9,8},{10,11... | collective-permute-start | bytes 626696 | tf_op jit(solution)/shard_map/ppermute | solution.py:479
  9.6 9.0 %collective-permute-start.3 = (f32[200,128]{1,0:T(8,128)S(1)}, f32[200,128]{1,0:T(8,128)S(1)}, u32[]{:S(2)}, u32[]{:S(2)}) collective-permute-start(f32[200,128]{1,0:T(8,128)S(1)} %get-tuple-element.45), channel_id=1, source_target_pairs={{0,4},{2,6},{4,0},{6,2},{1,5},{3,7},{5,1},{7,3},{8,12},{10,14},{12... | collective-permute-start | bytes 307208 | tf_op jit(solution)/shard_map/ppermute | solution.py:479
  10.9 6.0 %collective-permute-start.1 = (f32[392,128]{1,0:T(8,128)S(1)}, f32[392,128]{1,0:T(8,128)S(1)}, u32[]{:S(2)}, u32[]{:S(2)}) collective-permute-start(f32[392,128]{1,0:T(8,128)S(1)} %get-tuple-element.39.chip_ref.own_ref), channel_id=1, source_target_pairs={{0,2},{2,4},{4,6},{6,0},{1,7},{3,1},{5,3},{7,5},{8,10},{10,12},{12... | collective-permute-start | bytes 602120 | tf_op jit(solution)/shard_map/ppermute | solution.py:486
  16.9 3.1 %collective-permute-start.2 = (f32[392,128]{1,0:T(8,128)S(1)}, f32[392,128]{1,0:T(8,128)S(1)}, u32[]{:S(2)}, u32[]{:S(2)}) collective-permute-start(f32[392,128]{1,0:T(8,128)S(1)} %collective-permute-done.1.near), channel_id=1, source_target_pairs={{0,1},{1,0},{2,3},{3,2},{4,5},{5,4},{6,7},{7,6},{8,9},{9,8},{10,11... | collective-permute-start | bytes 602120 | tf_op jit(solution)/shard_map/ppermute | solution.py:479
  18.7 1.3 %collective-permute-start.4 = (f32[200,128]{1,0:T(8,128)S(1)}, f32[200,128]{1,0:T(8,128)S(1)}, u32[]{:S(2)}, u32[]{:S(2)}) collective-permute-start(f32[200,128]{1,0:T(8,128)S(1)} %collective-permute-done.3.two), channel_id=1, source_target_pairs={{0,1},{1,0},{2,3},{3,2},{4,5},{5,4},{6,7},{7,6},{8,9},{9,8},{10,11... | collective-permute-start | bytes 307208 | tf_op jit(solution)/shard_map/ppermute | solution.py:479
  20.9 10.1 %collective-permute-start.7 = (f32[200,128]{1,0:T(8,128)S(1)}, f32[200,128]{1,0:T(8,128)S(1)}, u32[]{:S(2)}, u32[]{:S(2)}) collective-permute-start(f32[200,128]{1,0:T(8,128)S(1)} %get-tuple-element.52), channel_id=1, source_target_pairs={{0,16},{8,24},{16,0},{24,8},{1,17},{9,25},{17,1},{25,9},{2,18},{10... | collective-permute-start | bytes 307208 | tf_op jit(solution)/shard_map/ppermute | solution.py:479
  23.5 5.9 %collective-permute-start.5 = (f32[392,128]{1,0:T(8,128)S(1)}, f32[392,128]{1,0:T(8,128)S(1)}, u32[]{:S(2)}, u32[]{:S(2)}) collective-permute-start(f32[392,128]{1,0:T(8,128)S(1)} %get-tuple-element.47.after_ref), channel_id=1, source_target_pairs={{0,8},{8,16},{16,24},{24,0},{1,25},{9,1},{17,9},{25,17},{2,10},{10... | collective-permute-start | bytes 602120 | tf_op jit(solution)/shard_map/ppermute | solution.py:486
  24.4 7.9 %copy-start = (f32[3,128]{1,0:T(4,128)S(1)}, f32[3,128]{1,0:T(4,128)}, u32[]{:S(2)}) copy-start(f32[3,128]{1,0:T(4,128)} %init_ref.1) | copy-start | bytes 4612
  29.4 2.9 %collective-permute-start.6 = (f32[392,128]{1,0:T(8,128)S(1)}, f32[392,128]{1,0:T(8,128)S(1)}, u32[]{:S(2)}, u32[]{:S(2)}) collective-permute-start(f32[392,128]{1,0:T(8,128)S(1)} %collective-permute-done.5.near), channel_id=1, source_target_pairs={{0,1},{1,0},{2,3},{3,2},{4,5},{5,4},{6,7},{7,6},{8,9},{9,8},{10,11... | collective-permute-start | bytes 602120 | tf_op jit(solution)/shard_map/ppermute | solution.py:479
  31.0 1.3 %collective-permute-start.8 = (f32[200,128]{1,0:T(8,128)S(1)}, f32[200,128]{1,0:T(8,128)S(1)}, u32[]{:S(2)}, u32[]{:S(2)}) collective-permute-start(f32[200,128]{1,0:T(8,128)S(1)} %collective-permute-done.7.two), channel_id=1, source_target_pairs={{0,1},{1,0},{2,3},{3,2},{4,5},{5,4},{6,7},{7,6},{8,9},{9,8},{10,11... | collective-permute-start | bytes 307208 | tf_op jit(solution)/shard_map/ppermute | solution.py:479

commit v4 on v3

--- a/solution.py
+++ b/solution.py
@@ -115,7 +115,7 @@
 
 def k_block(
     flags, sensors_ref, eye_ref, obs_raw, pres_ref, lp_ref, dyn_ref, pv_ref, map_ref,
-    root_ref, dynt_ref, table, nodes, offs, step_ref, u_ref, mask_ref, obs_ref, rows_ref, mask_scr, u_scr,
+    root_ref, dynt_ref, table, nodes, offs, step_ref, twos_ref, u_ref, mask_ref, obs_ref, rows_ref, mask_scr, u_scr,
 ):
     on = on_row(sensors_ref)
     weight = jnp.exp(lp_ref[...]) * on
@@ -140,6 +140,7 @@
     two = mul_exact(stacked(dyn_t, filt_t), lanes(dyn_t, filt_t))
     twos = [two[i * N : (i + 1) * N, j * N : (j + 1) * N] for i in (0, 1) for j in (0, 1)]
     wide = lanes(*twos)
+    twos_ref[...] = pair(wide)
     for i in range(4):
         four = mul_exact(twos[i], wide)
         for j in range(4):
@@ -210,27 +211,19 @@
     )
 
 
-def around(refs, b):
-    near, near_mate, two, two_mate = refs
-    first = lax.axis_index("tm_2") == 0
-    return (
-        chosen(first, near, near_mate, b),
-        in_order(two, two_mate, b),
-        chosen(first, near_mate, near, b),
-    )
-
-
 def then(p, q):
     return joined(pair(p[0]), p[1], pair(q[0]), q[1])
 
 
-def put_both(full_ref, mine_ref, maps):
+def put_all(ref, maps):
+    for b, (matrix, _) in enumerate(maps):
+        put(ref, b, matrix)
+    put_offsets(ref, [off for _, off in maps])
+
+
+def put_halves(ref, maps):
     first = lax.axis_index("tm_2") == 0
-    for b, (matrix, off) in enumerate(maps):
-        put(full_ref, b, matrix)
-        put(mine_ref, b, pick(first, matrix[:HALF], matrix[HALF:]))
-    for ref in (full_ref, mine_ref):
-        put_offsets(ref, [off for _, off in maps])
+    put_all(ref, [(pick(first, m[:HALF], m[HALF:]), off) for m, off in maps])
 
 
 def k_core(own_ref, mate_ref, out_ref, mine_ref):
@@ -240,13 +233,22 @@
         own, mate = own_ref[b], mate_ref[b]
         p, q = pick(first, own, mate), pick(first, mate, own)
         maps.append(then((p[:N], p[N : N + 1]), (q[:N], q[N : N + 1])))
-    put_both(out_ref, mine_ref, maps)
-
-
-def k_total(own_ref, near, near_mate, two, two_mate, out_ref, mine_ref, ahead_ref, maps, offs):
-    me = lax.axis_index("tm_1")
-    for b in range(SEQ):
-        for d, (matrix, off) in enumerate(around((near, near_mate, two, two_mate), b)):
+    put_all(out_ref, maps)
+    put_halves(mine_ref, maps)
+
+
+def k_total(
+    own_ref, near, near_mate, two, two_mate, init_ref, mine_ref, state_ref, ahead_ref, maps, offs
+):
+    me, first = lax.axis_index("tm_1"), lax.axis_index("tm_2") == 0
+    state_ref[...] = jnp.zeros_like(state_ref)
+    for b in range(SEQ):
+        ring = (
+            chosen(first, near, near_mate, b),
+            in_order(two, two_mate, b),
+            chosen(first, near_mate, near, b),
+        )
+        for d, (matrix, off) in enumerate(ring):
             slot = lax.rem(me + 3 - d, 4)
             off = jnp.broadcast_to(off, (8, N))
             maps[slot, b] = matrix
@@ -259,10 +261,15 @@
     for b in range(SEQ):
         p = [(maps[k, b], offs[k, b, 0:1, :]) for k in range(4)]
         ends.append(then(then(p[0], p[1]), then(p[2], p[3])))
-    put_both(out_ref, mine_ref, ends)
-
-
-def k_prefix(chip_ref, flags, table, nodes, offs, pre_ref, preoff_ref):
+        state_ref[b : b + 1, :] = apply_row(init_ref[b : b + 1, :], ends[b][0]) + ends[b][1]
+    put_halves(mine_ref, ends)
+
+
+def k_prefix(flags, table, nodes, offs, step_ref, u_ref, mask_ref, pre_ref, preoff_ref, u2_ref):
+    y = lanes(step_ref[:, 0 : 2 * N], step_ref[:, 3 * N : 5 * N])
+    for i in range(SUB // 2):
+        d = mul_pair(pair(u_ref[2 * i]), y)
+        u2_ref[i] = pick(mask_ref[2 * i + 1] > 0.5, d[:, N:], d[:, :N]) + u_ref[2 * i + 1]
     preoff_ref[...] = jnp.zeros_like(preoff_ref)
     for b in range(SEQ):
         pre_ref[b * LEAVES] = jnp.zeros((N, N), F32)
@@ -324,7 +331,7 @@
     cross_ref[10] = pair(mul_exact(w16, powers[8]))
 
 
-def k_entry(ahead_ref, mate_ref, entry_ref, entryoff_ref):
+def k_entry(after_ref, ahead_ref, mate_ref, entry_ref, entryoff_ref):
     me, second = lax.axis_index("tm_1"), lax.axis_index("tm_2") == 1
     entryoff_ref[...] = jnp.zeros_like(entryoff_ref)
     for b in range(SEQ):
@@ -340,27 +347,28 @@
 
 
 def k_tables(
-    after_ref, eye_ref, dyn_ref, dynt_ref, ahead_ref, mate_ref,
-    near_ref, far_ref, reach_ref, cross_ref, resid_ref, entry_ref, entryoff_ref,
+    after_ref, flags, table, nodes, offs, step_ref, u_ref, mask_ref, eye_ref, dyn_ref, dynt_ref,
+    pre_ref, preoff_ref, u2_ref, near_ref, far_ref, reach_ref, cross_ref, resid_ref,
 ):
-    k_entry(ahead_ref, mate_ref, entry_ref, entryoff_ref)
+    k_prefix(flags, table, nodes, offs, step_ref, u_ref, mask_ref, pre_ref, preoff_ref, u2_ref)
     k_powers(eye_ref, dyn_ref, dynt_ref, near_ref, far_ref, reach_ref, cross_ref, resid_ref)
 
 
 def k_filter(
-    near, near_mate, two, two_mate, entry_ref, entryoff_ref, init_ref, obs_ref,
-    rows_ref, dynt_ref, pre_ref, preoff_ref, step_ref, u_ref, mask_ref, reach_ref,
+    one, one_mate, two, two_mate, sent, sent_mate, entry_ref, entryoff_ref, init_ref, obs_ref,
+    rows_ref, dynt_ref, pre_ref, preoff_ref, step_ref, twos_ref, u_ref, u2_ref, mask_ref, reach_ref,
     resid_ref, cross_ref, send_ref, local_ref, suffix_ref, final_ref,
 ):
-    group = lax.axis_index("tm_0")
+    group, core = lax.axis_index("tm_0"), lax.axis_index("tm_2")
+    direct = ((group == 2) & (core == 0)) | ((group == 3) & (core == 1))
     last = (group == 3) & (lax.axis_index("tm_1") == 3) & (lax.axis_index("tm_2") == 1)
     starts = []
     for b in range(SEQ):
-        row = init_ref[b : b + 1, :]
-        ahead = around((near, near_mate, two, two_mate), b)
-        for d in (3, 2, 1):
-            matrix, off = ahead[d - 1]
-            row = pick(group >= d, apply_row(row, matrix) + off, row)
+        row = pick(direct, sent[b : b + 1, :], sent_mate[b : b + 1, :])
+        row = pick(group >= 2, row, init_ref[b : b + 1, :])
+        for flag, mine, mate in ((group == 3, two, two_mate), (group >= 1, one, one_mate)):
+            matrix, off = in_order(mine, mate, b)
+            row = pick(flag, apply_row(row, matrix) + off, row)
         starts.append(apply_row(row, entry_ref[b]) + entryoff_ref[b : b + 1, :])
     rows = []
     for b in range(SEQ):
@@ -377,17 +385,28 @@
     square = jnp.zeros((ROWS, N), F32)
     seen = jnp.zeros((ROWS, N), F32)
     sums = [None] * SUB
-    for i in range(SUB):
-        d = mul_pair(pair(state), step)
-        mask = mask_ref[i]
-        error = obs_ref[i] - d[:, 2 * N :]
-        square = square + mask * (error * error)
-        seen = seen + mask
-        state = pick(mask > 0.5, d[:, N : 2 * N], d[:, :N]) + u_ref[i]
+    out_pair = lanes(step[:, 2 * N : 3 * N], step[:, 5 * N : 6 * N])
+    for i in range(0, SUB, 2):
         x = pair(state)
-        for k in range(i + 1):
-            add = mul_pair(x, resid_ref[i - k])
-            sums[k] = add if k == i else sums[k] + add
+        d = mul_pair(x, step)
+        q = mul_pair(x, twos_ref[...])
+        m1, m2 = mask_ref[i], mask_ref[i + 1]
+        on1, on2 = m1 > 0.5, m2 > 0.5
+        middle = pick(on1, d[:, N : 2 * N], d[:, :N]) + u_ref[i]
+        state = u2_ref[i // 2] + pick(
+            on1,
+            pick(on2, q[:, 3 * N :], q[:, 2 * N : 3 * N]),
+            pick(on2, q[:, N : 2 * N], q[:, :N]),
+        )
+        x1 = pair(middle)
+        e1 = obs_ref[i] - d[:, 2 * N :]
+        e2 = obs_ref[i + 1] - mul_pair(x1, out_pair)
+        square = square + m1 * (e1 * e1) + m2 * (e2 * e2)
+        seen = seen + m1 + m2
+        for j, x in ((i, x1), (i + 1, pair(state))):
+            for k in range(j + 1):
+                add = mul_pair(x, resid_ref[j - k])
+                sums[k] = add if k == j else sums[k] + add
     square = jnp.sum(square, axis=0, keepdims=True) * weight
     seen = jnp.sum(seen, axis=0, keepdims=True)
     ends = stacked(*(state[(b + 1) * LEAVES - 1 : (b + 1) * LEAVES, :] for b in range(SEQ)))
@@ -479,14 +498,13 @@
     return lax.ppermute(a, axis, [(i, (i + by) % count) for i in range(count)])
 
 
-def exchanged(full, mine, axis, work):
-    ring = [(2 * i, (2 * i + 2) % 8) for i in range(4)] + [
-        (2 * i + 1, (2 * i + 7) % 8) for i in range(4)
-    ]
-    got = [lax.ppermute(full, (axis, "tm_2"), ring), shifted(mine, axis, 2)]
-    done = work(full)
-    swaps = [shifted(lax.optimization_barrier((a, done[-1]))[0], "tm_2", 1) for a in got]
-    return (got[0], swaps[0], got[1], swaps[1]), done
+def swapped(a, *done):
+    return shifted(lax.optimization_barrier((a, done))[0], "tm_2", 1)
+
+
+RING = [(2 * i, (2 * i + 2) % 8) for i in range(4)] + [(2 * i + 1, (2 * i + 7) % 8) for i in range(4)]
+SKIP = [(2, 6), (3, 7), (6, 2), (7, 3), (0, 1), (1, 0), (4, 5), (5, 4)]
+FIRST = [(0, 4), (1, 7), (4, 0), (7, 1), (2, 3), (3, 2), (5, 6), (6, 5)]
 
 
 def local(obs, present, sensors, log_prec, dynamics, prior_var, obs_map, init_state):
@@ -495,7 +513,7 @@
     square = out((N, N))
     square = out((N, N))
     eye = call(k_first, "k_first", [], square, (), 4 * 10**9, 10**7)()
-    root, dyn_t, table, nodes, offs, step, u, mask, obs_s, rows = call(
+    root, dyn_t, table, nodes, offs, step, twos, u, mask, obs_s, rows = call(
         k_block,
         "k_block",
         [SM] * 2 + [VM] * 7,
@@ -506,6 +524,7 @@
             out((42, N, 2 * N), BF16),
             out((96, N)),
             out((N, 6 * N), BF16),
+            out((N, 8 * N), BF16),
             out((SUB, ROWS, N)),
             out((SUB, ROWS, N)),
             out((SUB, ROWS, N)),
@@ -517,57 +536,56 @@
     )(present, sensors, eye, obs, present, lp, dynamics, pv, obs_map)
     mate = shifted(root, "tm_2", 1)
     chip, mine = call(k_core, "k_core", [VM] * 2, both, (), 10**7, 10**6)(root, mate)
-    prefix = call(
-        k_prefix,
-        "k_prefix",
-        [VM, SM] + [VM] * 3,
-        (out((ROWS, N, N)), out((ROWS, N))),
-        (),
-        3 * 10**9,
-        10**7,
-    )
-    got, (pre, preoff) = exchanged(
-        chip, mine, "tm_1", lambda a: prefix(a, present, table, nodes, offs)
-    )
-    group, mine, ahead = call(
-        k_total,
-        "k_total",
-        [VM] * 5,
-        (*both, out((3, SEQ, N + 8, N))),
-        [pltpu.VMEM((4, SEQ, N, N), F32), pltpu.VMEM((4, SEQ, 8, N), F32)],
-        10**8,
-        10**6,
-    )(chip, *got)
-    tables = call(
+    near = lax.ppermute(chip, ("tm_1", "tm_2"), RING)
+    two = shifted(mine, "tm_1", 2)
+    pre, preoff, u2, step_near, far, reach, cross, resid = call(
         k_tables,
         "k_tables",
-        [VM] * 6,
+        [VM, SM] + [VM] * 9,
         (
+            out((ROWS, N, N)),
+            out((ROWS, N)),
+            out((SUB // 2, ROWS, N)),
             out((SUB, N, 2 * N), BF16),
             out((LEAVES, N, N)),
             out((len(REACH), N, 2 * N), BF16),
             out((11, N, 2 * N), BF16),
             out((SUB, N, 2 * N), BF16),
-            out((SEQ, N, N)),
-            out((8, N)),
         ),
         (),
         4 * 10**9,
         10**7,
-    )
-    got, (near, far, reach, cross, resid, entry, entryoff) = exchanged(
-        group, mine, "tm_0", lambda a: tables(a, eye, dynamics, dyn_t, ahead, mate)
+    )(chip, present, table, nodes, offs, step, u, mask, eye, dynamics, dyn_t)
+    got = near, swapped(near, resid), two, swapped(two, resid)
+    mine, state, ahead = call(
+        k_total,
+        "k_total",
+        [VM] * 6,
+        (out((PART, N)), out((8, N)), out((3, SEQ, N + 8, N))),
+        [pltpu.VMEM((4, SEQ, N, N), F32), pltpu.VMEM((4, SEQ, 8, N), F32)],
+        10**8,
+        10**6,
+    )(chip, *got, init_state)
+    one = shifted(mine, "tm_0", 1)
+    two = lax.ppermute(mine, ("tm_0", "tm_2"), SKIP)
+    sent = lax.ppermute(state, ("tm_0", "tm_2"), FIRST)
+    entry, entryoff = call(
+        k_entry, "k_entry", [VM] * 3, (out((SEQ, N, N)), out((8, N))), (), 4 * 10**9, 10**7
+    )(mine, ahead, mate)
+    got = (
+        one, swapped(one, entryoff, sent), two, swapped(two, entryoff, sent),
+        sent, swapped(sent, entryoff),
     )
     send, near_sums, suffix, final = call(
         k_filter,
         "k_filter",
-        [VM] * 18,
+        [VM] * 22,
         (out((BLOCKS, 8, N)), out((SUB, ROWS, N)), out((ROWS, N)), out((8, N))),
         (),
         10**7,
         10**6,
     )(
-        *got, entry, entryoff, init_state, obs_s, rows, dyn_t, pre, preoff, step, u,
+        *got, entry, entryoff, init_state, obs_s, rows, dyn_t, pre, preoff, step, twos, u, u2,
         mask, reach, resid, cross,
     )
     got = lax.all_to_all(send, TM, 0, 0, tiled=True)
@@ -579,7 +597,7 @@
         (),
         10**7,
         10**6,
-    )(got, near_sums, suffix, final, rows, far, near, cross)
+    )(got, near_sums, suffix, final, rows, far, step_near, cross)
     return smoothed, prec.reshape(N), lik[0, :1]
 
 

time: 47.9 us -> 46.9 us (0.979)
  waiting for transfers between devices: 8.84 us -> 6.79 us
  starting transfers between devices: 12.3 us -> 13.1 us
    ppermute x2 -> x3, waiting for transfers between devices: 5.13 us -> 3.46 us  [the longest x1 2.31 us: local(): sent = lax.ppermute(state, ('tm_0', 'tm_2'), FIRST)]
    ppermute x7 -> x8, starting transfers between devices: 10.6 us -> 11.4 us  [shifted(): return lax.ppermute(a, axis, [(i, (i + by) % count) for i in range(count)])]
    ppermute x7 -> x8, waiting for transfers between devices: 3.7 us -> 3.33 us  [shifted(): return lax.ppermute(a, axis, [(i, (i + by) % count) for i in range(count)])]
    ppermute x2 -> x3, starting transfers between devices: 1.65 us -> 1.68 us  [the longest x1 0.76 us: local(): near = lax.ppermute(chip, ('tm_1', 'tm_2'), RING)]
  transfers between devices with their start and end apart: 9 -> 11, of which waited for: 5 -> 5; matrix products, arithmetic and copies ran while one was open for 0% -> 0% of each run, Pallas kernels for 11% -> 11%
where the time goes in v4:
time: 46.9 us; the launch traced here: 46.8 us
  starting transfers between devices  13.1 us (28%)
  Pallas kernels  13 us (28%)
  blocking collectives  12.3 us (26%)
  waiting for transfers between devices  6.79 us (14%)
  between operations  1.48 us (3%)
    all_to_all x1, blocking collectives, local(): got = lax.all_to_all(send, TM, 0, 0, tiled=True)  12.3 us
    ppermute x8, starting transfers between devices, shifted(): return lax.ppermute(a, axis, [(i, (i + by) % count) for i in range(count)])  11.4 us
    pallas_call x1, Pallas kernels, local(): call(k_tables, 'k_tables', [VM, SM] + [VM] * 9, (out((ROWS, N, N)), out((...  4.07 us
    pallas_call x1, Pallas kernels, local(): call(k_block, 'k_block', [SM] * 2 + [VM] * 7, (out((SEQ, N + 8, N)), squa...  3.33 us
    ppermute x8, waiting for transfers between devices, shifted(): return lax.ppermute(a, axis, [(i, (i + by) % count) for i in range(count)])  3.33 us
    ppermute x1, waiting for transfers between devices, local(): sent = lax.ppermute(state, ('tm_0', 'tm_2'), FIRST)  2.31 us
    pallas_call x1, Pallas kernels, local(): call(k_filter, 'k_filter', [VM] * 22, (out((BLOCKS, 8, N)), out((SUB, ROW...  1.71 us
    pallas_call x1, Pallas kernels, local(): call(k_smooth, 'k_smooth', [VM] * 8, (out((SEQ, STEPS, N)), out((1, N)),...  1.59 us
  transfers between devices with their start and end apart: 11, of which 5 were waited for; matrix products, arithmetic and copies ran while one was open for 0% of the time, Pallas kernels for 11%

profile of v4, /device:TPU:1, one launch (start us, length us, event | category | flops | bytes accessed | tf_op | source)
XLA Modules:
  0.0 46.8 jit_solution(9333808167927276313)
XLA Ops:
  1.5 0.0 copy-done.3
  1.5 0.0 copy-done.2
  1.5 0.1 copy-done.1
  1.6 3.3 %k_block.1 = (f32[3,136,128]{2,1,0:T(8,128)S(1)}, f32[128,128]{1,0:T(8,128)S(1)}, bf16[16,128,256]{2,1,0:T(8,128)(2,1)S(1)}, bf16[42,128,256]{2,1,0:T(8,128)(2,1...) custom-call(s32[3,64]{1,0:T(4,128)S(1)} %copy-done.4, ...), custom_call_target="tpu_custom_call" | custom-call | flops 1000000000 | bytes 1000000 | tf_op jit(solution)/shard_map/k_block/pallas_call | solution.py:516
  5.0 3.3 %collective-permute-start = (f32[3,136,128]{2,1,0:T(8,128)S(1)}, f32[3,136,128]{2,1,0:T(8,128)S(1)}, u32[]{:S(2)}, u32[]{:S(2)}) collective-permute-start(f32[3,136,128]{2,1,0:T(8,128)S(1)} %get-tuple-element.41.own_ref), channel_id=1, source_target_pairs={{0,1},{1,0},{2,3},{3,2},{4,5},{5,4},{6,7},{7,6},{8,9},{9,8},{10,11... | collective-permute-start | bytes 626696 | tf_op jit(solution)/shard_map/ppermute | solution.py:498
  8.3 1.1 %collective-permute-done.mate_ref = f32[3,136,128]{2,1,0:T(8,128)S(1)} collective-permute-done((f32[3,136,128]{2,1,0:T(8,128)S(1)}, f32[3,136,128]{2,1,0:T(8,128)S(1)}, u32[]{:S(2)}, u32[]{:S(2)}) %collective-permute-start) | collective-permute-done | bytes 208928 | tf_op jit(solution)/shard_map/ppermute | solution.py:498
  9.4 0.2 k_core.1
  9.6 1.3 %collective-permute-start.3 = (f32[200,128]{1,0:T(8,128)S(1)}, f32[200,128]{1,0:T(8,128)S(1)}, u32[]{:S(2)}, u32[]{:S(2)}) collective-permute-start(f32[200,128]{1,0:T(8,128)S(1)} %get-tuple-element.52), channel_id=1, source_target_pairs={{0,4},{2,6},{4,0},{6,2},{1,5},{3,7},{5,1},{7,3},{8,12},{10,14},{12... | collective-permute-start | bytes 307208 | tf_op jit(solution)/shard_map/ppermute | solution.py:498
  10.9 0.8 %collective-permute-start.1 = (f32[392,128]{1,0:T(8,128)S(1)}, f32[392,128]{1,0:T(8,128)S(1)}, u32[]{:S(2)}, u32[]{:S(2)}) collective-permute-start(f32[392,128]{1,0:T(8,128)S(1)} %get-tuple-element.42.after_ref.own_ref), channel_id=1, source_target_pairs={{0,2},{2,4},{4,6},{6,0},{1,7},{3,1},{5,3},{7,5},{8,10},{10,12},{12... | collective-permute-start | bytes 602120 | tf_op jit(solution)/shard_map/ppermute | solution.py:539
  11.7 4.1 %k_tables.1 = (f32[48,128,128]{2,1,0:T(8,128)S(1)}, f32[48,128]{1,0:T(8,128)S(1)}, f32[2,48,128]{2,1,0:T(8,128)S(1)}, bf16[4,128,256]{2,1,0:T(8,128)(2,1)S(1)}, ...) custom-call(f32[392,128]{1,0:T(8,128)S(1)} %get-tuple-element.42.aft, ...), custom_call_target="tpu_custom_call" | custom-call | flops 4000000000 | bytes 10000000 | tf_op jit(solution)/shard_map/k_tables/pallas_call | solution.py:541
  15.7 1.1 %collective-permute-done.1.near = f32[392,128]{1,0:T(8,128)S(1)} collective-permute-done((f32[392,128]{1,0:T(8,128)S(1)}, f32[392,128]{1,0:T(8,128)S(1)}, u32[]{:S(2)}, u32[]{:S(2)}) %collective-permute-start.1) | collective-permute-done | bytes 200736 | tf_op jit(solution)/shard_map/ppermute | solution.py:539
  16.9 1.8 %collective-permute-start.2 = (f32[392,128]{1,0:T(8,128)S(1)}, f32[392,128]{1,0:T(8,128)S(1)}, u32[]{:S(2)}, u32[]{:S(2)}) collective-permute-start(f32[392,128]{1,0:T(8,128)S(1)} %collective-permute-done.1.near), channel_id=1, source_target_pairs={{0,1},{1,0},{2,3},{3,2},{4,5},{5,4},{6,7},{7,6},{8,9},{9,8},{10,11... | collective-permute-start | bytes 602120 | tf_op jit(solution)/shard_map/ppermute | solution.py:498
  18.7 0.0 collective-permute-done.3.two
  18.7 0.0 collective-permute-start.4
  18.7 1.3 %collective-permute-done.4.two_mate = f32[200,128]{1,0:T(8,128)S(1)} collective-permute-done((f32[200,128]{1,0:T(8,128)S(1)}, f32[200,128]{1,0:T(8,128)S(1)}, u32[]{:S(2)}, u32[]{:S(2)}) %collective-permute-start.4) | collective-permute-done | bytes 102432 | tf_op jit(solution)/shard_map/ppermute | solution.py:498
  20.0 0.0 collective-permute-done.2.near_mate
  20.0 0.9 %k_total.1 = (f32[200,128]{1,0:T(8,128)S(1)}, f32[8,128]{1,0:T(8,128)S(1)}, f32[3,3,136,128]{3,2,1,0:T(8,128)S(1)}) custom-call(f32[392,128]{1,0:T(8,128)S(1)} %get-tuple-element.42.after_ref.own_ref, f32[392,128]{1,0:T(8,128)S(1)} %collective-permute-done.1.near, f32[392,128]{1,0:T(8,128)S(1)} %collective-permute-done.2.near_mate, ...), custom_call_target="tpu_custom_call" | custom-call | flops 100000000 | bytes 1000000 | tf_op jit(solution)/shard_map/k_total/pallas_call | solution.py:560
  20.9 0.4 collective-permute-start.8
  21.2 2.6 %collective-permute-start.5 = (f32[200,128]{1,0:T(8,128)S(1)}, f32[200,128]{1,0:T(8,128)S(1)}, u32[]{:S(2)}, u32[]{:S(2)}) collective-permute-start(f32[200,128]{1,0:T(8,128)S(1)} %get-tuple-element.54.after_ref), channel_id=1, source_target_pairs={{0,8},{8,16},{16,24},{24,0},{1,9},{9,17},{17,25},{25,1},{2,10},{10... | collective-permute-start | bytes 307208 | tf_op jit(solution)/shard_map/ppermute | solution.py:498
  23.8 0.5 %collective-permute-start.6 = (f32[8,128]{1,0:T(8,128)S(1)}, f32[8,128]{1,0:T(8,128)S(1)}, u32[]{:S(2)}, u32[]{:S(2)}) collective-permute-start(f32[8,128]{1,0:T(8,128)S(1)} %get-tuple-element.57), channel_id=1, source_target_pairs={{0,16},{1,25},{16,0},{25,1},{8,9},{9,8},{17,24},{24,17},{2,18},{3,... | collective-permute-start | bytes 12296 | tf_op jit(solution)/shard_map/ppermute | solution.py:571
  24.4 1.1 %k_entry.1 = (f32[3,128,128]{2,1,0:T(8,128)S(1)}, f32[8,128]{1,0:T(8,128)S(1)}) custom-call(f32[200,128]{1,0:T(8,128)S(1)} %get-tuple-element.54.after_ref, f32[3,3,136,128]{3,2,1,0:T(8,128)S(1)} %get-tuple-element.55.ahead_ref, f32[3,136,128]{2,1,0:T(8,128)S(1)} %collective-permute-done.mate_ref), custom_call_target="tpu_custom_call" | custom-call | flops 4000000000 | bytes 10000000 | tf_op jit(solution)/shard_map/k_entry/pallas_call | solution.py:572
  25.5 2.3 %collective-permute-done.6.sent = f32[8,128]{1,0:T(8,128)S(1)} collective-permute-done((f32[8,128]{1,0:T(8,128)S(1)}, f32[8,128]{1,0:T(8,128)S(1)}, u32[]{:S(2)}, u32[]{:S(2)}) %collective-permute-start.6) | collective-permute-done | bytes 4128 | tf_op jit(solution)/shard_map/ppermute | solution.py:571
  27.8 0.0 collective-permute-done.8.two
  27.8 2.0 %collective-permute-start.9 = (f32[200,128]{1,0:T(8,128)S(1)}, f32[200,128]{1,0:T(8,128)S(1)}, u32[]{:S(2)}, u32[]{:S(2)}) collective-permute-start(f32[200,128]{1,0:T(8,128)S(1)} %collective-permute-done.8.two), channel_id=1, source_target_pairs={{0,1},{1,0},{2,3},{3,2},{4,5},{5,4},{6,7},{7,6},{8,9},{9,8},{10,11... | collective-permute-start | bytes 307208 | tf_op jit(solution)/shard_map/ppermute | solution.py:498
  29.8 0.0 collective-permute-done.5.one
  29.8 0.3 collective-permute-start.7
  30.0 0.2 collective-permute-start.10
  30.3 0.9 %collective-permute-done.10.sent_mate = f32[8,128]{1,0:T(8,128)S(1)} collective-permute-done((f32[8,128]{1,0:T(8,128)S(1)}, f32[8,128]{1,0:T(8,128)S(1)}, u32[]{:S(2)}, u32[]{:S(2)}) %collective-permute-start.10) | collective-permute-done | bytes 4128 | tf_op jit(solution)/shard_map/ppermute | solution.py:498
  31.2 0.0 collective-permute-done.9.two_mate
  31.2 1.7 %k_filter.1 = (f32[32,8,128]{2,1,0:T(8,128)S(1)}, f32[4,48,128]{2,1,0:T(8,128)S(1)}, f32[48,128]{1,0:T(8,128)S(1)}, f32[8,128]{1,0:T(8,128)S(1)}) custom-call(f32[200,128]{1,0:T(8,128)S(1)} %collective-permute-done.5.one, f32[200,128]{1,0:T(8,128)S(1)} %collective-permute-done.7.one_mate, f32[200,128]{1,0:T(8,128)S(1)} %collective-permute-done.8.two, ...), custom_call_target="tpu_custom_call" | custom-call | flops 10000000 | bytes 1000000 | tf_op jit(solution)/shard_map/k_filter/pallas_call | solution.py:579
  32.9 12.3 %all_to_all.5.got_ref = f32[32,8,128]{2,1,0:T(8,128)S(1)} all-to-all(f32[32,8,128]{2,1,0:T(8,128)S(1)} %get-tuple-element.70), channel_id=1, replica_groups=mesh['cluster'=8,'tm_0'=4,'tm_1'=4,'tm_2'=2] {'tm_0','tm_1','tm_2'}, dimensions={0} | all-to-all | bytes 262144 | tf_op jit(solution)/shard_map/all_to_all | solution.py:591
  45.2 1.6 %k_smooth.1 = (f32[3,64,128]{2,1,0:T(8,128)}, f32[1,128]{1,0:T(1,128)}, f32[1,128]{1,0:T(1,128)}) custom-call(f32[32,8,128]{2,1,0:T(8,128)S(1)} %all_to_all.5.got_ref, f32[4,48,128]{2,1,0:T(8,128)S(1)} %get-tuple-element.71.local_ref, f32[48,128]{1,0:T(8,128)S(1)} %get-tuple-element.72.suffix_ref, f32[8,128]{1,0:T(8,128)S(1)} %get-tuple-element.73.final_ref, ...), custom_call_target="tpu_custom_call" | custom-call | flops 10000000 | bytes 1000000 | tf_op jit(solution)/shard_map/k_smooth/pallas_call | solution.py:592
  (13 shorter events, 0.0 us)
Async XLA Ops:
  0.6 0.8 %copy-start.5 = (f32[128]{0:T(128)S(1)}, f32[128]{0:T(128)}, u32[]{:S(2)}) copy-start(f32[128]{0:T(128)} %param.11) | copy-start | bytes 1540
  0.6 0.8 %copy-start.6 = (f32[128]{0:T(128)S(1)}, f32[128]{0:T(128)}, u32[]{:S(2)}) copy-start(f32[128]{0:T(128)} %param.13) | copy-start | bytes 1540
  0.7 0.9 %copy-start.3 = (f32[128,128]{1,0:T(8,128)S(1)}, f32[128,128]{1,0:T(8,128)}, u32[]{:S(2)}) copy-start(f32[128,128]{1,0:T(8,128)} %dyn_ref.3) | copy-start | bytes 196612
  0.7 0.9 %copy-start.2 = (f32[128,128]{1,0:T(8,128)S(1)}, f32[128,128]{1,0:T(8,128)}, u32[]{:S(2)}) copy-start(f32[128,128]{1,0:T(8,128)} %map_ref.1) | copy-start | bytes 196612
  0.7 1.0 %copy-start.1 = (f32[3,64,128]{2,1,0:T(8,128)S(1)}, f32[3,64,128]{2,1,0:T(8,128)}, u32[]{:S(2)}) copy-start(f32[3,64,128]{2,1,0:T(8,128)} %obs_raw.1) | copy-start | bytes 294916
  0.7 1.0 %copy-start.4 = (s32[3,64]{1,0:T(4,128)S(1)}, s32[3,64]{1,0:T(4,128)}, u32[]{:S(2)}) copy-start(s32[3,64]{1,0:T(4,128)} %flags.3) | copy-start | bytes 2308
  5.0 4.4 %collective-permute-start = (f32[3,136,128]{2,1,0:T(8,128)S(1)}, f32[3,136,128]{2,1,0:T(8,128)S(1)}, u32[]{:S(2)}, u32[]{:S(2)}) collective-permute-start(f32[3,136,128]{2,1,0:T(8,128)S(1)} %get-tuple-element.41.own_ref), channel_id=1, source_target_pairs={{0,1},{1,0},{2,3},{3,2},{4,5},{5,4},{6,7},{7,6},{8,9},{9,8},{10,11... | collective-permute-start | bytes 626696 | tf_op jit(solution)/shard_map/ppermute | solution.py:498
  9.6 9.0 %collective-permute-start.3 = (f32[200,128]{1,0:T(8,128)S(1)}, f32[200,128]{1,0:T(8,128)S(1)}, u32[]{:S(2)}, u32[]{:S(2)}) collective-permute-start(f32[200,128]{1,0:T(8,128)S(1)} %get-tuple-element.52), channel_id=1, source_target_pairs={{0,4},{2,6},{4,0},{6,2},{1,5},{3,7},{5,1},{7,3},{8,12},{10,14},{12... | collective-permute-start | bytes 307208 | tf_op jit(solution)/shard_map/ppermute | solution.py:498
  10.9 6.0 %collective-permute-start.1 = (f32[392,128]{1,0:T(8,128)S(1)}, f32[392,128]{1,0:T(8,128)S(1)}, u32[]{:S(2)}, u32[]{:S(2)}) collective-permute-start(f32[392,128]{1,0:T(8,128)S(1)} %get-tuple-element.42.after_ref.own_ref), channel_id=1, source_target_pairs={{0,2},{2,4},{4,6},{6,0},{1,7},{3,1},{5,3},{7,5},{8,10},{10,12},{12... | collective-permute-start | bytes 602120 | tf_op jit(solution)/shard_map/ppermute | solution.py:539
  11.7 8.3 %copy-start = (f32[3,128]{1,0:T(4,128)S(1)}, f32[3,128]{1,0:T(4,128)}, u32[]{:S(2)}) copy-start(f32[3,128]{1,0:T(4,128)} %init_ref.3) | copy-start | bytes 4612
  16.9 3.1 %collective-permute-start.2 = (f32[392,128]{1,0:T(8,128)S(1)}, f32[392,128]{1,0:T(8,128)S(1)}, u32[]{:S(2)}, u32[]{:S(2)}) collective-permute-start(f32[392,128]{1,0:T(8,128)S(1)} %collective-permute-done.1.near), channel_id=1, source_target_pairs={{0,1},{1,0},{2,3},{3,2},{4,5},{5,4},{6,7},{7,6},{8,9},{9,8},{10,11... | collective-permute-start | bytes 602120 | tf_op jit(solution)/shard_map/ppermute | solution.py:498
  18.7 1.3 %collective-permute-start.4 = (f32[200,128]{1,0:T(8,128)S(1)}, f32[200,128]{1,0:T(8,128)S(1)}, u32[]{:S(2)}, u32[]{:S(2)}) collective-permute-start(f32[200,128]{1,0:T(8,128)S(1)} %collective-permute-done.3.two), channel_id=1, source_target_pairs={{0,1},{1,0},{2,3},{3,2},{4,5},{5,4},{6,7},{7,6},{8,9},{9,8},{10,11... | collective-permute-start | bytes 307208 | tf_op jit(solution)/shard_map/ppermute | solution.py:498
  20.9 6.9 %collective-permute-start.8 = (f32[200,128]{1,0:T(8,128)S(1)}, f32[200,128]{1,0:T(8,128)S(1)}, u32[]{:S(2)}, u32[]{:S(2)}) collective-permute-start(f32[200,128]{1,0:T(8,128)S(1)} %get-tuple-element.54.after_ref), channel_id=1, source_target_pairs={{8,24},{9,25},{24,8},{25,9},{0,1},{1,0},{16,17},{17,16},{10,26},{1... | collective-permute-start | bytes 307208 | tf_op jit(solution)/shard_map/ppermute | solution.py:570
  21.2 8.5 %collective-permute-start.5 = (f32[200,128]{1,0:T(8,128)S(1)}, f32[200,128]{1,0:T(8,128)S(1)}, u32[]{:S(2)}, u32[]{:S(2)}) collective-permute-start(f32[200,128]{1,0:T(8,128)S(1)} %get-tuple-element.54.after_ref), channel_id=1, source_target_pairs={{0,8},{8,16},{16,24},{24,0},{1,9},{9,17},{17,25},{25,1},{2,10},{10... | collective-permute-start | bytes 307208 | tf_op jit(solution)/shard_map/ppermute | solution.py:498
  23.8 4.0 %collective-permute-start.6 = (f32[8,128]{1,0:T(8,128)S(1)}, f32[8,128]{1,0:T(8,128)S(1)}, u32[]{:S(2)}, u32[]{:S(2)}) collective-permute-start(f32[8,128]{1,0:T(8,128)S(1)} %get-tuple-element.57), channel_id=1, source_target_pairs={{0,16},{1,25},{16,0},{25,1},{8,9},{9,8},{17,24},{24,17},{2,18},{3,... | collective-permute-start | bytes 12296 | tf_op jit(solution)/shard_map/ppermute | solution.py:571
  27.8 3.4 %collective-permute-start.9 = (f32[200,128]{1,0:T(8,128)S(1)}, f32[200,128]{1,0:T(8,128)S(1)}, u32[]{:S(2)}, u32[]{:S(2)}) collective-permute-start(f32[200,128]{1,0:T(8,128)S(1)} %collective-permute-done.8.two), channel_id=1, source_target_pairs={{0,1},{1,0},{2,3},{3,2},{4,5},{5,4},{6,7},{7,6},{8,9},{9,8},{10,11... | collective-permute-start | bytes 307208 | tf_op jit(solution)/shard_map/ppermute | solution.py:498
  29.8 1.4 %collective-permute-start.7 = (f32[200,128]{1,0:T(8,128)S(1)}, f32[200,128]{1,0:T(8,128)S(1)}, u32[]{:S(2)}, u32[]{:S(2)}) collective-permute-start(f32[200,128]{1,0:T(8,128)S(1)} %collective-permute-done.5.one), channel_id=1, source_target_pairs={{0,1},{1,0},{2,3},{3,2},{4,5},{5,4},{6,7},{7,6},{8,9},{9,8},{10,11... | collective-permute-start | bytes 307208 | tf_op jit(solution)/shard_map/ppermute | solution.py:498
  30.0 1.2 %collective-permute-start.10 = (f32[8,128]{1,0:T(8,128)S(1)}, f32[8,128]{1,0:T(8,128)S(1)}, u32[]{:S(2)}, u32[]{:S(2)}) collective-permute-start(f32[8,128]{1,0:T(8,128)S(1)} %collective-permute-done.6.sent), channel_id=1, source_target_pairs={{0,1},{1,0},{2,3},{3,2},{4,5},{5,4},{6,7},{7,6},{8,9},{9,8},{10,11... | collective-permute-start | bytes 12296 | tf_op jit(solution)/shard_map/ppermute | solution.py:498

commit v5 on v4

--- a/solution.py
+++ b/solution.py
@@ -573,7 +573,7 @@
         k_entry, "k_entry", [VM] * 3, (out((SEQ, N, N)), out((8, N))), (), 4 * 10**9, 10**7
     )(mine, ahead, mate)
     got = (
-        one, swapped(one, entryoff, sent), two, swapped(two, entryoff, sent),
+        one, swapped(one, entryoff, sent), two, swapped(two, entryoff),
         sent, swapped(sent, entryoff),
     )
     send, near_sums, suffix, final = call(

time: 46.9 us -> 46.6 us (level)
  waiting for transfers between devices: 6.79 us -> 4.72 us
  starting transfers between devices: 13.1 us -> 14.9 us
    ppermute x1, waiting for transfers between devices: 2.31 us -> 0.01 us  [local(): sent = lax.ppermute(state, ('tm_0', 'tm_2'), FIRST)]
    ppermute x8, starting transfers between devices: 11.4 us -> 13.2 us  [shifted(): return lax.ppermute(a, axis, [(i, (i + by) % count) for i in range(count)])]
  transfers between devices with their start and end apart: 11 -> 11, of which waited for: 5 -> 4; matrix products, arithmetic and copies ran while one was open for 0% -> 0% of each run, Pallas kernels for 11% -> 11%
where the time goes in v5:
time: 46.6 us; the launch traced here: 46.4 us
  starting transfers between devices  14.9 us (32%)
  Pallas kernels  13 us (28%)
  blocking collectives  12.2 us (26%)
  waiting for transfers between devices  4.72 us (10%)
  between operations  1.49 us (3%)
    ppermute x8, starting transfers between devices, shifted(): return lax.ppermute(a, axis, [(i, (i + by) % count) for i in range(count)])  13.2 us
    all_to_all x1, blocking collectives, local(): got = lax.all_to_all(send, TM, 0, 0, tiled=True)  12.2 us
    pallas_call x1, Pallas kernels, local(): call(k_tables, 'k_tables', [VM, SM] + [VM] * 9, (out((ROWS, N, N)), out((...  4.07 us
    ppermute x8, waiting for transfers between devices, shifted(): return lax.ppermute(a, axis, [(i, (i + by) % count) for i in range(count)])  3.57 us
    pallas_call x1, Pallas kernels, local(): call(k_block, 'k_block', [SM] * 2 + [VM] * 7, (out((SEQ, N + 8, N)), squa...  3.33 us
    pallas_call x1, Pallas kernels, local(): call(k_filter, 'k_filter', [VM] * 22, (out((BLOCKS, 8, N)), out((SUB, ROW...  1.71 us
    pallas_call x1, Pallas kernels, local(): call(k_smooth, 'k_smooth', [VM] * 8, (out((SEQ, STEPS, N)), out((1, N)),...  1.59 us
    ppermute x1, waiting for transfers between devices, local(): near = lax.ppermute(chip, ('tm_1', 'tm_2'), RING)  1.15 us
  transfers between devices with their start and end apart: 11, of which 4 were waited for; matrix products, arithmetic and copies ran while one was open for 0% of the time, Pallas kernels for 11%

profile of v5, /device:TPU:1, one launch (start us, length us, event | category | flops | bytes accessed | tf_op | source)
XLA Modules:
  0.0 46.4 jit_solution(7474607418012260995)
XLA Ops:
  1.5 0.0 copy-done.3
  1.5 0.0 copy-done.2
  1.5 0.1 copy-done.1
  1.6 3.3 %k_block.1 = (f32[3,136,128]{2,1,0:T(8,128)S(1)}, f32[128,128]{1,0:T(8,128)S(1)}, bf16[16,128,256]{2,1,0:T(8,128)(2,1)S(1)}, bf16[42,128,256]{2,1,0:T(8,128)(2,1...) custom-call(s32[3,64]{1,0:T(4,128)S(1)} %copy-done.4, ...), custom_call_target="tpu_custom_call" | custom-call | flops 1000000000 | bytes 1000000 | tf_op jit(solution)/shard_map/k_block/pallas_call | solution.py:516
  5.0 3.3 %collective-permute-start = (f32[3,136,128]{2,1,0:T(8,128)S(1)}, f32[3,136,128]{2,1,0:T(8,128)S(1)}, u32[]{:S(2)}, u32[]{:S(2)}) collective-permute-start(f32[3,136,128]{2,1,0:T(8,128)S(1)} %get-tuple-element.41.own_ref), channel_id=1, source_target_pairs={{0,1},{1,0},{2,3},{3,2},{4,5},{5,4},{6,7},{7,6},{8,9},{9,8},{10,11... | collective-permute-start | bytes 626696 | tf_op jit(solution)/shard_map/ppermute | solution.py:498
  8.3 1.1 %collective-permute-done.mate_ref = f32[3,136,128]{2,1,0:T(8,128)S(1)} collective-permute-done((f32[3,136,128]{2,1,0:T(8,128)S(1)}, f32[3,136,128]{2,1,0:T(8,128)S(1)}, u32[]{:S(2)}, u32[]{:S(2)}) %collective-permute-start) | collective-permute-done | bytes 208928 | tf_op jit(solution)/shard_map/ppermute | solution.py:498
  9.4 0.2 k_core.1
  9.6 1.3 %collective-permute-start.3 = (f32[200,128]{1,0:T(8,128)S(1)}, f32[200,128]{1,0:T(8,128)S(1)}, u32[]{:S(2)}, u32[]{:S(2)}) collective-permute-start(f32[200,128]{1,0:T(8,128)S(1)} %get-tuple-element.52), channel_id=1, source_target_pairs={{0,4},{2,6},{4,0},{6,2},{1,5},{3,7},{5,1},{7,3},{8,12},{10,14},{12... | collective-permute-start | bytes 307208 | tf_op jit(solution)/shard_map/ppermute | solution.py:498
  10.9 0.8 %collective-permute-start.1 = (f32[392,128]{1,0:T(8,128)S(1)}, f32[392,128]{1,0:T(8,128)S(1)}, u32[]{:S(2)}, u32[]{:S(2)}) collective-permute-start(f32[392,128]{1,0:T(8,128)S(1)} %get-tuple-element.42.after_ref.own_ref), channel_id=1, source_target_pairs={{0,2},{2,4},{4,6},{6,0},{1,7},{3,1},{5,3},{7,5},{8,10},{10,12},{12... | collective-permute-start | bytes 602120 | tf_op jit(solution)/shard_map/ppermute | solution.py:539
  11.7 4.1 %k_tables.1 = (f32[48,128,128]{2,1,0:T(8,128)S(1)}, f32[48,128]{1,0:T(8,128)S(1)}, f32[2,48,128]{2,1,0:T(8,128)S(1)}, bf16[4,128,256]{2,1,0:T(8,128)(2,1)S(1)}, ...) custom-call(f32[392,128]{1,0:T(8,128)S(1)} %get-tuple-element.42.aft, ...), custom_call_target="tpu_custom_call" | custom-call | flops 4000000000 | bytes 10000000 | tf_op jit(solution)/shard_map/k_tables/pallas_call | solution.py:541
  15.7 1.1 %collective-permute-done.1.near = f32[392,128]{1,0:T(8,128)S(1)} collective-permute-done((f32[392,128]{1,0:T(8,128)S(1)}, f32[392,128]{1,0:T(8,128)S(1)}, u32[]{:S(2)}, u32[]{:S(2)}) %collective-permute-start.1) | collective-permute-done | bytes 200736 | tf_op jit(solution)/shard_map/ppermute | solution.py:539
  16.9 1.8 %collective-permute-start.2 = (f32[392,128]{1,0:T(8,128)S(1)}, f32[392,128]{1,0:T(8,128)S(1)}, u32[]{:S(2)}, u32[]{:S(2)}) collective-permute-start(f32[392,128]{1,0:T(8,128)S(1)} %collective-permute-done.1.near), channel_id=1, source_target_pairs={{0,1},{1,0},{2,3},{3,2},{4,5},{5,4},{6,7},{7,6},{8,9},{9,8},{10,11... | collective-permute-start | bytes 602120 | tf_op jit(solution)/shard_map/ppermute | solution.py:498
  18.7 0.0 collective-permute-done.3.two
  18.7 0.0 collective-permute-start.4
  18.7 1.3 %collective-permute-done.4.two_mate = f32[200,128]{1,0:T(8,128)S(1)} collective-permute-done((f32[200,128]{1,0:T(8,128)S(1)}, f32[200,128]{1,0:T(8,128)S(1)}, u32[]{:S(2)}, u32[]{:S(2)}) %collective-permute-start.4) | collective-permute-done | bytes 102432 | tf_op jit(solution)/shard_map/ppermute | solution.py:498
  20.0 0.0 collective-permute-done.2.near_mate
  20.0 0.9 %k_total.1 = (f32[200,128]{1,0:T(8,128)S(1)}, f32[8,128]{1,0:T(8,128)S(1)}, f32[3,3,136,128]{3,2,1,0:T(8,128)S(1)}) custom-call(f32[392,128]{1,0:T(8,128)S(1)} %get-tuple-element.42.after_ref.own_ref, f32[392,128]{1,0:T(8,128)S(1)} %collective-permute-done.1.near, f32[392,128]{1,0:T(8,128)S(1)} %collective-permute-done.2.near_mate, ...), custom_call_target="tpu_custom_call" | custom-call | flops 100000000 | bytes 1000000 | tf_op jit(solution)/shard_map/k_total/pallas_call | solution.py:560
  20.9 0.4 collective-permute-start.8
  21.2 2.6 %collective-permute-start.5 = (f32[200,128]{1,0:T(8,128)S(1)}, f32[200,128]{1,0:T(8,128)S(1)}, u32[]{:S(2)}, u32[]{:S(2)}) collective-permute-start(f32[200,128]{1,0:T(8,128)S(1)} %get-tuple-element.54.after_ref), channel_id=1, source_target_pairs={{0,8},{8,16},{16,24},{24,0},{1,9},{9,17},{17,25},{25,1},{2,10},{10... | collective-permute-start | bytes 307208 | tf_op jit(solution)/shard_map/ppermute | solution.py:498
  23.8 0.5 %collective-permute-start.6 = (f32[8,128]{1,0:T(8,128)S(1)}, f32[8,128]{1,0:T(8,128)S(1)}, u32[]{:S(2)}, u32[]{:S(2)}) collective-permute-start(f32[8,128]{1,0:T(8,128)S(1)} %get-tuple-element.57), channel_id=1, source_target_pairs={{0,16},{1,25},{16,0},{25,1},{8,9},{9,8},{17,24},{24,17},{2,18},{3,... | collective-permute-start | bytes 12296 | tf_op jit(solution)/shard_map/ppermute | solution.py:571
  24.4 1.1 %k_entry.1 = (f32[3,128,128]{2,1,0:T(8,128)S(1)}, f32[8,128]{1,0:T(8,128)S(1)}) custom-call(f32[200,128]{1,0:T(8,128)S(1)} %get-tuple-element.54.after_ref, f32[3,3,136,128]{3,2,1,0:T(8,128)S(1)} %get-tuple-element.55.ahead_ref, f32[3,136,128]{2,1,0:T(8,128)S(1)} %collective-permute-done.mate_ref), custom_call_target="tpu_custom_call" | custom-call | flops 4000000000 | bytes 10000000 | tf_op jit(solution)/shard_map/k_entry/pallas_call | solution.py:572
  25.5 0.0 collective-permute-done.8.two
  25.5 2.4 %collective-permute-start.9 = (f32[200,128]{1,0:T(8,128)S(1)}, f32[200,128]{1,0:T(8,128)S(1)}, u32[]{:S(2)}, u32[]{:S(2)}) collective-permute-start(f32[200,128]{1,0:T(8,128)S(1)} %collective-permute-done.8.two), channel_id=1, source_target_pairs={{0,1},{1,0},{2,3},{3,2},{4,5},{5,4},{6,7},{7,6},{8,9},{9,8},{10,11... | collective-permute-start | bytes 307208 | tf_op jit(solution)/shard_map/ppermute | solution.py:498
  27.9 0.0 collective-permute-done.6.sent
  27.9 0.0 collective-permute-done.5.one
  27.9 1.9 %collective-permute-start.7 = (f32[200,128]{1,0:T(8,128)S(1)}, f32[200,128]{1,0:T(8,128)S(1)}, u32[]{:S(2)}, u32[]{:S(2)}) collective-permute-start(f32[200,128]{1,0:T(8,128)S(1)} %collective-permute-done.5.one), channel_id=1, source_target_pairs={{0,1},{1,0},{2,3},{3,2},{4,5},{5,4},{6,7},{7,6},{8,9},{9,8},{10,11... | collective-permute-start | bytes 307208 | tf_op jit(solution)/shard_map/ppermute | solution.py:498
  29.8 0.0 collective-permute-start.10
  29.8 1.2 %collective-permute-done.10.sent_mate = f32[8,128]{1,0:T(8,128)S(1)} collective-permute-done((f32[8,128]{1,0:T(8,128)S(1)}, f32[8,128]{1,0:T(8,128)S(1)}, u32[]{:S(2)}, u32[]{:S(2)}) %collective-permute-start.10) | collective-permute-done | bytes 4128 | tf_op jit(solution)/shard_map/ppermute | solution.py:498
  30.9 0.0 collective-permute-done.9.two_mate
  30.9 1.7 %k_filter.1 = (f32[32,8,128]{2,1,0:T(8,128)S(1)}, f32[4,48,128]{2,1,0:T(8,128)S(1)}, f32[48,128]{1,0:T(8,128)S(1)}, f32[8,128]{1,0:T(8,128)S(1)}) custom-call(f32[200,128]{1,0:T(8,128)S(1)} %collective-permute-done.5.one, f32[200,128]{1,0:T(8,128)S(1)} %collective-permute-done.7.one_mate, f32[200,128]{1,0:T(8,128)S(1)} %collective-permute-done.8.two, ...), custom_call_target="tpu_custom_call" | custom-call | flops 10000000 | bytes 1000000 | tf_op jit(solution)/shard_map/k_filter/pallas_call | solution.py:579
  32.7 12.2 %all_to_all.5.got_ref = f32[32,8,128]{2,1,0:T(8,128)S(1)} all-to-all(f32[32,8,128]{2,1,0:T(8,128)S(1)} %get-tuple-element.70), channel_id=1, replica_groups=mesh['cluster'=8,'tm_0'=4,'tm_1'=4,'tm_2'=2] {'tm_0','tm_1','tm_2'}, dimensions={0} | all-to-all | bytes 262144 | tf_op jit(solution)/shard_map/all_to_all | solution.py:591
  44.9 1.6 %k_smooth.1 = (f32[3,64,128]{2,1,0:T(8,128)}, f32[1,128]{1,0:T(1,128)}, f32[1,128]{1,0:T(1,128)}) custom-call(f32[32,8,128]{2,1,0:T(8,128)S(1)} %all_to_all.5.got_ref, f32[4,48,128]{2,1,0:T(8,128)S(1)} %get-tuple-element.71.local_ref, f32[48,128]{1,0:T(8,128)S(1)} %get-tuple-element.72.suffix_ref, f32[8,128]{1,0:T(8,128)S(1)} %get-tuple-element.73.final_ref, ...), custom_call_target="tpu_custom_call" | custom-call | flops 10000000 | bytes 1000000 | tf_op jit(solution)/shard_map/k_smooth/pallas_call | solution.py:592
  (13 shorter events, 0.0 us)
Async XLA Ops:
  0.6 0.8 %copy-start.5 = (f32[128]{0:T(128)S(1)}, f32[128]{0:T(128)}, u32[]{:S(2)}) copy-start(f32[128]{0:T(128)} %param.11) | copy-start | bytes 1540
  0.6 0.8 %copy-start.6 = (f32[128]{0:T(128)S(1)}, f32[128]{0:T(128)}, u32[]{:S(2)}) copy-start(f32[128]{0:T(128)} %param.13) | copy-start | bytes 1540
  0.7 0.9 %copy-start.3 = (f32[128,128]{1,0:T(8,128)S(1)}, f32[128,128]{1,0:T(8,128)}, u32[]{:S(2)}) copy-start(f32[128,128]{1,0:T(8,128)} %dyn_ref.3) | copy-start | bytes 196612
  0.7 0.9 %copy-start.2 = (f32[128,128]{1,0:T(8,128)S(1)}, f32[128,128]{1,0:T(8,128)}, u32[]{:S(2)}) copy-start(f32[128,128]{1,0:T(8,128)} %map_ref.1) | copy-start | bytes 196612
  0.7 1.0 %copy-start.1 = (f32[3,64,128]{2,1,0:T(8,128)S(1)}, f32[3,64,128]{2,1,0:T(8,128)}, u32[]{:S(2)}) copy-start(f32[3,64,128]{2,1,0:T(8,128)} %obs_raw.1) | copy-start | bytes 294916
  0.7 1.0 %copy-start.4 = (s32[3,64]{1,0:T(4,128)S(1)}, s32[3,64]{1,0:T(4,128)}, u32[]{:S(2)}) copy-start(s32[3,64]{1,0:T(4,128)} %flags.3) | copy-start | bytes 2308
  5.0 4.4 %collective-permute-start = (f32[3,136,128]{2,1,0:T(8,128)S(1)}, f32[3,136,128]{2,1,0:T(8,128)S(1)}, u32[]{:S(2)}, u32[]{:S(2)}) collective-permute-start(f32[3,136,128]{2,1,0:T(8,128)S(1)} %get-tuple-element.41.own_ref), channel_id=1, source_target_pairs={{0,1},{1,0},{2,3},{3,2},{4,5},{5,4},{6,7},{7,6},{8,9},{9,8},{10,11... | collective-permute-start | bytes 626696 | tf_op jit(solution)/shard_map/ppermute | solution.py:498
  9.6 9.0 %collective-permute-start.3 = (f32[200,128]{1,0:T(8,128)S(1)}, f32[200,128]{1,0:T(8,128)S(1)}, u32[]{:S(2)}, u32[]{:S(2)}) collective-permute-start(f32[200,128]{1,0:T(8,128)S(1)} %get-tuple-element.52), channel_id=1, source_target_pairs={{0,4},{2,6},{4,0},{6,2},{1,5},{3,7},{5,1},{7,3},{8,12},{10,14},{12... | collective-permute-start | bytes 307208 | tf_op jit(solution)/shard_map/ppermute | solution.py:498
  10.9 6.0 %collective-permute-start.1 = (f32[392,128]{1,0:T(8,128)S(1)}, f32[392,128]{1,0:T(8,128)S(1)}, u32[]{:S(2)}, u32[]{:S(2)}) collective-permute-start(f32[392,128]{1,0:T(8,128)S(1)} %get-tuple-element.42.after_ref.own_ref), channel_id=1, source_target_pairs={{0,2},{2,4},{4,6},{6,0},{1,7},{3,1},{5,3},{7,5},{8,10},{10,12},{12... | collective-permute-start | bytes 602120 | tf_op jit(solution)/shard_map/ppermute | solution.py:539
  11.7 8.3 %copy-start = (f32[3,128]{1,0:T(4,128)S(1)}, f32[3,128]{1,0:T(4,128)}, u32[]{:S(2)}) copy-start(f32[3,128]{1,0:T(4,128)} %init_ref.3) | copy-start | bytes 4612
  16.9 3.1 %collective-permute-start.2 = (f32[392,128]{1,0:T(8,128)S(1)}, f32[392,128]{1,0:T(8,128)S(1)}, u32[]{:S(2)}, u32[]{:S(2)}) collective-permute-start(f32[392,128]{1,0:T(8,128)S(1)} %collective-permute-done.1.near), channel_id=1, source_target_pairs={{0,1},{1,0},{2,3},{3,2},{4,5},{5,4},{6,7},{7,6},{8,9},{9,8},{10,11... | collective-permute-start | bytes 602120 | tf_op jit(solution)/shard_map/ppermute | solution.py:498
  18.7 1.3 %collective-permute-start.4 = (f32[200,128]{1,0:T(8,128)S(1)}, f32[200,128]{1,0:T(8,128)S(1)}, u32[]{:S(2)}, u32[]{:S(2)}) collective-permute-start(f32[200,128]{1,0:T(8,128)S(1)} %collective-permute-done.3.two), channel_id=1, source_target_pairs={{0,1},{1,0},{2,3},{3,2},{4,5},{5,4},{6,7},{7,6},{8,9},{9,8},{10,11... | collective-permute-start | bytes 307208 | tf_op jit(solution)/shard_map/ppermute | solution.py:498
  20.9 4.6 %collective-permute-start.8 = (f32[200,128]{1,0:T(8,128)S(1)}, f32[200,128]{1,0:T(8,128)S(1)}, u32[]{:S(2)}, u32[]{:S(2)}) collective-permute-start(f32[200,128]{1,0:T(8,128)S(1)} %get-tuple-element.54.after_ref), channel_id=1, source_target_pairs={{8,24},{9,25},{24,8},{25,9},{0,1},{1,0},{16,17},{17,16},{10,26},{1... | collective-permute-start | bytes 307208 | tf_op jit(solution)/shard_map/ppermute | solution.py:570
  21.2 6.7 %collective-permute-start.5 = (f32[200,128]{1,0:T(8,128)S(1)}, f32[200,128]{1,0:T(8,128)S(1)}, u32[]{:S(2)}, u32[]{:S(2)}) collective-permute-start(f32[200,128]{1,0:T(8,128)S(1)} %get-tuple-element.54.after_ref), channel_id=1, source_target_pairs={{0,8},{8,16},{16,24},{24,0},{1,9},{9,17},{17,25},{25,1},{2,10},{10... | collective-permute-start | bytes 307208 | tf_op jit(solution)/shard_map/ppermute | solution.py:498
  23.8 4.1 %collective-permute-start.6 = (f32[8,128]{1,0:T(8,128)S(1)}, f32[8,128]{1,0:T(8,128)S(1)}, u32[]{:S(2)}, u32[]{:S(2)}) collective-permute-start(f32[8,128]{1,0:T(8,128)S(1)} %get-tuple-element.57), channel_id=1, source_target_pairs={{0,16},{1,25},{16,0},{25,1},{8,9},{9,8},{17,24},{24,17},{2,18},{3,... | collective-permute-start | bytes 12296 | tf_op jit(solution)/shard_map/ppermute | solution.py:571
  25.5 5.4 %collective-permute-start.9 = (f32[200,128]{1,0:T(8,128)S(1)}, f32[200,128]{1,0:T(8,128)S(1)}, u32[]{:S(2)}, u32[]{:S(2)}) collective-permute-start(f32[200,128]{1,0:T(8,128)S(1)} %collective-permute-done.8.two), channel_id=1, source_target_pairs={{0,1},{1,0},{2,3},{3,2},{4,5},{5,4},{6,7},{7,6},{8,9},{9,8},{10,11... | collective-permute-start | bytes 307208 | tf_op jit(solution)/shard_map/ppermute | solution.py:498
  27.9 3.0 %collective-permute-start.7 = (f32[200,128]{1,0:T(8,128)S(1)}, f32[200,128]{1,0:T(8,128)S(1)}, u32[]{:S(2)}, u32[]{:S(2)}) collective-permute-start(f32[200,128]{1,0:T(8,128)S(1)} %collective-permute-done.5.one), channel_id=1, source_target_pairs={{0,1},{1,0},{2,3},{3,2},{4,5},{5,4},{6,7},{7,6},{8,9},{9,8},{10,11... | collective-permute-start | bytes 307208 | tf_op jit(solution)/shard_map/ppermute | solution.py:498
  29.8 1.2 %collective-permute-start.10 = (f32[8,128]{1,0:T(8,128)S(1)}, f32[8,128]{1,0:T(8,128)S(1)}, u32[]{:S(2)}, u32[]{:S(2)}) collective-permute-start(f32[8,128]{1,0:T(8,128)S(1)} %collective-permute-done.6.sent), channel_id=1, source_target_pairs={{0,1},{1,0},{2,3},{3,2},{4,5},{5,4},{6,7},{7,6},{8,9},{9,8},{10,11... | collective-permute-start | bytes 12296 | tf_op jit(solution)/shard_map/ppermute | solution.py:498

commit v6 on v4

--- a/solution.py
+++ b/solution.py
@@ -211,6 +211,16 @@
     )
 
 
+def around(refs, b):
+    near, near_mate, two, two_mate = refs
+    first = lax.axis_index("tm_2") == 0
+    return (
+        chosen(first, near, near_mate, b),
+        in_order(two, two_mate, b),
+        chosen(first, near_mate, near, b),
+    )
+
+
 def then(p, q):
     return joined(pair(p[0]), p[1], pair(q[0]), q[1])
 
@@ -238,23 +248,16 @@
 
 
 def k_total(
-    own_ref, near, near_mate, two, two_mate, init_ref, mine_ref, state_ref, ahead_ref, maps, offs
+    own_ref, near, near_mate, two, two_mate, init_ref, mine_ref, state_ref, maps, offs
 ):
-    me, first = lax.axis_index("tm_1"), lax.axis_index("tm_2") == 0
+    me = lax.axis_index("tm_1")
     state_ref[...] = jnp.zeros_like(state_ref)
     for b in range(SEQ):
-        ring = (
-            chosen(first, near, near_mate, b),
-            in_order(two, two_mate, b),
-            chosen(first, near_mate, near, b),
-        )
-        for d, (matrix, off) in enumerate(ring):
+        for d, (matrix, off) in enumerate(around((near, near_mate, two, two_mate), b)):
             slot = lax.rem(me + 3 - d, 4)
             off = jnp.broadcast_to(off, (8, N))
             maps[slot, b] = matrix
             offs[slot, b] = off
-            ahead_ref[d, b, 0:N, :] = matrix
-            ahead_ref[d, b, N : N + 8, :] = off
         maps[me, b] = full_of(own_ref, b)
         offs[me, b] = jnp.broadcast_to(offset_of(own_ref, b), (8, N))
     ends = []
@@ -331,16 +334,17 @@
     cross_ref[10] = pair(mul_exact(w16, powers[8]))
 
 
-def k_entry(after_ref, ahead_ref, mate_ref, entry_ref, entryoff_ref):
+def k_entry(after_ref, near, near_mate, two, two_mate, mate_ref, entry_ref, entryoff_ref):
     me, second = lax.axis_index("tm_1"), lax.axis_index("tm_2") == 1
     entryoff_ref[...] = jnp.zeros_like(entryoff_ref)
     for b in range(SEQ):
         so_far = (identity(), jnp.zeros((1, N), F32))
+        ring = around((near, near_mate, two, two_mate), b)
+        mate = mate_ref[b, 0:N, :], mate_ref[b, N : N + 1, :]
         for source, flag in (
-            (ahead_ref.at[2], me >= 3), (ahead_ref.at[1], me >= 2), (ahead_ref.at[0], me >= 1),
-            (mate_ref, second),
+            (ring[2], me >= 3), (ring[1], me >= 2), (ring[0], me >= 1), (mate, second),
         ):
-            got = then(so_far, (source[b, 0:N, :], source[b, N : N + 1, :]))
+            got = then(so_far, source)
             so_far = (pick(flag, got[0], so_far[0]), pick(flag, got[1], so_far[1]))
         entry_ref[b] = so_far[0]
         entryoff_ref[b : b + 1, :] = so_far[1]
@@ -557,11 +561,11 @@
         10**7,
     )(chip, present, table, nodes, offs, step, u, mask, eye, dynamics, dyn_t)
     got = near, swapped(near, resid), two, swapped(two, resid)
-    mine, state, ahead = call(
+    mine, state = call(
         k_total,
         "k_total",
         [VM] * 6,
-        (out((PART, N)), out((8, N)), out((3, SEQ, N + 8, N))),
+        (out((PART, N)), out((8, N))),
         [pltpu.VMEM((4, SEQ, N, N), F32), pltpu.VMEM((4, SEQ, 8, N), F32)],
         10**8,
         10**6,
@@ -570,8 +574,8 @@
     two = lax.ppermute(mine, ("tm_0", "tm_2"), SKIP)
     sent = lax.ppermute(state, ("tm_0", "tm_2"), FIRST)
     entry, entryoff = call(
-        k_entry, "k_entry", [VM] * 3, (out((SEQ, N, N)), out((8, N))), (), 4 * 10**9, 10**7
-    )(mine, ahead, mate)
+        k_entry, "k_entry", [VM] * 6, (out((SEQ, N, N)), out((8, N))), (), 4 * 10**9, 10**7
+    )(mine, *got, mate)
     got = (
         one, swapped(one, entryoff, sent), two, swapped(two, entryoff, sent),
         sent, swapped(sent, entryoff),

time: 46.9 us -> 46.9 us (level)
  no operation moved by 1% of the time
where the time goes in v6:
time: 46.9 us; the launch traced here: 46.8 us
  starting transfers between devices  13.1 us (28%)
  Pallas kernels  13 us (28%)
  blocking collectives  12.3 us (26%)
  waiting for transfers between devices  6.75 us (14%)
  between operations  1.48 us (3%)
    all_to_all x1, blocking collectives, local(): got = lax.all_to_all(send, TM, 0, 0, tiled=True)  12.3 us
    ppermute x8, starting transfers between devices, shifted(): return lax.ppermute(a, axis, [(i, (i + by) % count) for i in range(count)])  11.5 us
    pallas_call x1, Pallas kernels, local(): call(k_tables, 'k_tables', [VM, SM] + [VM] * 9, (out((ROWS, N, N)), out((...  4.08 us
    ppermute x8, waiting for transfers between devices, shifted(): return lax.ppermute(a, axis, [(i, (i + by) % count) for i in range(count)])  3.33 us
    pallas_call x1, Pallas kernels, local(): call(k_block, 'k_block', [SM] * 2 + [VM] * 7, (out((SEQ, N + 8, N)), squa...  3.32 us
    ppermute x1, waiting for transfers between devices, local(): sent = lax.ppermute(state, ('tm_0', 'tm_2'), FIRST)  2.29 us
    pallas_call x1, Pallas kernels, local(): call(k_filter, 'k_filter', [VM] * 22, (out((BLOCKS, 8, N)), out((SUB, ROW...  1.72 us
    pallas_call x1, Pallas kernels, local(): call(k_smooth, 'k_smooth', [VM] * 8, (out((SEQ, STEPS, N)), out((1, N)),...  1.59 us
  transfers between devices with their start and end apart: 11, of which 5 were waited for; matrix products, arithmetic and copies ran while one was open for 0% of the time, Pallas kernels for 11%

profile of v6, /device:TPU:1, one launch (start us, length us, event | category | flops | bytes accessed | tf_op | source)
XLA Modules:
  0.0 46.8 jit_solution(15556094893592423911)
XLA Ops:
  1.5 0.0 copy-done.3
  1.5 0.0 copy-done.2
  1.5 0.1 copy-done.1
  1.6 3.3 %k_block.1 = (f32[3,136,128]{2,1,0:T(8,128)S(1)}, f32[128,128]{1,0:T(8,128)S(1)}, bf16[16,128,256]{2,1,0:T(8,128)(2,1)S(1)}, bf16[42,128,256]{2,1,0:T(8,128)(2,1...) custom-call(s32[3,64]{1,0:T(4,128)S(1)} %copy-done.4, ...), custom_call_target="tpu_custom_call" | custom-call | flops 1000000000 | bytes 1000000 | tf_op jit(solution)/shard_map/k_block/pallas_call | solution.py:520
  5.0 3.3 %collective-permute-start = (f32[3,136,128]{2,1,0:T(8,128)S(1)}, f32[3,136,128]{2,1,0:T(8,128)S(1)}, u32[]{:S(2)}, u32[]{:S(2)}) collective-permute-start(f32[3,136,128]{2,1,0:T(8,128)S(1)} %get-tuple-element.40.own_ref), channel_id=1, source_target_pairs={{0,1},{1,0},{2,3},{3,2},{4,5},{5,4},{6,7},{7,6},{8,9},{9,8},{10,11... | collective-permute-start | bytes 626696 | tf_op jit(solution)/shard_map/ppermute | solution.py:502
  8.3 1.1 %collective-permute-done.mate_ref = f32[3,136,128]{2,1,0:T(8,128)S(1)} collective-permute-done((f32[3,136,128]{2,1,0:T(8,128)S(1)}, f32[3,136,128]{2,1,0:T(8,128)S(1)}, u32[]{:S(2)}, u32[]{:S(2)}) %collective-permute-start) | collective-permute-done | bytes 208928 | tf_op jit(solution)/shard_map/ppermute | solution.py:502
  9.4 0.2 k_core.1
  9.6 1.3 %collective-permute-start.3 = (f32[200,128]{1,0:T(8,128)S(1)}, f32[200,128]{1,0:T(8,128)S(1)}, u32[]{:S(2)}, u32[]{:S(2)}) collective-permute-start(f32[200,128]{1,0:T(8,128)S(1)} %get-tuple-element.51), channel_id=1, source_target_pairs={{0,4},{2,6},{4,0},{6,2},{1,5},{3,7},{5,1},{7,3},{8,12},{10,14},{12... | collective-permute-start | bytes 307208 | tf_op jit(solution)/shard_map/ppermute | solution.py:502
  10.9 0.8 %collective-permute-start.1 = (f32[392,128]{1,0:T(8,128)S(1)}, f32[392,128]{1,0:T(8,128)S(1)}, u32[]{:S(2)}, u32[]{:S(2)}) collective-permute-start(f32[392,128]{1,0:T(8,128)S(1)} %get-tuple-element.41.after_ref.own_ref), channel_id=1, source_target_pairs={{0,2},{2,4},{4,6},{6,0},{1,7},{3,1},{5,3},{7,5},{8,10},{10,12},{12... | collective-permute-start | bytes 602120 | tf_op jit(solution)/shard_map/ppermute | solution.py:543
  11.7 4.1 %k_tables.1 = (f32[48,128,128]{2,1,0:T(8,128)S(1)}, f32[48,128]{1,0:T(8,128)S(1)}, f32[2,48,128]{2,1,0:T(8,128)S(1)}, bf16[4,128,256]{2,1,0:T(8,128)(2,1)S(1)}, ...) custom-call(f32[392,128]{1,0:T(8,128)S(1)} %get-tuple-element.41.aft, ...), custom_call_target="tpu_custom_call" | custom-call | flops 4000000000 | bytes 10000000 | tf_op jit(solution)/shard_map/k_tables/pallas_call | solution.py:545
  15.8 1.1 %collective-permute-done.1.near = f32[392,128]{1,0:T(8,128)S(1)} collective-permute-done((f32[392,128]{1,0:T(8,128)S(1)}, f32[392,128]{1,0:T(8,128)S(1)}, u32[]{:S(2)}, u32[]{:S(2)}) %collective-permute-start.1) | collective-permute-done | bytes 200736 | tf_op jit(solution)/shard_map/ppermute | solution.py:543
  16.9 1.8 %collective-permute-start.2 = (f32[392,128]{1,0:T(8,128)S(1)}, f32[392,128]{1,0:T(8,128)S(1)}, u32[]{:S(2)}, u32[]{:S(2)}) collective-permute-start(f32[392,128]{1,0:T(8,128)S(1)} %collective-permute-done.1.near), channel_id=1, source_target_pairs={{0,1},{1,0},{2,3},{3,2},{4,5},{5,4},{6,7},{7,6},{8,9},{9,8},{10,11... | collective-permute-start | bytes 602120 | tf_op jit(solution)/shard_map/ppermute | solution.py:502
  18.7 0.0 collective-permute-done.3.two
  18.7 0.0 collective-permute-start.4
  18.7 1.3 %collective-permute-done.4.two_mate = f32[200,128]{1,0:T(8,128)S(1)} collective-permute-done((f32[200,128]{1,0:T(8,128)S(1)}, f32[200,128]{1,0:T(8,128)S(1)}, u32[]{:S(2)}, u32[]{:S(2)}) %collective-permute-start.4) | collective-permute-done | bytes 102432 | tf_op jit(solution)/shard_map/ppermute | solution.py:502
  20.0 0.0 collective-permute-done.2.near_mate
  20.0 0.9 %k_total.1 = (f32[200,128]{1,0:T(8,128)S(1)}, f32[8,128]{1,0:T(8,128)S(1)}) custom-call(f32[392,128]{1,0:T(8,128)S(1)} %get-tuple-element.41.after_ref.own_ref, f32[392,128]{1,0:T(8,128)S(1)} %collective-permute-done.1.near, f32[392,128]{1,0:T(8,128)S(1)} %collective-permute-done.2.near_mate, f32[200,128]{1,0:T(8,128)S(1)} %collective-permute-done.3.two, ...), custom_call_target="tpu_custom_call" | custom-call | flops 100000000 | bytes 1000000 | tf_op jit(solution)/shard_map/k_total/pallas_call | solution.py:564
  20.8 0.4 collective-permute-start.8
  21.2 2.6 %collective-permute-start.5 = (f32[200,128]{1,0:T(8,128)S(1)}, f32[200,128]{1,0:T(8,128)S(1)}, u32[]{:S(2)}, u32[]{:S(2)}) collective-permute-start(f32[200,128]{1,0:T(8,128)S(1)} %get-tuple-element.53.after_ref), channel_id=1, source_target_pairs={{0,8},{8,16},{16,24},{24,0},{1,9},{9,17},{17,25},{25,1},{2,10},{10... | collective-permute-start | bytes 307208 | tf_op jit(solution)/shard_map/ppermute | solution.py:502
  23.8 0.5 %collective-permute-start.6 = (f32[8,128]{1,0:T(8,128)S(1)}, f32[8,128]{1,0:T(8,128)S(1)}, u32[]{:S(2)}, u32[]{:S(2)}) collective-permute-start(f32[8,128]{1,0:T(8,128)S(1)} %get-tuple-element.55), channel_id=1, source_target_pairs={{0,16},{1,25},{16,0},{25,1},{8,9},{9,8},{17,24},{24,17},{2,18},{3,... | collective-permute-start | bytes 12296 | tf_op jit(solution)/shard_map/ppermute | solution.py:575
  24.3 1.1 %k_entry.1 = (f32[3,128,128]{2,1,0:T(8,128)S(1)}, f32[8,128]{1,0:T(8,128)S(1)}) custom-call(f32[200,128]{1,0:T(8,128)S(1)} %get-tuple-element.53.after_ref, f32[392,128]{1,0:T(8,128)S(1)} %collective-permute-done.1.near, f32[392,128]{1,0:T(8,128)S(1)} %collective-permute-done.2.near_mate, f32[200,128]{1,0:T(8,128)S(1)} %collective-permute-done.3.two, ...), custom_call_target="tpu_custom_call" | custom-call | flops 4000000000 | bytes 10000000 | tf_op jit(solution)/shard_map/k_entry/pallas_call | solution.py:576
  25.5 2.3 %collective-permute-done.6.sent = f32[8,128]{1,0:T(8,128)S(1)} collective-permute-done((f32[8,128]{1,0:T(8,128)S(1)}, f32[8,128]{1,0:T(8,128)S(1)}, u32[]{:S(2)}, u32[]{:S(2)}) %collective-permute-start.6) | collective-permute-done | bytes 4128 | tf_op jit(solution)/shard_map/ppermute | solution.py:575
  27.8 0.0 collective-permute-done.8.two
  27.8 2.0 %collective-permute-start.9 = (f32[200,128]{1,0:T(8,128)S(1)}, f32[200,128]{1,0:T(8,128)S(1)}, u32[]{:S(2)}, u32[]{:S(2)}) collective-permute-start(f32[200,128]{1,0:T(8,128)S(1)} %collective-permute-done.8.two), channel_id=1, source_target_pairs={{0,1},{1,0},{2,3},{3,2},{4,5},{5,4},{6,7},{7,6},{8,9},{9,8},{10,11... | collective-permute-start | bytes 307208 | tf_op jit(solution)/shard_map/ppermute | solution.py:502
  29.8 0.3 collective-permute-start.7
  30.0 0.2 collective-permute-start.10
  30.3 0.9 %collective-permute-done.10.sent_mate = f32[8,128]{1,0:T(8,128)S(1)} collective-permute-done((f32[8,128]{1,0:T(8,128)S(1)}, f32[8,128]{1,0:T(8,128)S(1)}, u32[]{:S(2)}, u32[]{:S(2)}) %collective-permute-start.10) | collective-permute-done | bytes 4128 | tf_op jit(solution)/shard_map/ppermute | solution.py:502
  31.2 0.0 collective-permute-done.9.two_mate
  31.2 0.0 collective-permute-done.7.one_mate
  31.2 1.7 %k_filter.1 = (f32[32,8,128]{2,1,0:T(8,128)S(1)}, f32[4,48,128]{2,1,0:T(8,128)S(1)}, f32[48,128]{1,0:T(8,128)S(1)}, f32[8,128]{1,0:T(8,128)S(1)}) custom-call(f32[200,128]{1,0:T(8,128)S(1)} %collective-permute-done.5.one, f32[200,128]{1,0:T(8,128)S(1)} %collective-permute-done.7.one_mate, f32[200,128]{1,0:T(8,128)S(1)} %collective-permute-done.8.two, ...), custom_call_target="tpu_custom_call" | custom-call | flops 10000000 | bytes 1000000 | tf_op jit(solution)/shard_map/k_filter/pallas_call | solution.py:583
  32.9 12.3 %all_to_all.5.got_ref = f32[32,8,128]{2,1,0:T(8,128)S(1)} all-to-all(f32[32,8,128]{2,1,0:T(8,128)S(1)} %get-tuple-element.68), channel_id=1, replica_groups=mesh['cluster'=8,'tm_0'=4,'tm_1'=4,'tm_2'=2] {'tm_0','tm_1','tm_2'}, dimensions={0} | all-to-all | bytes 262144 | tf_op jit(solution)/shard_map/all_to_all | solution.py:595
  45.2 1.6 %k_smooth.1 = (f32[3,64,128]{2,1,0:T(8,128)}, f32[1,128]{1,0:T(1,128)}, f32[1,128]{1,0:T(1,128)}) custom-call(f32[32,8,128]{2,1,0:T(8,128)S(1)} %all_to_all.5.got_ref, f32[4,48,128]{2,1,0:T(8,128)S(1)} %get-tuple-element.69.local_ref, f32[48,128]{1,0:T(8,128)S(1)} %get-tuple-element.70.suffix_ref, f32[8,128]{1,0:T(8,128)S(1)} %get-tuple-element.71.final_ref, ...), custom_call_target="tpu_custom_call" | custom-call | flops 10000000 | bytes 1000000 | tf_op jit(solution)/shard_map/k_smooth/pallas_call | solution.py:596
  (13 shorter events, 0.0 us)
Async XLA Ops:
  0.6 0.8 %copy-start.5 = (f32[128]{0:T(128)S(1)}, f32[128]{0:T(128)}, u32[]{:S(2)}) copy-start(f32[128]{0:T(128)} %param.11) | copy-start | bytes 1540
  0.6 0.8 %copy-start.6 = (f32[128]{0:T(128)S(1)}, f32[128]{0:T(128)}, u32[]{:S(2)}) copy-start(f32[128]{0:T(128)} %param.13) | copy-start | bytes 1540
  0.7 0.9 %copy-start.3 = (f32[128,128]{1,0:T(8,128)S(1)}, f32[128,128]{1,0:T(8,128)}, u32[]{:S(2)}) copy-start(f32[128,128]{1,0:T(8,128)} %dyn_ref.3) | copy-start | bytes 196612
  0.7 0.9 %copy-start.2 = (f32[128,128]{1,0:T(8,128)S(1)}, f32[128,128]{1,0:T(8,128)}, u32[]{:S(2)}) copy-start(f32[128,128]{1,0:T(8,128)} %map_ref.1) | copy-start | bytes 196612
  0.7 1.0 %copy-start.1 = (f32[3,64,128]{2,1,0:T(8,128)S(1)}, f32[3,64,128]{2,1,0:T(8,128)}, u32[]{:S(2)}) copy-start(f32[3,64,128]{2,1,0:T(8,128)} %obs_raw.1) | copy-start | bytes 294916
  0.7 1.0 %copy-start.4 = (s32[3,64]{1,0:T(4,128)S(1)}, s32[3,64]{1,0:T(4,128)}, u32[]{:S(2)}) copy-start(s32[3,64]{1,0:T(4,128)} %flags.3) | copy-start | bytes 2308
  5.0 4.4 %collective-permute-start = (f32[3,136,128]{2,1,0:T(8,128)S(1)}, f32[3,136,128]{2,1,0:T(8,128)S(1)}, u32[]{:S(2)}, u32[]{:S(2)}) collective-permute-start(f32[3,136,128]{2,1,0:T(8,128)S(1)} %get-tuple-element.40.own_ref), channel_id=1, source_target_pairs={{0,1},{1,0},{2,3},{3,2},{4,5},{5,4},{6,7},{7,6},{8,9},{9,8},{10,11... | collective-permute-start | bytes 626696 | tf_op jit(solution)/shard_map/ppermute | solution.py:502
  9.6 9.0 %collective-permute-start.3 = (f32[200,128]{1,0:T(8,128)S(1)}, f32[200,128]{1,0:T(8,128)S(1)}, u32[]{:S(2)}, u32[]{:S(2)}) collective-permute-start(f32[200,128]{1,0:T(8,128)S(1)} %get-tuple-element.51), channel_id=1, source_target_pairs={{0,4},{2,6},{4,0},{6,2},{1,5},{3,7},{5,1},{7,3},{8,12},{10,14},{12... | collective-permute-start | bytes 307208 | tf_op jit(solution)/shard_map/ppermute | solution.py:502
  10.9 6.0 %collective-permute-start.1 = (f32[392,128]{1,0:T(8,128)S(1)}, f32[392,128]{1,0:T(8,128)S(1)}, u32[]{:S(2)}, u32[]{:S(2)}) collective-permute-start(f32[392,128]{1,0:T(8,128)S(1)} %get-tuple-element.41.after_ref.own_ref), channel_id=1, source_target_pairs={{0,2},{2,4},{4,6},{6,0},{1,7},{3,1},{5,3},{7,5},{8,10},{10,12},{12... | collective-permute-start | bytes 602120 | tf_op jit(solution)/shard_map/ppermute | solution.py:543
  11.7 8.3 %copy-start = (f32[3,128]{1,0:T(4,128)S(1)}, f32[3,128]{1,0:T(4,128)}, u32[]{:S(2)}) copy-start(f32[3,128]{1,0:T(4,128)} %init_ref.3) | copy-start | bytes 4612
  16.9 3.1 %collective-permute-start.2 = (f32[392,128]{1,0:T(8,128)S(1)}, f32[392,128]{1,0:T(8,128)S(1)}, u32[]{:S(2)}, u32[]{:S(2)}) collective-permute-start(f32[392,128]{1,0:T(8,128)S(1)} %collective-permute-done.1.near), channel_id=1, source_target_pairs={{0,1},{1,0},{2,3},{3,2},{4,5},{5,4},{6,7},{7,6},{8,9},{9,8},{10,11... | collective-permute-start | bytes 602120 | tf_op jit(solution)/shard_map/ppermute | solution.py:502
  18.7 1.3 %collective-permute-start.4 = (f32[200,128]{1,0:T(8,128)S(1)}, f32[200,128]{1,0:T(8,128)S(1)}, u32[]{:S(2)}, u32[]{:S(2)}) collective-permute-start(f32[200,128]{1,0:T(8,128)S(1)} %collective-permute-done.3.two), channel_id=1, source_target_pairs={{0,1},{1,0},{2,3},{3,2},{4,5},{5,4},{6,7},{7,6},{8,9},{9,8},{10,11... | collective-permute-start | bytes 307208 | tf_op jit(solution)/shard_map/ppermute | solution.py:502
  20.8 6.9 %collective-permute-start.8 = (f32[200,128]{1,0:T(8,128)S(1)}, f32[200,128]{1,0:T(8,128)S(1)}, u32[]{:S(2)}, u32[]{:S(2)}) collective-permute-start(f32[200,128]{1,0:T(8,128)S(1)} %get-tuple-element.53.after_ref), channel_id=1, source_target_pairs={{8,24},{9,25},{24,8},{25,9},{0,1},{1,0},{16,17},{17,16},{10,26},{1... | collective-permute-start | bytes 307208 | tf_op jit(solution)/shard_map/ppermute | solution.py:574
  21.2 8.5 %collective-permute-start.5 = (f32[200,128]{1,0:T(8,128)S(1)}, f32[200,128]{1,0:T(8,128)S(1)}, u32[]{:S(2)}, u32[]{:S(2)}) collective-permute-start(f32[200,128]{1,0:T(8,128)S(1)} %get-tuple-element.53.after_ref), channel_id=1, source_target_pairs={{0,8},{8,16},{16,24},{24,0},{1,9},{9,17},{17,25},{25,1},{2,10},{10... | collective-permute-start | bytes 307208 | tf_op jit(solution)/shard_map/ppermute | solution.py:502
  23.8 4.0 %collective-permute-start.6 = (f32[8,128]{1,0:T(8,128)S(1)}, f32[8,128]{1,0:T(8,128)S(1)}, u32[]{:S(2)}, u32[]{:S(2)}) collective-permute-start(f32[8,128]{1,0:T(8,128)S(1)} %get-tuple-element.55), channel_id=1, source_target_pairs={{0,16},{1,25},{16,0},{25,1},{8,9},{9,8},{17,24},{24,17},{2,18},{3,... | collective-permute-start | bytes 12296 | tf_op jit(solution)/shard_map/ppermute | solution.py:575
  27.8 3.4 %collective-permute-start.9 = (f32[200,128]{1,0:T(8,128)S(1)}, f32[200,128]{1,0:T(8,128)S(1)}, u32[]{:S(2)}, u32[]{:S(2)}) collective-permute-start(f32[200,128]{1,0:T(8,128)S(1)} %collective-permute-done.8.two), channel_id=1, source_target_pairs={{0,1},{1,0},{2,3},{3,2},{4,5},{5,4},{6,7},{7,6},{8,9},{9,8},{10,11... | collective-permute-start | bytes 307208 | tf_op jit(solution)/shard_map/ppermute | solution.py:502
  29.8 1.4 %collective-permute-start.7 = (f32[200,128]{1,0:T(8,128)S(1)}, f32[200,128]{1,0:T(8,128)S(1)}, u32[]{:S(2)}, u32[]{:S(2)}) collective-permute-start(f32[200,128]{1,0:T(8,128)S(1)} %collective-permute-done.5.one), channel_id=1, source_target_pairs={{0,1},{1,0},{2,3},{3,2},{4,5},{5,4},{6,7},{7,6},{8,9},{9,8},{10,11... | collective-permute-start | bytes 307208 | tf_op jit(solution)/shard_map/ppermute | solution.py:502
  30.0 1.2 %collective-permute-start.10 = (f32[8,128]{1,0:T(8,128)S(1)}, f32[8,128]{1,0:T(8,128)S(1)}, u32[]{:S(2)}, u32[]{:S(2)}) collective-permute-start(f32[8,128]{1,0:T(8,128)S(1)} %collective-permute-done.6.sent), channel_id=1, source_target_pairs={{0,1},{1,0},{2,3},{3,2},{4,5},{5,4},{6,7},{7,6},{8,9},{9,8},{10,11... | collective-permute-start | bytes 12296 | tf_op jit(solution)/shard_map/ppermute | solution.py:502

commit v7 on v4

--- a/solution.py
+++ b/solution.py
@@ -115,7 +115,7 @@
 
 def k_block(
     flags, sensors_ref, eye_ref, obs_raw, pres_ref, lp_ref, dyn_ref, pv_ref, map_ref,
-    root_ref, dynt_ref, table, nodes, offs, step_ref, twos_ref, u_ref, mask_ref, obs_ref, rows_ref, mask_scr, u_scr,
+    root_ref, dynt_ref, table, nodes, offs, step_ref, wide_ref, u_ref, mask_ref, rows_ref, mask_scr, u_scr,
 ):
     on = on_row(sensors_ref)
     weight = jnp.exp(lp_ref[...]) * on
@@ -136,11 +136,10 @@
     for i in range(SUB):
         u_ref[i] = step_major(u_scr, i)
         mask_ref[i] = step_major(mask_scr, i)
-        obs_ref[i] = step_major(obs_raw, i)
     two = mul_exact(stacked(dyn_t, filt_t), lanes(dyn_t, filt_t))
     twos = [two[i * N : (i + 1) * N, j * N : (j + 1) * N] for i in (0, 1) for j in (0, 1)]
     wide = lanes(*twos)
-    twos_ref[...] = pair(wide)
+    wide_ref[...] = wide
     for i in range(4):
         four = mul_exact(twos[i], wide)
         for j in range(4):
@@ -348,8 +347,11 @@
 
 def k_tables(
     after_ref, flags, table, nodes, offs, step_ref, u_ref, mask_ref, eye_ref, dyn_ref, dynt_ref,
-    pre_ref, preoff_ref, u2_ref, near_ref, far_ref, reach_ref, cross_ref, resid_ref,
+    obs_raw, wide_ref, obs_ref, twos_ref, pre_ref, preoff_ref, u2_ref, near_ref, far_ref, reach_ref, cross_ref, resid_ref,
 ):
+    twos_ref[...] = pair(wide_ref[...])
+    for i in range(SUB):
+        obs_ref[i] = step_major(obs_raw, i)
     k_prefix(flags, table, nodes, offs, step_ref, u_ref, mask_ref, pre_ref, preoff_ref, u2_ref)
     k_powers(eye_ref, dyn_ref, dynt_ref, near_ref, far_ref, reach_ref, cross_ref, resid_ref)
 
@@ -513,7 +515,7 @@
     square = out((N, N))
     square = out((N, N))
     eye = call(k_first, "k_first", [], square, (), 4 * 10**9, 10**7)()
-    root, dyn_t, table, nodes, offs, step, twos, u, mask, obs_s, rows = call(
+    root, dyn_t, table, nodes, offs, step, wide, u, mask, rows = call(
         k_block,
         "k_block",
         [SM] * 2 + [VM] * 7,
@@ -524,8 +526,7 @@
             out((42, N, 2 * N), BF16),
             out((96, N)),
             out((N, 6 * N), BF16),
-            out((N, 8 * N), BF16),
-            out((SUB, ROWS, N)),
+            out((N, 4 * N)),
             out((SUB, ROWS, N)),
             out((SUB, ROWS, N)),
             out((8, N)),
@@ -538,11 +539,13 @@
     chip, mine = call(k_core, "k_core", [VM] * 2, both, (), 10**7, 10**6)(root, mate)
     near = lax.ppermute(chip, ("tm_1", "tm_2"), RING)
     two = shifted(mine, "tm_1", 2)
-    pre, preoff, u2, step_near, far, reach, cross, resid = call(
+    obs_s, twos, pre, preoff, u2, step_near, far, reach, cross, resid = call(
         k_tables,
         "k_tables",
-        [VM, SM] + [VM] * 9,
+        [VM, SM] + [VM] * 11,
         (
+            out((SUB, ROWS, N)),
+            out((N, 8 * N), BF16),
             out((ROWS, N, N)),
             out((ROWS, N)),
             out((SUB // 2, ROWS, N)),
@@ -555,7 +558,7 @@
         (),
         4 * 10**9,
         10**7,
-    )(chip, present, table, nodes, offs, step, u, mask, eye, dynamics, dyn_t)
+    )(chip, present, table, nodes, offs, step, u, mask, eye, dynamics, dyn_t, obs, wide)
     got = near, swapped(near, resid), two, swapped(two, resid)
     mine, state, ahead = call(
         k_total,

time: 46.9 us -> 46.9 us (level)
  no operation moved by 1% of the time
where the time goes in v7:
time: 46.9 us; the launch traced here: 46.8 us
  starting transfers between devices  13.2 us (28%)
  Pallas kernels  13 us (28%)
  blocking collectives  12.2 us (26%)
  waiting for transfers between devices  6.72 us (14%)
  between operations  1.48 us (3%)
    all_to_all x1, blocking collectives, local(): got = lax.all_to_all(send, TM, 0, 0, tiled=True)  12.2 us
    ppermute x8, starting transfers between devices, shifted(): return lax.ppermute(a, axis, [(i, (i + by) % count) for i in range(count)])  11.5 us
    pallas_call x1, Pallas kernels, local(): call(k_tables, 'k_tables', [VM, SM] + [VM] * 11, (out((SUB, ROWS, N)), ou...  4.13 us
    ppermute x8, waiting for transfers between devices, shifted(): return lax.ppermute(a, axis, [(i, (i + by) % count) for i in range(count)])  3.33 us
    pallas_call x1, Pallas kernels, local(): call(k_block, 'k_block', [SM] * 2 + [VM] * 7, (out((SEQ, N + 8, N)), squa...  3.3 us
    ppermute x1, waiting for transfers between devices, local(): sent = lax.ppermute(state, ('tm_0', 'tm_2'), FIRST)  2.3 us
    pallas_call x1, Pallas kernels, local(): call(k_filter, 'k_filter', [VM] * 22, (out((BLOCKS, 8, N)), out((SUB, ROW...  1.72 us
    pallas_call x1, Pallas kernels, local(): call(k_smooth, 'k_smooth', [VM] * 8, (out((SEQ, STEPS, N)), out((1, N)),...  1.59 us
  transfers between devices with their start and end apart: 11, of which 5 were waited for; matrix products, arithmetic and copies ran while one was open for 0% of the time, Pallas kernels for 11%

profile of v7, /device:TPU:1, one launch (start us, length us, event | category | flops | bytes accessed | tf_op | source)
XLA Modules:
  0.0 46.8 jit_solution(1645804325781247676)
XLA Ops:
  1.5 0.0 copy-done.3
  1.5 0.0 copy-done.2
  1.5 0.1 copy-done.1
  1.6 3.3 %k_block.1 = (f32[3,136,128]{2,1,0:T(8,128)S(1)}, f32[128,128]{1,0:T(8,128)S(1)}, bf16[16,128,256]{2,1,0:T(8,128)(2,1)S(1)}, bf16[42,128,256]{2,1,0:T(8,128)(2,1...) custom-call(s32[3,64]{1,0:T(4,128)S(1)} %copy-done.4, ...), custom_call_target="tpu_custom_call" | custom-call | flops 1000000000 | bytes 1000000 | tf_op jit(solution)/shard_map/k_block/pallas_call | solution.py:518
  4.9 3.3 %collective-permute-start = (f32[3,136,128]{2,1,0:T(8,128)S(1)}, f32[3,136,128]{2,1,0:T(8,128)S(1)}, u32[]{:S(2)}, u32[]{:S(2)}) collective-permute-start(f32[3,136,128]{2,1,0:T(8,128)S(1)} %get-tuple-element.42.own_ref), channel_id=1, source_target_pairs={{0,1},{1,0},{2,3},{3,2},{4,5},{5,4},{6,7},{7,6},{8,9},{9,8},{10,11... | collective-permute-start | bytes 626696 | tf_op jit(solution)/shard_map/ppermute | solution.py:500
  8.3 1.1 %collective-permute-done.mate_ref = f32[3,136,128]{2,1,0:T(8,128)S(1)} collective-permute-done((f32[3,136,128]{2,1,0:T(8,128)S(1)}, f32[3,136,128]{2,1,0:T(8,128)S(1)}, u32[]{:S(2)}, u32[]{:S(2)}) %collective-permute-start) | collective-permute-done | bytes 208928 | tf_op jit(solution)/shard_map/ppermute | solution.py:500
  9.4 0.2 k_core.1
  9.6 1.3 %collective-permute-start.3 = (f32[200,128]{1,0:T(8,128)S(1)}, f32[200,128]{1,0:T(8,128)S(1)}, u32[]{:S(2)}, u32[]{:S(2)}) collective-permute-start(f32[200,128]{1,0:T(8,128)S(1)} %get-tuple-element.54), channel_id=1, source_target_pairs={{0,4},{2,6},{4,0},{6,2},{1,5},{3,7},{5,1},{7,3},{8,12},{10,14},{12... | collective-permute-start | bytes 307208 | tf_op jit(solution)/shard_map/ppermute | solution.py:500
  10.9 0.8 %collective-permute-start.1 = (f32[392,128]{1,0:T(8,128)S(1)}, f32[392,128]{1,0:T(8,128)S(1)}, u32[]{:S(2)}, u32[]{:S(2)}) collective-permute-start(f32[392,128]{1,0:T(8,128)S(1)} %get-tuple-element.43.after_ref.own_ref), channel_id=1, source_target_pairs={{0,2},{2,4},{4,6},{6,0},{1,7},{3,1},{5,3},{7,5},{8,10},{10,12},{12... | collective-permute-start | bytes 602120 | tf_op jit(solution)/shard_map/ppermute | solution.py:540
  11.6 4.1 %k_tables.1 = (f32[4,48,128]{2,1,0:T(8,128)S(1)}, bf16[128,1024]{1,0:T(8,128)(2,1)S(1)}, f32[48,128,128]{2,1,0:T(8,128)S(1)}, f32[48,128]{1,0:T(8,128)S(1)}, f32...) custom-call(f32[392,128]{1,0:T(8,128)S(1)} %get-tuple-element.43.aft, ...), custom_call_target="tpu_custom_call" | custom-call | flops 4000000000 | bytes 10000000 | tf_op jit(solution)/shard_map/k_tables/pallas_call | solution.py:542
  15.8 1.1 %collective-permute-done.1.near = f32[392,128]{1,0:T(8,128)S(1)} collective-permute-done((f32[392,128]{1,0:T(8,128)S(1)}, f32[392,128]{1,0:T(8,128)S(1)}, u32[]{:S(2)}, u32[]{:S(2)}) %collective-permute-start.1) | collective-permute-done | bytes 200736 | tf_op jit(solution)/shard_map/ppermute | solution.py:540
  16.9 1.8 %collective-permute-start.2 = (f32[392,128]{1,0:T(8,128)S(1)}, f32[392,128]{1,0:T(8,128)S(1)}, u32[]{:S(2)}, u32[]{:S(2)}) collective-permute-start(f32[392,128]{1,0:T(8,128)S(1)} %collective-permute-done.1.near), channel_id=1, source_target_pairs={{0,1},{1,0},{2,3},{3,2},{4,5},{5,4},{6,7},{7,6},{8,9},{9,8},{10,11... | collective-permute-start | bytes 602120 | tf_op jit(solution)/shard_map/ppermute | solution.py:500
  18.7 0.0 collective-permute-done.3.two
  18.7 0.0 collective-permute-start.4
  18.7 1.3 %collective-permute-done.4.two_mate = f32[200,128]{1,0:T(8,128)S(1)} collective-permute-done((f32[200,128]{1,0:T(8,128)S(1)}, f32[200,128]{1,0:T(8,128)S(1)}, u32[]{:S(2)}, u32[]{:S(2)}) %collective-permute-start.4) | collective-permute-done | bytes 102432 | tf_op jit(solution)/shard_map/ppermute | solution.py:500
  20.0 0.0 collective-permute-done.2.near_mate
  20.0 0.9 %k_total.1 = (f32[200,128]{1,0:T(8,128)S(1)}, f32[8,128]{1,0:T(8,128)S(1)}, f32[3,3,136,128]{3,2,1,0:T(8,128)S(1)}) custom-call(f32[392,128]{1,0:T(8,128)S(1)} %get-tuple-element.43.after_ref.own_ref, f32[392,128]{1,0:T(8,128)S(1)} %collective-permute-done.1.near, f32[392,128]{1,0:T(8,128)S(1)} %collective-permute-done.2.near_mate, ...), custom_call_target="tpu_custom_call" | custom-call | flops 100000000 | bytes 1000000 | tf_op jit(solution)/shard_map/k_total/pallas_call | solution.py:563
  20.8 0.4 collective-permute-start.8
  21.2 2.6 %collective-permute-start.5 = (f32[200,128]{1,0:T(8,128)S(1)}, f32[200,128]{1,0:T(8,128)S(1)}, u32[]{:S(2)}, u32[]{:S(2)}) collective-permute-start(f32[200,128]{1,0:T(8,128)S(1)} %get-tuple-element.56.after_ref), channel_id=1, source_target_pairs={{0,8},{8,16},{16,24},{24,0},{1,9},{9,17},{17,25},{25,1},{2,10},{10... | collective-permute-start | bytes 307208 | tf_op jit(solution)/shard_map/ppermute | solution.py:500
  23.8 0.5 %collective-permute-start.6 = (f32[8,128]{1,0:T(8,128)S(1)}, f32[8,128]{1,0:T(8,128)S(1)}, u32[]{:S(2)}, u32[]{:S(2)}) collective-permute-start(f32[8,128]{1,0:T(8,128)S(1)} %get-tuple-element.59), channel_id=1, source_target_pairs={{0,16},{1,25},{16,0},{25,1},{8,9},{9,8},{17,24},{24,17},{2,18},{3,... | collective-permute-start | bytes 12296 | tf_op jit(solution)/shard_map/ppermute | solution.py:574
  24.3 1.1 %k_entry.1 = (f32[3,128,128]{2,1,0:T(8,128)S(1)}, f32[8,128]{1,0:T(8,128)S(1)}) custom-call(f32[200,128]{1,0:T(8,128)S(1)} %get-tuple-element.56.after_ref, f32[3,3,136,128]{3,2,1,0:T(8,128)S(1)} %get-tuple-element.57.ahead_ref, f32[3,136,128]{2,1,0:T(8,128)S(1)} %collective-permute-done.mate_ref), custom_call_target="tpu_custom_call" | custom-call | flops 4000000000 | bytes 10000000 | tf_op jit(solution)/shard_map/k_entry/pallas_call | solution.py:575
  25.5 2.3 %collective-permute-done.6.sent = f32[8,128]{1,0:T(8,128)S(1)} collective-permute-done((f32[8,128]{1,0:T(8,128)S(1)}, f32[8,128]{1,0:T(8,128)S(1)}, u32[]{:S(2)}, u32[]{:S(2)}) %collective-permute-start.6) | collective-permute-done | bytes 4128 | tf_op jit(solution)/shard_map/ppermute | solution.py:574
  27.8 0.0 collective-permute-done.8.two
  27.8 2.0 %collective-permute-start.9 = (f32[200,128]{1,0:T(8,128)S(1)}, f32[200,128]{1,0:T(8,128)S(1)}, u32[]{:S(2)}, u32[]{:S(2)}) collective-permute-start(f32[200,128]{1,0:T(8,128)S(1)} %collective-permute-done.8.two), channel_id=1, source_target_pairs={{0,1},{1,0},{2,3},{3,2},{4,5},{5,4},{6,7},{7,6},{8,9},{9,8},{10,11... | collective-permute-start | bytes 307208 | tf_op jit(solution)/shard_map/ppermute | solution.py:500
  29.8 0.0 collective-permute-done.5.one
  29.8 0.3 collective-permute-start.7
  30.0 0.2 collective-permute-start.10
  30.3 0.9 %collective-permute-done.10.sent_mate = f32[8,128]{1,0:T(8,128)S(1)} collective-permute-done((f32[8,128]{1,0:T(8,128)S(1)}, f32[8,128]{1,0:T(8,128)S(1)}, u32[]{:S(2)}, u32[]{:S(2)}) %collective-permute-start.10) | collective-permute-done | bytes 4128 | tf_op jit(solution)/shard_map/ppermute | solution.py:500
  31.2 0.0 collective-permute-done.9.two_mate
  31.2 1.7 %k_filter.1 = (f32[32,8,128]{2,1,0:T(8,128)S(1)}, f32[4,48,128]{2,1,0:T(8,128)S(1)}, f32[48,128]{1,0:T(8,128)S(1)}, f32[8,128]{1,0:T(8,128)S(1)}) custom-call(f32[200,128]{1,0:T(8,128)S(1)} %collective-permute-done.5.one, f32[200,128]{1,0:T(8,128)S(1)} %collective-permute-done.7.one_mate, f32[200,128]{1,0:T(8,128)S(1)} %collective-permute-done.8.two, ...), custom_call_target="tpu_custom_call" | custom-call | flops 10000000 | bytes 1000000 | tf_op jit(solution)/shard_map/k_filter/pallas_call | solution.py:582
  32.9 12.2 %all_to_all.5.got_ref = f32[32,8,128]{2,1,0:T(8,128)S(1)} all-to-all(f32[32,8,128]{2,1,0:T(8,128)S(1)} %get-tuple-element.72), channel_id=1, replica_groups=mesh['cluster'=8,'tm_0'=4,'tm_1'=4,'tm_2'=2] {'tm_0','tm_1','tm_2'}, dimensions={0} | all-to-all | bytes 262144 | tf_op jit(solution)/shard_map/all_to_all | solution.py:594
  45.2 1.6 %k_smooth.1 = (f32[3,64,128]{2,1,0:T(8,128)}, f32[1,128]{1,0:T(1,128)}, f32[1,128]{1,0:T(1,128)}) custom-call(f32[32,8,128]{2,1,0:T(8,128)S(1)} %all_to_all.5.got_ref, f32[4,48,128]{2,1,0:T(8,128)S(1)} %get-tuple-element.73.local_ref, f32[48,128]{1,0:T(8,128)S(1)} %get-tuple-element.74.suffix_ref, f32[8,128]{1,0:T(8,128)S(1)} %get-tuple-element.75.final_ref, ...), custom_call_target="tpu_custom_call" | custom-call | flops 10000000 | bytes 1000000 | tf_op jit(solution)/shard_map/k_smooth/pallas_call | solution.py:595
  (13 shorter events, 0.0 us)
Async XLA Ops:
  0.6 0.8 %copy-start.5 = (f32[128]{0:T(128)S(1)}, f32[128]{0:T(128)}, u32[]{:S(2)}) copy-start(f32[128]{0:T(128)} %param.11) | copy-start | bytes 1540
  0.6 0.8 %copy-start.6 = (f32[128]{0:T(128)S(1)}, f32[128]{0:T(128)}, u32[]{:S(2)}) copy-start(f32[128]{0:T(128)} %param.13) | copy-start | bytes 1540
  0.7 0.9 %copy-start.3 = (f32[128,128]{1,0:T(8,128)S(1)}, f32[128,128]{1,0:T(8,128)}, u32[]{:S(2)}) copy-start(f32[128,128]{1,0:T(8,128)} %dyn_ref.3) | copy-start | bytes 196612
  0.7 0.9 %copy-start.2 = (f32[128,128]{1,0:T(8,128)S(1)}, f32[128,128]{1,0:T(8,128)}, u32[]{:S(2)}) copy-start(f32[128,128]{1,0:T(8,128)} %map_ref.1) | copy-start | bytes 196612
  0.7 1.0 %copy-start.1 = (f32[3,64,128]{2,1,0:T(8,128)S(1)}, f32[3,64,128]{2,1,0:T(8,128)}, u32[]{:S(2)}) copy-start(f32[3,64,128]{2,1,0:T(8,128)} %obs_raw.3) | copy-start | bytes 294916
  0.7 1.0 %copy-start.4 = (s32[3,64]{1,0:T(4,128)S(1)}, s32[3,64]{1,0:T(4,128)}, u32[]{:S(2)}) copy-start(s32[3,64]{1,0:T(4,128)} %flags.3) | copy-start | bytes 2308
  4.9 4.4 %collective-permute-start = (f32[3,136,128]{2,1,0:T(8,128)S(1)}, f32[3,136,128]{2,1,0:T(8,128)S(1)}, u32[]{:S(2)}, u32[]{:S(2)}) collective-permute-start(f32[3,136,128]{2,1,0:T(8,128)S(1)} %get-tuple-element.42.own_ref), channel_id=1, source_target_pairs={{0,1},{1,0},{2,3},{3,2},{4,5},{5,4},{6,7},{7,6},{8,9},{9,8},{10,11... | collective-permute-start | bytes 626696 | tf_op jit(solution)/shard_map/ppermute | solution.py:500
  9.6 9.0 %collective-permute-start.3 = (f32[200,128]{1,0:T(8,128)S(1)}, f32[200,128]{1,0:T(8,128)S(1)}, u32[]{:S(2)}, u32[]{:S(2)}) collective-permute-start(f32[200,128]{1,0:T(8,128)S(1)} %get-tuple-element.54), channel_id=1, source_target_pairs={{0,4},{2,6},{4,0},{6,2},{1,5},{3,7},{5,1},{7,3},{8,12},{10,14},{12... | collective-permute-start | bytes 307208 | tf_op jit(solution)/shard_map/ppermute | solution.py:500
  10.9 6.0 %collective-permute-start.1 = (f32[392,128]{1,0:T(8,128)S(1)}, f32[392,128]{1,0:T(8,128)S(1)}, u32[]{:S(2)}, u32[]{:S(2)}) collective-permute-start(f32[392,128]{1,0:T(8,128)S(1)} %get-tuple-element.43.after_ref.own_ref), channel_id=1, source_target_pairs={{0,2},{2,4},{4,6},{6,0},{1,7},{3,1},{5,3},{7,5},{8,10},{10,12},{12... | collective-permute-start | bytes 602120 | tf_op jit(solution)/shard_map/ppermute | solution.py:540
  11.6 8.3 %copy-start = (f32[3,128]{1,0:T(4,128)S(1)}, f32[3,128]{1,0:T(4,128)}, u32[]{:S(2)}) copy-start(f32[3,128]{1,0:T(4,128)} %init_ref.3) | copy-start | bytes 4612
  16.9 3.1 %collective-permute-start.2 = (f32[392,128]{1,0:T(8,128)S(1)}, f32[392,128]{1,0:T(8,128)S(1)}, u32[]{:S(2)}, u32[]{:S(2)}) collective-permute-start(f32[392,128]{1,0:T(8,128)S(1)} %collective-permute-done.1.near), channel_id=1, source_target_pairs={{0,1},{1,0},{2,3},{3,2},{4,5},{5,4},{6,7},{7,6},{8,9},{9,8},{10,11... | collective-permute-start | bytes 602120 | tf_op jit(solution)/shard_map/ppermute | solution.py:500
  18.7 1.3 %collective-permute-start.4 = (f32[200,128]{1,0:T(8,128)S(1)}, f32[200,128]{1,0:T(8,128)S(1)}, u32[]{:S(2)}, u32[]{:S(2)}) collective-permute-start(f32[200,128]{1,0:T(8,128)S(1)} %collective-permute-done.3.two), channel_id=1, source_target_pairs={{0,1},{1,0},{2,3},{3,2},{4,5},{5,4},{6,7},{7,6},{8,9},{9,8},{10,11... | collective-permute-start | bytes 307208 | tf_op jit(solution)/shard_map/ppermute | solution.py:500
  20.8 6.9 %collective-permute-start.8 = (f32[200,128]{1,0:T(8,128)S(1)}, f32[200,128]{1,0:T(8,128)S(1)}, u32[]{:S(2)}, u32[]{:S(2)}) collective-permute-start(f32[200,128]{1,0:T(8,128)S(1)} %get-tuple-element.56.after_ref), channel_id=1, source_target_pairs={{8,24},{9,25},{24,8},{25,9},{0,1},{1,0},{16,17},{17,16},{10,26},{1... | collective-permute-start | bytes 307208 | tf_op jit(solution)/shard_map/ppermute | solution.py:573
  21.2 8.6 %collective-permute-start.5 = (f32[200,128]{1,0:T(8,128)S(1)}, f32[200,128]{1,0:T(8,128)S(1)}, u32[]{:S(2)}, u32[]{:S(2)}) collective-permute-start(f32[200,128]{1,0:T(8,128)S(1)} %get-tuple-element.56.after_ref), channel_id=1, source_target_pairs={{0,8},{8,16},{16,24},{24,0},{1,9},{9,17},{17,25},{25,1},{2,10},{10... | collective-permute-start | bytes 307208 | tf_op jit(solution)/shard_map/ppermute | solution.py:500
  23.8 4.0 %collective-permute-start.6 = (f32[8,128]{1,0:T(8,128)S(1)}, f32[8,128]{1,0:T(8,128)S(1)}, u32[]{:S(2)}, u32[]{:S(2)}) collective-permute-start(f32[8,128]{1,0:T(8,128)S(1)} %get-tuple-element.59), channel_id=1, source_target_pairs={{0,16},{1,25},{16,0},{25,1},{8,9},{9,8},{17,24},{24,17},{2,18},{3,... | collective-permute-start | bytes 12296 | tf_op jit(solution)/shard_map/ppermute | solution.py:574
  27.8 3.4 %collective-permute-start.9 = (f32[200,128]{1,0:T(8,128)S(1)}, f32[200,128]{1,0:T(8,128)S(1)}, u32[]{:S(2)}, u32[]{:S(2)}) collective-permute-start(f32[200,128]{1,0:T(8,128)S(1)} %collective-permute-done.8.two), channel_id=1, source_target_pairs={{0,1},{1,0},{2,3},{3,2},{4,5},{5,4},{6,7},{7,6},{8,9},{9,8},{10,11... | collective-permute-start | bytes 307208 | tf_op jit(solution)/shard_map/ppermute | solution.py:500
  29.8 1.4 %collective-permute-start.7 = (f32[200,128]{1,0:T(8,128)S(1)}, f32[200,128]{1,0:T(8,128)S(1)}, u32[]{:S(2)}, u32[]{:S(2)}) collective-permute-start(f32[200,128]{1,0:T(8,128)S(1)} %collective-permute-done.5.one), channel_id=1, source_target_pairs={{0,1},{1,0},{2,3},{3,2},{4,5},{5,4},{6,7},{7,6},{8,9},{9,8},{10,11... | collective-permute-start | bytes 307208 | tf_op jit(solution)/shard_map/ppermute | solution.py:500
  30.0 1.2 %collective-permute-start.10 = (f32[8,128]{1,0:T(8,128)S(1)}, f32[8,128]{1,0:T(8,128)S(1)}, u32[]{:S(2)}, u32[]{:S(2)}) collective-permute-start(f32[8,128]{1,0:T(8,128)S(1)} %collective-permute-done.6.sent), channel_id=1, source_target_pairs={{0,1},{1,0},{2,3},{3,2},{4,5},{5,4},{6,7},{7,6},{8,9},{9,8},{10,11... | collective-permute-start | bytes 12296 | tf_op jit(solution)/shard_map/ppermute | solution.py:500
